TPU v7x, 128 devices: a whole 4x4x4 slice. The times are simulated.
128 devices in a mesh: row: 8 (over y, core), col: 16 (over z, x).
Axes of the slice: x: 4, y: 4, z: 4, core: 2. Of those that a mesh axis runs over, the one named last changes fastest.
Arguments:
- noise_latents: bfloat16 [8192, 2048], P('row', 'col'), may hold values from -40 to 40
- data_latents: bfloat16 [32768, 2048], P('col', 'row'), may hold values from -6 to 6
- noise_sizes: int32 [8], replicated, may hold values from 1 to 2048, 8192 in all
- data_sizes: int32 [8], replicated, may hold values from 1 to 8192, 32768 in all
Outputs:
- velocity: float32 [8192, 2048], P('row', 'col')
- noise_potential: float32 [8192], P('row')
- data_potential: float32 [32768], P('col')
Inputs may be any that keep to these rules, and one draw needn't show every extreme that they name: `noise_sizes`: clusters take consecutive runs of noise samples in order of the cluster number; every cluster is non-empty and the largest holds exactly 2048. `data_sizes`: clusters take consecutive runs of data samples in order of the cluster number; every cluster is non-empty and the largest holds exactly 8192.
All inputs are finite; a program needn't handle non-finite values.
Results may differ from a plain program's by a relative error of at most 0.007.
Values may be sent and summed in bfloat16 or wider, within the bound.
No kernel may reach another device: no remote copies, remote signals or barrier semaphores. Data moves between devices by JAX's collectives and lax.ppermute only.
A program may use at most 128 MiB of HBM per device.

v0:
```python
import jax
import jax.numpy as jnp
from jax import lax
from jax.sharding import PartitionSpec as P

ITERS = 3


epsilon = 0.05
masked_value = -1e30


def cluster_of(positions, cluster_sizes):
    boundaries = jnp.cumsum(cluster_sizes)[:-1]
    return jnp.sum((positions[:, None] >= boundaries[None, :]).astype(jnp.int32), axis=1)


def lse_over_cols(scores, same_cluster):
    masked = jnp.where(same_cluster, scores, masked_value)
    largest = lax.pmax(jnp.max(masked, axis=1), "col")
    totals = lax.psum(
        jnp.sum(jnp.where(same_cluster, jnp.exp(masked - largest[:, None]), 0.0), axis=1), "col"
    )
    return largest + jnp.log(totals)


def lse_over_rows(scores, same_cluster):
    masked = jnp.where(same_cluster, scores, masked_value)
    largest = lax.pmax(jnp.max(masked, axis=0), "row")
    totals = lax.psum(
        jnp.sum(jnp.where(same_cluster, jnp.exp(masked - largest[None, :]), 0.0), axis=0), "row"
    )
    return largest + jnp.log(totals)


def per_device(noise_latents, data_latents, noise_sizes, data_sizes):
    row_count = noise_latents.shape[0]
    col_count = data_latents.shape[0]
    full_width = noise_latents.shape[1] * lax.axis_size("col")
    row_positions = lax.axis_index("row") * row_count + jnp.arange(row_count, dtype=jnp.int32)
    col_positions = lax.axis_index("col") * col_count + jnp.arange(col_count, dtype=jnp.int32)
    noise_cluster = cluster_of(row_positions, noise_sizes)
    data_cluster = cluster_of(col_positions, data_sizes)
    same_cluster = noise_cluster[:, None] == data_cluster[None, :]
    data_full = lax.all_gather(data_latents, "row", axis=1, tiled=True)
    data_sq = jnp.sum(jnp.square(data_full.astype(jnp.float32)), axis=1)
    shard_piece = lax.all_gather(noise_latents, "col", axis=1, tiled=True)
    inner = lax.dot_general(
        shard_piece, data_full, (((1,), (1,)), ((), ())), preferred_element_type=jnp.float32
    )
    inner, noise_sq = (inner, jnp.sum(jnp.square(shard_piece.astype(jnp.float32)), axis=1))
    cost = (noise_sq[:, None] + data_sq[None, :] - 2.0 * inner) / full_width
    data_potential = jnp.zeros((col_count,), jnp.float32)
    noise_potential = jnp.zeros((row_count,), jnp.float32)
    for iteration in range(ITERS):
        noise_potential = -epsilon * lse_over_cols(
            (data_potential[None, :] - cost) / epsilon, same_cluster
        )
        data_potential = -epsilon * lse_over_rows(
            (noise_potential[:, None] - cost) / epsilon, same_cluster
        )
    scores = (data_potential[None, :] - cost) / epsilon
    row_lse = lse_over_cols(scores, same_cluster)
    weights = jnp.where(
        same_cluster, jnp.exp(jnp.where(same_cluster, scores, masked_value) - row_lse[:, None]), 0.0
    ).astype(jnp.bfloat16)
    partials = jnp.dot(weights, data_full, preferred_element_type=jnp.float32)
    share_width = noise_latents.shape[1]
    summed = lax.psum(partials.astype(jnp.bfloat16), "col").astype(jnp.float32)
    target = lax.dynamic_slice_in_dim(summed, lax.axis_index("col") * share_width, share_width, 1)
    velocity = target - noise_latents.astype(jnp.float32)
    return (velocity, noise_potential, data_potential)


def solution(mesh):
    placed = (P("row", "col"), P("col", "row"), P(), P())
    return jax.shard_map(
        per_device,
        mesh=mesh,
        in_specs=placed,
        out_specs=(P("row", "col"), P("row"), P("col")),
        check_vma=False,
    )
```

profile of v0, /device:TPU:0, one launch (start us, length us, event | category | flops | bytes accessed | tf_op | source)
XLA Modules:
  0.0 701.3 jit_solution(4044345735516133163)
XLA Ops:
  7.2 0.0 all-gather.3.cloned.1.call-start
  7.2 0.7 all-gather.3.cloned.1.call-update
  7.9 0.0 all-gather.5.cloned.1.call-start
  7.9 0.7 all-gather.5.cloned.1.call-update
  8.6 0.0 all-reduce.2.cloned.1.call-start
  8.7 0.8 reduce-window.6
  9.5 0.8 reduce-window.9
  10.4 0.1 convert_reduce_fusion.1
  10.5 0.1 convert_reduce_fusion
  10.6 59.7 %all-gather.3.cloned.1.call-done = bf16[1024,2048]{1,0:T(8,128)(2,1)} async-done(((bf16[1024,128]{1,0:T(8,128)(2,1)}), bf16[1024,2048]{1,0:T(8,128)(2,1)}) %all-gather.3.cloned.1.call-update) | async-done | bytes 4194320 | tf_op jit(solution)/shard_map/all_gather | solution.py:47
  70.3 3.1 multiply_reduce_fusion.1
  73.4 51.9 %all-gather.5.cloned.1.call-done = bf16[2048,2048]{1,0:T(8,128)(2,1)} async-done(((bf16[2048,256]{1,0:T(8,128)(2,1)}), bf16[2048,2048]{1,0:T(8,128)(2,1)}) %all-gather.5.cloned.1.call-update) | async-done | bytes 8388624 | tf_op jit(solution)/shard_map/all_gather | solution.py:45
  125.2 5.2 multiply_reduce_fusion
  130.5 0.5 copy-done
  131.0 14.0 %fusion.8 = (f32[1024]{0:T(1024)S(1)}, f32[1024,2048]{1,0:T(8,128)}) fusion(s32[2048]{0:T(1024)S(1)} %convert_reduce_fusion, s32[1024]{0:T(1024)S(1)} %convert_reduce_fusion.1, bf16[1024,2048]{1,0:T(8,128)(2,1)} %all-gather.3.cloned.1.call-done, bf16[2048,2048]{1,0:T(8,128)(2,1)S(1)} %copy-done, f32[2048]{0:T(1024)S(1)} %multiply_reduce_fusion, ...), kind=kOutput, calls=%fused_computation.26 | convolution fusion | flops 8608807936 | bytes 21000192 | tf_op jit(solution)/shard_map/dot_general | solution.py:48
  145.0 40.5 %pmax.49 = f32[1024]{0:T(1024)S(1)} all-reduce(f32[1024]{0:T(1024)S(1)} %get-tuple-element.3), channel_id=1, replica_groups=mesh['row'=8,'col'=16] {'col'}, use_global_device_ids=true, to_apply=%region_7.8 | all-reduce | flops 1024 | bytes 8192 | tf_op jit(solution)/shard_map/pmax | solution.py:20
  185.5 5.0 fusion
  190.6 35.5 %psum.56 = f32[1024]{0:T(1024)S(1)} all-reduce(f32[1024]{0:T(1024)S(1)} %fusion), channel_id=1, replica_groups=mesh['row'=8,'col'=16] {'col'}, use_global_device_ids=true, to_apply=%region_9.10 | all-reduce | flops 1024 | bytes 8192 | tf_op jit(solution)/shard_map/psum | solution.py:21
  226.1 4.3 fusion.9
  230.4 12.7 %pmax.50 = f32[2048]{0:T(1024)S(1)} all-reduce(f32[2048]{0:T(1024)S(1)} %fusion.9), channel_id=1, replica_groups=mesh['row'=8,'col'=16] {'row'}, use_global_device_ids=true, to_apply=%region_11.12 | all-reduce | flops 2048 | bytes 16384 | tf_op jit(solution)/shard_map/pmax | solution.py:29
  243.0 5.1 fusion.1
  248.1 12.8 %psum.57 = f32[2048]{0:T(1024)S(1)} all-reduce(f32[2048]{0:T(1024)S(1)} %fusion.1), channel_id=1, replica_groups=mesh['row'=8,'col'=16] {'row'}, use_global_device_ids=true, to_apply=%region_13.14 | all-reduce | flops 2048 | bytes 16384 | tf_op jit(solution)/shard_map/psum | solution.py:30
  261.0 4.4 fusion.10
  265.4 37.5 %pmax.51 = f32[1024]{0:T(1024)S(1)} all-reduce(f32[1024]{0:T(1024)S(1)} %fusion.10), channel_id=1, replica_groups=mesh['row'=8,'col'=16] {'col'}, use_global_device_ids=true, to_apply=%region_15.16 | all-reduce | flops 1024 | bytes 8192 | tf_op jit(solution)/shard_map/pmax | solution.py:20
  302.9 5.1 fusion.2
  307.9 35.5 %psum.58 = f32[1024]{0:T(1024)S(1)} all-reduce(f32[1024]{0:T(1024)S(1)} %fusion.2), channel_id=1, replica_groups=mesh['row'=8,'col'=16] {'col'}, use_global_device_ids=true, to_apply=%region_17.18 | all-reduce | flops 1024 | bytes 8192 | tf_op jit(solution)/shard_map/psum | solution.py:21
  343.4 4.3 fusion.11
  347.7 12.7 %pmax.52 = f32[2048]{0:T(1024)S(1)} all-reduce(f32[2048]{0:T(1024)S(1)} %fusion.11), channel_id=1, replica_groups=mesh['row'=8,'col'=16] {'row'}, use_global_device_ids=true, to_apply=%region_19.20 | all-reduce | flops 2048 | bytes 16384 | tf_op jit(solution)/shard_map/pmax | solution.py:29
  360.4 5.1 fusion.3
  365.5 12.7 %psum.59 = f32[2048]{0:T(1024)S(1)} all-reduce(f32[2048]{0:T(1024)S(1)} %fusion.3), channel_id=1, replica_groups=mesh['row'=8,'col'=16] {'row'}, use_global_device_ids=true, to_apply=%region_21.22 | all-reduce | flops 2048 | bytes 16384 | tf_op jit(solution)/shard_map/psum | solution.py:30
  378.2 4.4 fusion.12
  382.6 37.5 %pmax.53 = f32[1024]{0:T(1024)S(1)} all-reduce(f32[1024]{0:T(1024)S(1)} %fusion.12), channel_id=1, replica_groups=mesh['row'=8,'col'=16] {'col'}, use_global_device_ids=true, to_apply=%region_23.24 | all-reduce | flops 1024 | bytes 8192 | tf_op jit(solution)/shard_map/pmax | solution.py:20
  420.1 5.1 fusion.4
  425.1 35.5 %psum.60 = f32[1024]{0:T(1024)S(1)} all-reduce(f32[1024]{0:T(1024)S(1)} %fusion.4), channel_id=1, replica_groups=mesh['row'=8,'col'=16] {'col'}, use_global_device_ids=true, to_apply=%region_25.26 | all-reduce | flops 1024 | bytes 8192 | tf_op jit(solution)/shard_map/psum | solution.py:21
  460.6 4.3 fusion.13
  464.9 12.7 %pmax.54 = f32[2048]{0:T(1024)S(1)} all-reduce(f32[2048]{0:T(1024)S(1)} %fusion.13), channel_id=1, replica_groups=mesh['row'=8,'col'=16] {'row'}, use_global_device_ids=true, to_apply=%region_27.28 | all-reduce | flops 2048 | bytes 16384 | tf_op jit(solution)/shard_map/pmax | solution.py:29
  477.6 5.1 fusion.5
  482.7 12.7 %psum.61 = f32[2048]{0:T(1024)S(1)} all-reduce(f32[2048]{0:T(1024)S(1)} %fusion.5), channel_id=1, replica_groups=mesh['row'=8,'col'=16] {'row'}, use_global_device_ids=true, to_apply=%region_29.30 | all-reduce | flops 2048 | bytes 16384 | tf_op jit(solution)/shard_map/psum | solution.py:30
  495.4 0.0 copy-start.2
  495.4 4.4 fusion.14
  499.8 37.7 %pmax.55 = f32[1024]{0:T(1024)S(1)} all-reduce(f32[1024]{0:T(1024)S(1)} %fusion.14), channel_id=1, replica_groups=mesh['row'=8,'col'=16] {'col'}, use_global_device_ids=true, to_apply=%region_31.32 | all-reduce | flops 1024 | bytes 8192 | tf_op jit(solution)/shard_map/pmax | solution.py:20
  537.5 5.1 fusion.6
  542.6 35.5 %psum.62 = f32[1024]{0:T(1024)S(1)} all-reduce(f32[1024]{0:T(1024)S(1)} %fusion.6), channel_id=1, replica_groups=mesh['row'=8,'col'=16] {'col'}, use_global_device_ids=true, to_apply=%region_33.34 | all-reduce | flops 1024 | bytes 8192 | tf_op jit(solution)/shard_map/psum | solution.py:21
  578.1 0.0 copy-start.1
  578.1 15.9 %fusion.24 = bf16[1024,2048]{1,0:T(8,128)(2,1)} fusion(bf16[2048,2048]{1,0:T(8,128)(2,1)} %all-gather.5.cloned.1.call-done, f32[1024,2048]{1,0:T(8,128)} %get-tuple-element.4, f32[1024]{0:T(1024)S(1)} %log_add_fusion, f32[2048]{0:T(1024)S(1)} %add_multiply_fusion, s32[2048]{0:T(1024)S(1)} %convert_reduce_fusion, s32[1024]{0:T(1024)S(1)} %convert_reduce_fusion.1), kind=kOutput, calls=%fused_computation.41 | convolution fusion | flops 8606711808 | bytes 20996096 | tf_op jit(solution)/shard_map/dot_general | solution.py:67
  593.9 0.0 all-reduce.2.cloned.1.call-update
  594.0 99.0 %all-reduce.2.cloned.1.call-done = bf16[1024,2048]{1,0:T(8,128)(2,1)} async-done(((bf16[1024,2048]{1,0:T(8,128)(2,1)}), bf16[1024,2048]{1,0:T(8,128)(2,1)}) %all-reduce.2.cloned.1.call-update) | async-done | bytes 4194320 | tf_op jit(solution)/shard_map/psum | solution.py:69
  692.9 1.8 convert_subtract_fusion
  (16 shorter events, 0.1 us)
Async XLA Ops:
  7.2 63.1 %all-gather.3.cloned.1.call-start = ((), (), s32[]{:S(2)}) async-start(), calls=%async_computation | async-start | bytes 4456448 | tf_op jit(solution)/shard_map/all_gather | solution.py:47
  7.9 117.3 %all-gather.5.cloned.1.call-start = ((), (), s32[]{:S(2)}) async-start(), calls=%async_computation.1 | async-start | bytes 9437184 | tf_op jit(solution)/shard_map/all_gather | solution.py:45
  8.6 684.3 %all-reduce.2.cloned.1.call-start = ((), (), s32[]{:S(2)}) async-start(), calls=%async_computation.2 | async-start | bytes 8388608 | tf_op jit(solution)/shard_map/psum | solution.py:69
  125.2 5.8 copy-start
  460.6 22.1 %copy-start.3 = (f32[1024]{0:T(1024)}, f32[1024]{0:T(1024)S(1)}, u32[]{:S(2)}) copy-start(f32[1024]{0:T(1024)S(1)} %add_multiply_fusion.3) | copy-start | bytes 12292
  495.4 82.6 %copy-start.2 = (f32[2048]{0:T(1024)}, f32[2048]{0:T(1024)S(1)}, u32[]{:S(2)}) copy-start(f32[2048]{0:T(1024)S(1)} %add_multiply_fusion) | copy-start | bytes 24580
  578.1 114.9 %copy-start.1 = (bf16[1024,128]{1,0:T(8,128)(2,1)S(1)}, bf16[1024,128]{1,0:T(8,128)(2,1)}, u32[]{:S(2)}) copy-start(bf16[1024,128]{1,0:T(8,128)(2,1)} %param.4) | copy-start | bytes 786436
Sparse Core Ops, SparseCore 0:
  10.1 60.1 all-gather.2
  72.0 53.2 all-gather.4
  594.1 98.8 all-reduce.1
where the time goes:
time: 702 us; the launch traced here: 701 us
  blocking collectives  371 us (53%)
  waiting for transfers between devices  212 us (30%)
  other arithmetic  73.6 us (10%)
  matrix products  29.9 us (4%)
  between operations  14 us (2%)
    pmax x4, blocking collectives, lse_over_cols(): largest = lax.pmax(jnp.max(masked, axis=1), 'col')  153 us
    psum x4, blocking collectives, lse_over_cols(): lax.psum(jnp.sum(jnp.where(same_cluster, jnp.exp(masked - largest[:, None...  142 us
    psum x1, waiting for transfers between devices, per_device(): summed = lax.psum(partials.astype(jnp.bfloat16), 'col').astype(jnp.float32)  99 us
    all_gather x1, waiting for transfers between devices, per_device(): shard_piece = lax.all_gather(noise_latents, 'col', axis=1, tiled=True)  59.7 us
    all_gather x1, waiting for transfers between devices, per_device(): data_full = lax.all_gather(data_latents, 'row', axis=1, tiled=True)  51.9 us
    psum x3, blocking collectives, lse_over_rows(): lax.psum(jnp.sum(jnp.where(same_cluster, jnp.exp(masked - largest[None, :...  38.2 us
    pmax x3, blocking collectives, lse_over_rows(): largest = lax.pmax(jnp.max(masked, axis=0), 'row')  38 us
    reduce_sum x4, other arithmetic, lse_over_cols(): jnp.sum(jnp.where(same_cluster, jnp.exp(masked - largest[:, None]), 0.0),...  20.3 us
  transfers between devices with their start and end apart: 3, of which 3 were waited for; matrix products, arithmetic and copies ran while one was open for 1% of the time, Pallas kernels for 0%

commit v1 on v0

v1 whole, which is shorter than its diff:
```python
import functools

import jax
import jax.numpy as jnp
from jax import lax
from jax.experimental import pallas as pl
from jax.experimental.pallas import tpu as pltpu
from jax.sharding import PartitionSpec as P

EPS = 0.05
LOG2E = 1.4426950408889634
LN2 = 0.6931471805599453
MASKED = -1e30
CLUSTERS = 8
F32 = jnp.float32
BF16 = jnp.bfloat16
MIB = 1 << 20

ROWS = 1024
COLS = 2048
WIDTH = 2048
COL_BLOCK = 256
ROW_BLOCK = 256
N_ROW = 8
N_COL = 16
KAPPA = LOG2E / (WIDTH * EPS)


def vmem(shape, index_map=None):
    if index_map is None:
        return pl.BlockSpec(shape, lambda *_: (0,) * len(shape))
    return pl.BlockSpec(shape, index_map)


def params(mib):
    return pltpu.CompilerParams(vmem_limit_bytes=mib * MIB, dimension_semantics=("arbitrary",))


def lane_totals(pieces):
    return [piece.T for piece in pieces]


def to_column(rows):
    n = rows.shape[0]
    return [jnp.broadcast_to(rows[a : a + 1, :], (128, 128)).T for a in range(n)]


def to_lanes(rows):
    return jnp.concatenate([rows[a : a + 1, :] for a in range(rows.shape[0])], axis=1)


def from_lanes(row):
    return jnp.concatenate([row[:, 128 * a : 128 * (a + 1)] for a in range(row.shape[1] // 128)], axis=0)


def score_kernel(info_ref, noise_ref, data_ref, score_ref, lse_ref, noise_sq_ref, data_sq_ref, big, total):
    step = pl.program_id(0)

    @pl.when(step == 0)
    def _():
        big[...] = jnp.full(big.shape, MASKED, F32)
        total[...] = jnp.zeros(total.shape, F32)
        for a in range(ROWS // 128):
            squares = jnp.zeros((128, 128), F32)
            for k in range(N_COL):
                piece = noise_ref[k, 128 * a : 128 * (a + 1), :].astype(F32)
                squares += piece * piece
            noise_sq_ref[a : a + 1, :] = jnp.sum(squares.T, axis=0, keepdims=True)

    data = jnp.concatenate([data_ref[k] for k in range(N_ROW)], axis=1)
    data_sq = []
    for a in range(COL_BLOCK // 128):
        squares = jnp.zeros((128, 128), F32)
        for k in range(WIDTH // 128):
            piece = data[128 * a : 128 * (a + 1), 128 * k : 128 * (k + 1)].astype(F32)
            squares += piece * piece
        data_sq.append(jnp.sum(squares.T, axis=0, keepdims=True))
        data_sq_ref[0, a : a + 1, :] = data_sq[a]

    j = info_ref[17] + step * COL_BLOCK + lax.broadcasted_iota(jnp.int32, (1, COL_BLOCK), 1)
    low = jnp.zeros((1, COL_BLOCK), jnp.int32)
    high = jnp.zeros((1, COL_BLOCK), jnp.int32)
    noise_at = jnp.int32(0)
    data_at = jnp.int32(0)
    for c in range(CLUSTERS):
        noise_end = noise_at + info_ref[c]
        data_end = data_at + info_ref[8 + c]
        if c == CLUSTERS - 1:
            inside = j >= data_at
        else:
            inside = (j >= data_at) & (j < data_end)
        low = jnp.where(inside, noise_at, low)
        high = jnp.where(inside, noise_end, high)
        noise_at, data_at = noise_end, data_end
    low = low - info_ref[16]
    high = high - info_ref[16]

    half = 256
    for r in range(ROWS // half):
        noise = jnp.concatenate([noise_ref[k, half * r : half * (r + 1), :] for k in range(N_COL)], axis=1)
        inner = lax.dot_general(noise, data, (((1,), (1,)), ((), ())), preferred_element_type=F32)
        i = half * r + lax.broadcasted_iota(jnp.int32, (half, COL_BLOCK), 0)
        score = jnp.where((i >= low) & (i < high), inner * (2.0 * KAPPA), MASKED)
        score_ref[half * r : half * (r + 1), :] = score
        lo = score[:, :128] - KAPPA * data_sq[0]
        hi = score[:, 128:] - KAPPA * data_sq[1]
        at = slice(half * r, half * (r + 1))
        old = big[at, :]
        new = jnp.maximum(old, jnp.maximum(lo, hi))
        total[at, :] = total[at, :] * jnp.exp2(old - new) + (jnp.exp2(lo - new) + jnp.exp2(hi - new))
        big[at, :] = new

    @pl.when(step == pl.num_programs(0) - 1)
    def _():
        rows = []
        for a in range(ROWS // 128):
            at = slice(128 * a, 128 * (a + 1))
            m = big[at, :].T
            s = total[at, :].T
            largest = jnp.max(m, axis=0, keepdims=True)
            summed = jnp.sum(s * jnp.exp2(m - largest), axis=0, keepdims=True)
            rows.append(largest + jnp.log2(summed))
        lse_ref[...] = jnp.broadcast_to(jnp.concatenate(rows, axis=0)[None], lse_ref.shape)


def scores(info, noise, data):
    return pl.pallas_call(
        score_kernel,
        grid=(COLS // COL_BLOCK,),
        in_specs=[
            pl.BlockSpec(memory_space=pltpu.SMEM),
            vmem((N_COL, ROWS, 128)),
            vmem((N_ROW, COL_BLOCK, 256), lambda j: (0, j, 0)),
        ],
        out_specs=[
            vmem((ROWS, COL_BLOCK), lambda j: (0, j)),
            vmem((N_COL, 8, 128)),
            vmem((8, 128)),
            vmem((1, 2, 128), lambda j: (j, 0, 0)),
        ],
        out_shape=[
            jax.ShapeDtypeStruct((ROWS, COLS), F32),
            jax.ShapeDtypeStruct((N_COL, 8, 128), F32),
            jax.ShapeDtypeStruct((8, 128), F32),
            jax.ShapeDtypeStruct((COLS // COL_BLOCK, 2, 128), F32),
        ],
        scratch_shapes=[pltpu.VMEM((ROWS, 128), F32), pltpu.VMEM((ROWS, 128), F32)],
        compiler_params=params(40),
        cost_estimate=pl.CostEstimate(flops=2 * ROWS * COLS * WIDTH, bytes_accessed=20 * MIB, transcendentals=3 << 20),
        name="scores",
    )(info, noise, data)


def merge_lse(parts_ref):
    parts = parts_ref[...]
    largest = jnp.max(parts, axis=0)
    return -(largest + jnp.log2(jnp.sum(jnp.exp2(parts - largest[None]), axis=0)))


def merge_scale(parts_ref):
    return 1.0 / jnp.sum(parts_ref[...], axis=0)


GROUP = 8


def first_columns_kernel(parts_ref, score_ref, lse_ref, noise_ref, column, big, total):
    step = pl.program_id(0)

    @pl.when(step == 0)
    def _():
        potential = merge_lse(parts_ref)
        noise_ref[...] = potential
        for a, piece in enumerate(to_column(potential)):
            column[128 * a : 128 * (a + 1), :] = piece
        big[...] = jnp.full(big.shape, MASKED, F32)
        total[...] = jnp.zeros(total.shape, F32)

    base = step * ROW_BLOCK
    tiles = COLS // 128

    def largest(g, carry):
        shift = column[pl.ds(pl.multiple_of(base + g * GROUP, GROUP), GROUP), :]
        at = pl.ds(pl.multiple_of(g * GROUP, GROUP), GROUP)
        return tuple(jnp.maximum(carry[t], score_ref[at, 128 * t : 128 * (t + 1)] + shift) for t in range(tiles))

    old = tuple(big[:, 128 * t : 128 * (t + 1)] for t in range(tiles))
    new = lax.fori_loop(0, ROW_BLOCK // GROUP, largest, old, unroll=2)

    def add(g, carry):
        shift = column[pl.ds(pl.multiple_of(base + g * GROUP, GROUP), GROUP), :]
        at = pl.ds(pl.multiple_of(g * GROUP, GROUP), GROUP)
        return tuple(
            carry[t] + jnp.exp2(score_ref[at, 128 * t : 128 * (t + 1)] + (shift - new[t])) for t in range(tiles)
        )

    start = tuple(total[:, 128 * t : 128 * (t + 1)] * jnp.exp2(old[t] - new[t]) for t in range(tiles))
    summed = lax.fori_loop(0, ROW_BLOCK // GROUP, add, start, unroll=2)
    for t in range(tiles):
        big[:, 128 * t : 128 * (t + 1)] = new[t]
        total[:, 128 * t : 128 * (t + 1)] = summed[t]

    @pl.when(step == pl.num_programs(0) - 1)
    def _():
        m = jnp.max(big[...], axis=0, keepdims=True)
        s = jnp.sum(total[...] * jnp.exp2(big[...] - m), axis=0, keepdims=True)
        lse_ref[...] = jnp.broadcast_to(from_lanes(m + jnp.log2(s))[None], lse_ref.shape)


def pass_call(kernel, inputs, in_specs, outs, out_specs, scratch, name, transcendentals=0):
    return pl.pallas_call(
        kernel,
        grid=(ROWS // ROW_BLOCK,),
        in_specs=in_specs,
        out_specs=out_specs,
        out_shape=outs,
        scratch_shapes=scratch,
        compiler_params=params(24),
        cost_estimate=pl.CostEstimate(flops=4 * ROWS * COLS, bytes_accessed=8 * MIB, transcendentals=transcendentals),
        name=name,
    )(*inputs)


FROM_COL = vmem((N_COL, 8, 128))
FROM_ROW = vmem((N_ROW, 16, 128))
NOISE = vmem((8, 128))
DATA = vmem((16, 128))
BLOCK = vmem((ROW_BLOCK, COLS), lambda i: (i, 0))
FROM_COL_SHAPE = jax.ShapeDtypeStruct((N_COL, 8, 128), F32)
FROM_ROW_SHAPE = jax.ShapeDtypeStruct((N_ROW, 16, 128), F32)
NOISE_SHAPE = jax.ShapeDtypeStruct((8, 128), F32)
DATA_SHAPE = jax.ShapeDtypeStruct((16, 128), F32)
BLOCK_SHAPE = jax.ShapeDtypeStruct((ROWS, COLS), F32)


def first_columns(parts, score):
    return pass_call(
        first_columns_kernel,
        (parts, score),
        [FROM_COL, BLOCK],
        [FROM_ROW_SHAPE, NOISE_SHAPE],
        [FROM_ROW, NOISE],
        [pltpu.VMEM((ROWS, 128), F32), pltpu.VMEM((8, COLS), F32), pltpu.VMEM((8, COLS), F32)],
        "first_columns",
        ROWS * COLS,
    )


def write_row_sums(sums, out_ref, rows, step):
    per = ROW_BLOCK // 128
    for a in range(per):
        piece = sums[128 * a : 128 * (a + 1), :].T
        rows[pl.ds(step * per + a, 1), :] = jnp.sum(piece, axis=0, keepdims=True)

    @pl.when(step == pl.num_programs(0) - 1)
    def _():
        out_ref[...] = jnp.broadcast_to(rows[...][None], out_ref.shape)


def kernel_matrix_kernel(parts_ref, noise_ref, score_ref, k_ref, sums_ref, data_ref, column, lanes, sums, rows):
    step = pl.program_id(0)

    @pl.when(step == 0)
    def _():
        potential = merge_lse(parts_ref)
        data_ref[...] = potential
        lanes[...] = jnp.broadcast_to(to_lanes(potential), lanes.shape)
        for a, piece in enumerate(to_column(noise_ref[...])):
            column[128 * a : 128 * (a + 1), :] = piece

    base = step * ROW_BLOCK
    tiles = COLS // 128
    shifts = [lanes[:, 128 * t : 128 * (t + 1)] for t in range(tiles)]

    def body(g, _):
        shift = column[pl.ds(pl.multiple_of(base + g * GROUP, GROUP), GROUP), :]
        at = pl.ds(pl.multiple_of(g * GROUP, GROUP), GROUP)
        summed = jnp.zeros((GROUP, 128), F32)
        for t in range(tiles):
            here = slice(128 * t, 128 * (t + 1))
            value = jnp.exp2(score_ref[at, here] + shift + shifts[t])
            k_ref[at, here] = value
            summed += value
        sums[at, :] = summed
        return 0

    lax.fori_loop(0, ROW_BLOCK // GROUP, body, 0, unroll=2)
    write_row_sums(sums, sums_ref, rows, step)


def kernel_matrix(parts, noise_potential, score):
    return pass_call(
        kernel_matrix_kernel,
        (parts, noise_potential, score),
        [FROM_ROW, NOISE, BLOCK],
        [BLOCK_SHAPE, FROM_COL_SHAPE, DATA_SHAPE],
        [BLOCK, FROM_COL, DATA],
        [
            pltpu.VMEM((ROWS, 128), F32),
            pltpu.VMEM((GROUP, COLS), F32),
            pltpu.VMEM((ROW_BLOCK, 128), F32),
            pltpu.VMEM((8, 128), F32),
        ],
        "kernel_matrix",
        ROWS * COLS,
    )


def column_sums_kernel(parts_ref, k_ref, sums_ref, scale_ref, column, total):
    step = pl.program_id(0)

    @pl.when(step == 0)
    def _():
        scale = merge_scale(parts_ref)
        scale_ref[...] = scale
        for a, piece in enumerate(to_column(scale)):
            column[128 * a : 128 * (a + 1), :] = piece
        total[...] = jnp.zeros(total.shape, F32)

    base = step * ROW_BLOCK
    tiles = COLS // 128

    def add(g, carry):
        scale = column[pl.ds(pl.multiple_of(base + g * GROUP, GROUP), GROUP), :]
        at = pl.ds(pl.multiple_of(g * GROUP, GROUP), GROUP)
        return tuple(carry[t] + k_ref[at, 128 * t : 128 * (t + 1)] * scale for t in range(tiles))

    start = tuple(total[:, 128 * t : 128 * (t + 1)] for t in range(tiles))
    summed = lax.fori_loop(0, ROW_BLOCK // GROUP, add, start, unroll=4)
    for t in range(tiles):
        total[:, 128 * t : 128 * (t + 1)] = summed[t]

    @pl.when(step == pl.num_programs(0) - 1)
    def _():
        s = jnp.sum(total[...], axis=0, keepdims=True)
        sums_ref[...] = jnp.broadcast_to(from_lanes(s)[None], sums_ref.shape)


def column_sums(parts, k):
    return pass_call(
        column_sums_kernel,
        (parts, k),
        [FROM_COL, BLOCK],
        [FROM_ROW_SHAPE, NOISE_SHAPE],
        [FROM_ROW, NOISE],
        [pltpu.VMEM((ROWS, 128), F32), pltpu.VMEM((GROUP, COLS), F32)],
        "column_sums",
    )


def row_sums_kernel(parts_ref, k_ref, sums_ref, lanes, sums, rows):
    step = pl.program_id(0)

    @pl.when(step == 0)
    def _():
        lanes[...] = jnp.broadcast_to(to_lanes(merge_scale(parts_ref)), lanes.shape)

    tiles = COLS // 128
    scales = [lanes[:, 128 * t : 128 * (t + 1)] for t in range(tiles)]

    def body(g, _):
        at = pl.ds(pl.multiple_of(g * GROUP, GROUP), GROUP)
        summed = [k_ref[at, 128 * t : 128 * (t + 1)] * scales[t] for t in range(4)]
        for t in range(4, tiles):
            summed[t % 4] += k_ref[at, 128 * t : 128 * (t + 1)] * scales[t]
        sums[at, :] = (summed[0] + summed[1]) + (summed[2] + summed[3])
        return 0

    lax.fori_loop(0, ROW_BLOCK // GROUP, body, 0, unroll=4)
    write_row_sums(sums, sums_ref, rows, step)


def row_sums(parts, k):
    return pass_call(
        row_sums_kernel,
        (parts, k),
        [FROM_ROW, BLOCK],
        [FROM_COL_SHAPE],
        [FROM_COL],
        [pltpu.VMEM((GROUP, COLS), F32), pltpu.VMEM((ROW_BLOCK, 128), F32), pltpu.VMEM((8, 128), F32)],
        "row_sums",
    )[0]


def coupling_kernel(parts_ref, scale_ref, k_ref, p_ref, sums_ref, data_scale_ref, column, lanes, sums, rows):
    step = pl.program_id(0)

    @pl.when(step == 0)
    def _():
        scale = merge_scale(parts_ref)
        data_scale_ref[...] = scale
        lanes[...] = jnp.broadcast_to(to_lanes(scale), lanes.shape)
        for a, piece in enumerate(to_column(scale_ref[...])):
            column[128 * a : 128 * (a + 1), :] = piece

    base = step * ROW_BLOCK
    tiles = COLS // 128

    def body(g, _):
        at = pl.ds(pl.multiple_of(g * 16, 16), 16)
        scale = column[pl.ds(pl.multiple_of(base + g * 16, 16), 16), :]
        summed = jnp.zeros((16, 128), F32)
        for t in range(tiles):
            here = slice(128 * t, 128 * (t + 1))
            value = k_ref[at, here] * (scale * lanes[:, here])
            p_ref[at, here] = value.astype(BF16)
            summed += value
        sums[at, :] = summed
        return 0

    lax.fori_loop(0, ROW_BLOCK // 16, body, 0, unroll=2)
    write_row_sums(sums, sums_ref, rows, step)


def coupling(parts, noise_scale, k):
    return pass_call(
        coupling_kernel,
        (parts, noise_scale, k),
        [FROM_ROW, NOISE, BLOCK],
        [jax.ShapeDtypeStruct((ROWS, COLS), BF16), FROM_COL_SHAPE, DATA_SHAPE],
        [BLOCK, FROM_COL, DATA],
        [
            pltpu.VMEM((ROWS, 128), F32),
            pltpu.VMEM((16, COLS), F32),
            pltpu.VMEM((ROW_BLOCK, 128), F32),
            pltpu.VMEM((8, 128), F32),
        ],
        "coupling",
    )


def target_kernel(p_ref, data_ref, out_ref):
    for r in range(ROWS // 256):
        at = slice(256 * r, 256 * (r + 1))
        summed = jnp.dot(p_ref[at, :], data_ref[0], preferred_element_type=F32)
        out_ref[0, at, :] = summed[:, :128].astype(BF16)
        out_ref[1, at, :] = summed[:, 128:].astype(BF16)


def targets(p, data):
    return pl.pallas_call(
        target_kernel,
        grid=(N_ROW,),
        in_specs=[vmem((ROWS, COLS)), vmem((1, COLS, 256), lambda k: (k, 0, 0))],
        out_specs=vmem((2, ROWS, 128), lambda k: (k, 0, 0)),
        out_shape=jax.ShapeDtypeStruct((N_COL, ROWS, 128), BF16),
        compiler_params=params(32),
        cost_estimate=pl.CostEstimate(flops=2 * ROWS * COLS * WIDTH, bytes_accessed=16 * MIB, transcendentals=0),
        name="targets",
    )(p, data)


def finish_kernel(parts_ref, sums_ref, noise_ref, out_ref):
    inverse = merge_scale(sums_ref)
    for a, piece in enumerate(to_column(inverse)):
        at = slice(128 * a, 128 * (a + 1))
        summed = parts_ref[0, at, :].astype(F32)
        for k in range(1, N_COL):
            summed += parts_ref[k, at, :].astype(F32)
        out_ref[at, :] = summed * piece - noise_ref[at, :].astype(F32)


def finish(parts, sums, noise):
    return pl.pallas_call(
        finish_kernel,
        out_shape=jax.ShapeDtypeStruct((ROWS, 128), F32),
        compiler_params=pltpu.CompilerParams(vmem_limit_bytes=24 * MIB),
        name="finish",
    )(parts, sums, noise)


def swap(x, axis):
    return lax.all_to_all(x, axis, 0, 0, tiled=True)


def per_device(noise_latents, data_latents, noise_sizes, data_sizes):
    places = jnp.stack([lax.axis_index("row") * ROWS, lax.axis_index("col") * COLS]).astype(jnp.int32)
    info = jnp.concatenate([noise_sizes, data_sizes, places])
    data = lax.all_gather(data_latents, "row")
    noise = lax.all_gather(noise_latents, "col")
    score, lse, noise_sq, data_sq = scores(info, noise, data)
    lse, noise_first = first_columns(swap(lse, "col"), score)
    k, sums, data_first = kernel_matrix(swap(lse, "row"), noise_first, score)
    sums, _ = column_sums(swap(sums, "col"), k)
    sums = row_sums(swap(sums, "row"), k)
    sums, noise_scale = column_sums(swap(sums, "col"), k)
    p, sums, data_scale = coupling(swap(sums, "row"), noise_scale, k)
    sums = swap(sums, "col")
    parts = swap(targets(p, data), "col")
    velocity = finish(parts, sums, noise_latents)
    noise_potential = (EPS * LN2) * (noise_first + jnp.log2(noise_scale)) + noise_sq / WIDTH
    data_potential = (EPS * LN2) * (data_first + jnp.log2(data_scale)) + data_sq.reshape(16, 128) / WIDTH
    return velocity, noise_potential.reshape(ROWS), data_potential.reshape(COLS)


def solution(mesh):
    placed = (P("row", "col"), P("col", "row"), P(), P())
    return jax.shard_map(
        per_device,
        mesh=mesh,
        in_specs=placed,
        out_specs=(P("row", "col"), P("row"), P("col")),
        check_vma=False,
    )
```

time: 702 us -> 310 us (0.44)
  blocking collectives: 371 us -> 60.6 us
  other arithmetic: 73.6 us -> 1.97 us
  waiting for transfers between devices: 212 us -> 168 us
  Pallas kernels: 0 us -> 42.2 us
  matrix products: 29.9 us -> 0 us
  local copies, waits for them, and re-layouts: 0.56 us -> 11.7 us
  starting transfers between devices: 0.11 us -> 10.9 us
    pmax x7 -> x0, blocking collectives: 191 us -> none  [the longest x4 153 us: lse_over_cols(): largest = lax.pmax(jnp.max(masked, axis=1), 'col')]
    psum x7 -> x0, blocking collectives: 180 us -> none  [the longest x4 142 us: lse_over_cols(): lax.psum(jnp.sum(jnp.where(same_cluster, jnp.exp(masked - largest[:, None...]
    psum x1 -> x0, waiting for transfers between devices: 99 us -> none  [per_device(): summed = lax.psum(partials.astype(jnp.bfloat16), 'col').astype(jnp.float32)]
    all_to_all x0 -> x2, waiting for transfers between devices: none -> 60.8 us  [swap(): return lax.all_to_all(x, axis, 0, 0, tiled=True)]
    all_to_all x0 -> x6, blocking collectives: none -> 60.6 us  [swap(): return lax.all_to_all(x, axis, 0, 0, tiled=True)]
    reduce_sum x11 -> x0, other arithmetic: 44.1 us -> none  [the longest x4 20.3 us: lse_over_cols(): jnp.sum(jnp.where(same_cluster, jnp.exp(masked - largest[:, None]), 0.0),...]
    pallas_call x0 -> x9, Pallas kernels: none -> 42.2 us  [the longest x1 15.5 us: scores(): pl.pallas_call(score_kernel, grid=(COLS // COL_BLOCK,), in_specs=[pl.Bloc...]
    dot_general x2 -> x0, matrix products: 29.9 us -> none  [the longest x1 15.9 us: per_device(): partials = jnp.dot(weights, data_full, preferred_element_type=jnp.float32)]
  transfers between devices with their start and end apart: 3 -> 4, of which waited for: 3 -> 3; matrix products, arithmetic and copies ran while one was open for 1% -> 1% of each run, Pallas kernels for 0% -> 3%
where the time goes in v1:
time: 310 us
  waiting for transfers between devices  168 us (54%)
  blocking collectives  60.6 us (20%)
  Pallas kernels  42.2 us (14%)
  between operations  14.1 us (5%)
  local copies, waits for them, and re-layouts  11.7 us (4%)
  starting transfers between devices  10.9 us (4%)
    all_to_all x2, waiting for transfers between devices, swap(): return lax.all_to_all(x, axis, 0, 0, tiled=True)  60.8 us
    all_to_all x6, blocking collectives, swap(): return lax.all_to_all(x, axis, 0, 0, tiled=True)  60.6 us
    all_gather x1, waiting for transfers between devices, per_device(): noise = lax.all_gather(noise_latents, 'col')  54.9 us
    all_gather x1, waiting for transfers between devices, per_device(): data = lax.all_gather(data_latents, 'row')  51.1 us
    pallas_call x1, Pallas kernels, scores(): pl.pallas_call(score_kernel, grid=(COLS // COL_BLOCK,), in_specs=[pl.Bloc...  15.5 us
    pallas_call x6, Pallas kernels, pass_call(): pl.pallas_call(kernel, grid=(ROWS // ROW_BLOCK,), in_specs=in_specs, out_...  13.1 us
    unnamed x12, local copies, waits for them, and re-layouts  11.7 us
    all_to_all x2, starting transfers between devices, swap(): return lax.all_to_all(x, axis, 0, 0, tiled=True)  10.8 us
  transfers between devices with their start and end apart: 4, of which 3 were waited for; matrix products, arithmetic and copies ran while one was open for 1% of the time, Pallas kernels for 3%

profile of v1, /device:TPU:0, one launch (start us, length us, event | category | flops | bytes accessed | tf_op | source)
XLA Modules:
  0.0 309.7 jit_solution(8103757526958371201)
XLA Ops:
  7.2 0.0 all-gather.5.cloned.1.call-start
  7.2 0.7 all-gather.5.cloned.1.call-update
  7.9 0.0 all-gather.7.cloned.1.call-start
  7.9 0.7 all-gather.7.cloned.1.call-update
  8.7 0.8 pad_add_fusion.info_ref
  9.4 54.9 %all-gather.5.cloned.1.call-done = bf16[16384,128]{1,0:T(8,128)(2,1)} async-done(((bf16[1024,128]{1,0:T(8,128)(2,1)}), bf16[16384,128]{1,0:T(8,128)(2,1)}) %all-gather.5.cloned.1.call-update) | async-done | bytes 4194320 | tf_op jit(solution)/shard_map/all_gather | solution.py:480
  64.3 51.1 %all-gather.7.cloned.1.call-done = bf16[16384,256]{1,0:T(8,128)(2,1)} async-done(((bf16[2048,256]{1,0:T(8,128)(2,1)}), bf16[16384,256]{1,0:T(8,128)(2,1)}) %all-gather.7.cloned.1.call-update) | async-done | bytes 8388624 | tf_op jit(solution)/shard_map/all_gather | solution.py:479
  115.4 0.0 copy-start.3
  115.4 2.2 copy-done.3
  117.5 15.5 %scores.1 = (f32[1024,2048]{1,0:T(8,128)S(1)}, f32[16,8,128]{2,1,0:T(8,128)S(1)}, f32[8,128]{1,0:T(8,128)S(1)}, f32[8,2,128]{2,1,0:T(2,128)S(1)}) custom-call(s32[18]{0:T(128)S(1)} %pad_add_fusion.info_ref, bf16[16,1024,128]{2,1,0:T(8,128)(2,1)S(1)} %bitcast.11, bf16[8,2048,256]{2,1,0:T(8,128)(2,1)} %bitcast.9), custom_call_target="tpu_custom_call" | custom-call | flops 8589934592 | bytes 20971520 | tf_op jit(solution)/shard_map/scores/pallas_call | solution.py:127
  133.0 14.4 %all_to_all.40.parts_ref = f32[16,8,128]{2,1,0:T(8,128)S(1)} all-to-all(f32[16,8,128]{2,1,0:T(8,128)S(1)} %get-tuple-element.18), channel_id=1, replica_groups=mesh['row'=8,'col'=16] {'col'}, dimensions={0} | all-to-all | bytes 131072 | tf_op jit(solution)/shard_map/all_to_all | solution.py:473
  147.4 3.3 %first_columns.1 = (f32[8,16,128]{2,1,0:T(8,128)S(1)}, f32[8,128]{1,0:T(8,128)S(1)}) custom-call(f32[16,8,128]{2,1,0:T(8,128)S(1)} %all_to_all.40.parts_ref, f32[1024,2048]{1,0:T(8,128)S(1)} %get-tuple-element.19.score_ref), custom_call_target="tpu_custom_call" | custom-call | flops 8388608 | bytes 8388608 | tf_op jit(solution)/shard_map/first_columns/pallas_call | solution.py:211
  150.7 8.6 %all_to_all.41.parts_ref = f32[8,16,128]{2,1,0:T(8,128)S(1)} all-to-all(f32[8,16,128]{2,1,0:T(8,128)S(1)} %get-tuple-element.20), channel_id=1, replica_groups=mesh['row'=8,'col'=16] {'row'}, dimensions={0} | all-to-all | bytes 131072 | tf_op jit(solution)/shard_map/all_to_all | solution.py:473
  159.3 3.0 kernel_matrix.1
  162.3 10.8 %all_to_all.42.parts_ref = f32[16,8,128]{2,1,0:T(8,128)S(1)} all-to-all(f32[16,8,128]{2,1,0:T(8,128)S(1)} %get-tuple-element.22), channel_id=1, replica_groups=mesh['row'=8,'col'=16] {'col'}, dimensions={0} | all-to-all | bytes 131072 | tf_op jit(solution)/shard_map/all_to_all | solution.py:473
  173.1 1.6 column_sums.2
  174.7 8.0 %all_to_all.43.parts_ref = f32[8,16,128]{2,1,0:T(8,128)S(1)} all-to-all(f32[8,16,128]{2,1,0:T(8,128)S(1)} %get-tuple-element.24), channel_id=1, replica_groups=mesh['row'=8,'col'=16] {'row'}, dimensions={0} | all-to-all | bytes 131072 | tf_op jit(solution)/shard_map/all_to_all | solution.py:473
  182.7 1.2 row_sums.1
  184.0 10.8 %all_to_all.44.parts_ref = f32[16,8,128]{2,1,0:T(8,128)S(1)} all-to-all(f32[16,8,128]{2,1,0:T(8,128)S(1)} %row_sums.1), channel_id=1, replica_groups=mesh['row'=8,'col'=16] {'col'}, dimensions={0} | all-to-all | bytes 131072 | tf_op jit(solution)/shard_map/all_to_all | solution.py:473
  194.8 1.0 column_sums.3
  195.8 8.0 %all_to_all.45.parts_ref = f32[8,16,128]{2,1,0:T(8,128)S(1)} all-to-all(f32[8,16,128]{2,1,0:T(8,128)S(1)} %get-tuple-element.25), channel_id=1, replica_groups=mesh['row'=8,'col'=16] {'row'}, dimensions={0} | all-to-all | bytes 131072 | tf_op jit(solution)/shard_map/all_to_all | solution.py:473
  203.8 2.9 coupling.1
  206.8 0.0 copy-start.4
  206.8 2.0 copy-done.4
  208.7 3.5 %all-to-all-start.7 = ((f32[16,8,128]{2,1,0:T(8,128)}), f32[16,8,128]{2,1,0:T(8,128)S(1)}, u32[]{:S(2)}, u32[]{:S(2)}) async-start(f32[16,8,128]{2,1,0:T(8,128)} %get-tuple-element.28), calls=%async_computation.7 | async-start | bytes 131072 | tf_op jit(solution)/shard_map/all_to_all | solution.py:473
  212.2 0.0 copy-start.2
  212.2 3.4 %copy-done.2 = bf16[16384,256]{1,0:T(8,128)(2,1)S(1)} copy-done((bf16[16384,256]{1,0:T(8,128)(2,1)S(1)}, bf16[16384,256]{1,0:T(8,128)(2,1)}, u32[]{:S(2)}) %copy-start.2) | copy-done | bytes 8388632
  215.6 0.0 copy-start.5
  215.6 2.2 copy-done.5
  217.8 10.1 %targets.1 = bf16[16,1024,128]{2,1,0:T(8,128)(2,1)S(1)} custom-call(bf16[1024,2048]{1,0:T(8,128)(2,1)S(1)} %copy-done.5, bf16[8,2048,256]{2,1,0:T(8,128)(2,1)S(1)} %bitcast.10), custom_call_target="tpu_custom_call" | custom-call | flops 8589934592 | bytes 16777216 | tf_op jit(solution)/shard_map/targets/pallas_call | solution.py:441
  227.9 0.0 copy-start
  227.9 2.0 copy-done
  229.9 0.0 copy-start.1
  229.9 0.0 all-to-all-done.7.sums_ref
  229.9 7.3 %all-to-all-start.6 = ((bf16[16,1024,128]{2,1,0:T(8,128)(2,1)}), bf16[16,1024,128]{2,1,0:T(8,128)(2,1)}, u32[]{:S(2)}, u32[]{:S(2)}) async-start(bf16[16,1024,128]{2,1,0:T(8,128)(2,1)} %copy-done), calls=%async_computation.6 | async-start | bytes 8388608 | tf_op jit(solution)/shard_map/all_to_all | solution.py:473
  237.3 0.6 add_bitcast_fusion.1
  237.9 0.6 add_bitcast_fusion
  238.5 60.8 %all-to-all-done.6.parts_ref = bf16[16,1024,128]{2,1,0:T(8,128)(2,1)} async-done(((bf16[16,1024,128]{2,1,0:T(8,128)(2,1)}), bf16[16,1024,128]{2,1,0:T(8,128)(2,1)}, u32[]{:S(2)}, u32[]{:S(2)}) %all-to-all-start.6) | async-done | bytes 4194336 | tf_op jit(solution)/shard_map/all_to_all | solution.py:473
  299.3 0.0 copy-done.1
  299.3 3.6 %finish.1 = f32[1024,128]{1,0:T(8,128)} custom-call(bf16[16,1024,128]{2,1,0:T(8,128)(2,1)} %all-to-all-done.6.parts_ref, f32[16,8,128]{2,1,0:T(8,128)S(1)} %all-to-all-done.7.sums_ref, bf16[1024,128]{1,0:T(8,128)(2,1)S(1)} %copy-done.1), custom_call_target="tpu_custom_call" | custom-call | tf_op jit(solution)/shard_map/finish/pallas_call | solution.py:464
  (1 shorter events, 0.0 us)
Async XLA Ops:
  7.2 57.1 %all-gather.5.cloned.1.call-start = ((), (), s32[]{:S(2)}) async-start(), calls=%async_computation.8 | async-start | bytes 4456448 | tf_op jit(solution)/shard_map/all_gather | solution.py:480
  7.9 107.5 %all-gather.7.cloned.1.call-start = ((), (), s32[]{:S(2)}) async-start(), calls=%async_computation.9 | async-start | bytes 9437184 | tf_op jit(solution)/shard_map/all_gather | solution.py:479
  115.4 2.2 copy-start.3
  206.8 2.0 copy-start.4
  208.7 21.2 %all-to-all-start.7 = ((f32[16,8,128]{2,1,0:T(8,128)}), f32[16,8,128]{2,1,0:T(8,128)S(1)}, u32[]{:S(2)}, u32[]{:S(2)}) async-start(f32[16,8,128]{2,1,0:T(8,128)} %get-tuple-element.28), calls=%async_computation.7 | async-start | bytes 131072 | tf_op jit(solution)/shard_map/all_to_all | solution.py:473
  212.2 3.4 %copy-start.2 = (bf16[16384,256]{1,0:T(8,128)(2,1)S(1)}, bf16[16384,256]{1,0:T(8,128)(2,1)}, u32[]{:S(2)}) copy-start(bf16[16384,256]{1,0:T(8,128)(2,1)} %all-gather.7.cloned.1.call-done) | copy-start | bytes 25165828
  215.6 2.2 copy-start.5
  227.9 2.0 copy-start
  229.9 69.4 %copy-start.1 = (bf16[1024,128]{1,0:T(8,128)(2,1)S(1)}, bf16[1024,128]{1,0:T(8,128)(2,1)}, u32[]{:S(2)}) copy-start(bf16[1024,128]{1,0:T(8,128)(2,1)} %noise_ref.1) | copy-start | bytes 786436
  229.9 69.4 %all-to-all-start.6 = ((bf16[16,1024,128]{2,1,0:T(8,128)(2,1)}), bf16[16,1024,128]{2,1,0:T(8,128)(2,1)}, u32[]{:S(2)}, u32[]{:S(2)}) async-start(bf16[16,1024,128]{2,1,0:T(8,128)(2,1)} %copy-done), calls=%async_computation.6 | async-start | bytes 8388608 | tf_op jit(solution)/shard_map/all_to_all | solution.py:473
Sparse Core Ops, SparseCore 0:
  10.1 54.1 all-gather.4
  66.0 49.2 all-gather.6

commit v2 on v1

--- a/solution.py
+++ b/solution.py
@@ -21,6 +21,7 @@
 WIDTH = 2048
 COL_BLOCK = 256
 ROW_BLOCK = 256
+HALF = 512
 N_ROW = 8
 N_COL = 16
 KAPPA = LOG2E / (WIDTH * EPS)
@@ -53,19 +54,69 @@
     return jnp.concatenate([row[:, 128 * a : 128 * (a + 1)] for a in range(row.shape[1] // 128)], axis=0)
 
 
-def score_kernel(info_ref, noise_ref, data_ref, score_ref, lse_ref, noise_sq_ref, data_sq_ref, big, total):
+def arrange_kernel(info_ref, *refs):
+    out_ref, noise_sq_ref = refs[10:]
+    z, x = info_ref[18], info_ref[19]
+    sums = []
+    for half in range(2):
+        own, before, after, second_a, second_b = refs[5 * half : 5 * half + 5]
+        at = slice(HALF * half, HALF * (half + 1))
+        squares = jnp.zeros((HALF, 128), F32)
+        for far, source in ((0, own), (1, before), (3, after), (2, None)):
+            for near in range(4):
+                if source is not None:
+                    piece = source[near]
+                else:
+                    piece = second_a[near] if near < 2 else second_b[near - 2]
+                if half == 0:
+                    index = lax.rem(z + 4 - far, 4) * 4 + lax.rem(x + 4 - near, 4)
+                else:
+                    index = lax.rem(z + 4 - near, 4) * 4 + lax.rem(x + 4 - far, 4)
+                out_ref[at, pl.ds(pl.multiple_of(index * 128, 128), 128)] = piece
+                squares += piece.astype(F32) * piece.astype(F32)
+        for a in range(HALF // 128):
+            sums.append(jnp.sum(squares[128 * a : 128 * (a + 1), :].T, axis=0, keepdims=True))
+    noise_sq_ref[...] = jnp.concatenate(sums, axis=0)
+
+
+def arrange(info, pieces):
+    return pl.pallas_call(
+        arrange_kernel,
+        in_specs=[pl.BlockSpec(memory_space=pltpu.SMEM)] + [pl.BlockSpec(memory_space=pltpu.VMEM)] * 10,
+        out_shape=[jax.ShapeDtypeStruct((ROWS, WIDTH), BF16), NOISE_SHAPE],
+        compiler_params=pltpu.CompilerParams(vmem_limit_bytes=24 * MIB),
+        cost_estimate=pl.CostEstimate(flops=4 << 20, bytes_accessed=8 * MIB, transcendentals=0),
+        name="arrange",
+    )(info, *pieces)
+
+
+def over_x(v, d):
+    return lax.ppermute(v, "col", [(4 * z + x, 4 * z + (x + d) % 4) for z in range(4) for x in range(4)])
+
+
+def over_z(v, d):
+    return lax.ppermute(v, "col", [(4 * z + x, 4 * ((z + d) % 4) + x) for z in range(4) for x in range(4)])
+
+
+def gather_noise(noise):
+    gathered = []
+    for half, (first, second) in enumerate(((over_x, over_z), (over_z, over_x))):
+        own = noise[HALF * half : HALF * (half + 1)]
+        own = jnp.stack([own] + [first(own, d) for d in (1, 2, 3)])
+        gathered.append((own, second(own, 1), second(own, 3), second))
+    pieces = []
+    for own, before, after, second in gathered:
+        pieces += [own, before, after, second(before[:2], 1), second(after[2:], 3)]
+    return pieces
+
+
+def score_kernel(info_ref, noise_ref, data_ref, score_ref, lse_ref, data_sq_ref, big, total):
     step = pl.program_id(0)
 
     @pl.when(step == 0)
     def _():
         big[...] = jnp.full(big.shape, MASKED, F32)
         total[...] = jnp.zeros(total.shape, F32)
-        for a in range(ROWS // 128):
-            squares = jnp.zeros((128, 128), F32)
-            for k in range(N_COL):
-                piece = noise_ref[k, 128 * a : 128 * (a + 1), :].astype(F32)
-                squares += piece * piece
-            noise_sq_ref[a : a + 1, :] = jnp.sum(squares.T, axis=0, keepdims=True)
 
     data = jnp.concatenate([data_ref[k] for k in range(N_ROW)], axis=1)
     data_sq = []
@@ -97,8 +148,7 @@
 
     half = 256
     for r in range(ROWS // half):
-        noise = jnp.concatenate([noise_ref[k, half * r : half * (r + 1), :] for k in range(N_COL)], axis=1)
-        inner = lax.dot_general(noise, data, (((1,), (1,)), ((), ())), preferred_element_type=F32)
+        inner = lax.dot_general(noise_ref[half * r : half * (r + 1), :], data, (((1,), (1,)), ((), ())), preferred_element_type=F32)
         i = half * r + lax.broadcasted_iota(jnp.int32, (half, COL_BLOCK), 0)
         score = jnp.where((i >= low) & (i < high), inner * (2.0 * KAPPA), MASKED)
         score_ref[half * r : half * (r + 1), :] = score
@@ -129,19 +179,17 @@
         grid=(COLS // COL_BLOCK,),
         in_specs=[
             pl.BlockSpec(memory_space=pltpu.SMEM),
-            vmem((N_COL, ROWS, 128)),
+            vmem((ROWS, WIDTH)),
             vmem((N_ROW, COL_BLOCK, 256), lambda j: (0, j, 0)),
         ],
         out_specs=[
             vmem((ROWS, COL_BLOCK), lambda j: (0, j)),
             vmem((N_COL, 8, 128)),
-            vmem((8, 128)),
             vmem((1, 2, 128), lambda j: (j, 0, 0)),
         ],
         out_shape=[
             jax.ShapeDtypeStruct((ROWS, COLS), F32),
             jax.ShapeDtypeStruct((N_COL, 8, 128), F32),
-            jax.ShapeDtypeStruct((8, 128), F32),
             jax.ShapeDtypeStruct((COLS // COL_BLOCK, 2, 128), F32),
         ],
         scratch_shapes=[pltpu.VMEM((ROWS, 128), F32), pltpu.VMEM((ROWS, 128), F32)],
@@ -382,91 +430,181 @@
     )[0]
 
 
-def coupling_kernel(parts_ref, scale_ref, k_ref, p_ref, sums_ref, data_scale_ref, column, lanes, sums, rows):
+def coupling_kernel(
+    parts_ref, scale_ref, noise_first, noise_sq, data_first, data_sq, k_ref,
+    pa_ref, pb_ref, sums_ref, noise_ref, data_ref, column, lanes, sums,
+):
     step = pl.program_id(0)
 
     @pl.when(step == 0)
     def _():
         scale = merge_scale(parts_ref)
-        data_scale_ref[...] = scale
         lanes[...] = jnp.broadcast_to(to_lanes(scale), lanes.shape)
         for a, piece in enumerate(to_column(scale_ref[...])):
             column[128 * a : 128 * (a + 1), :] = piece
+        noise_ref[...] = (EPS * LN2) * (noise_first[...] + jnp.log2(scale_ref[...])) + noise_sq[...] * (1.0 / WIDTH)
+        potential = (EPS * LN2) * (data_first[...] + jnp.log2(scale))
+        for k in range(8):
+            data_ref[2 * k : 2 * k + 2, :] = potential[2 * k : 2 * k + 2, :] + data_sq[k] * (1.0 / WIDTH)
 
     base = step * ROW_BLOCK
     tiles = COLS // 128
 
-    def body(g, _):
-        at = pl.ds(pl.multiple_of(g * 16, 16), 16)
-        scale = column[pl.ds(pl.multiple_of(base + g * 16, 16), 16), :]
-        summed = jnp.zeros((16, 128), F32)
-        for t in range(tiles):
-            here = slice(128 * t, 128 * (t + 1))
-            value = k_ref[at, here] * (scale * lanes[:, here])
-            p_ref[at, here] = value.astype(BF16)
-            summed += value
-        sums[at, :] = summed
-        return 0
-
-    lax.fori_loop(0, ROW_BLOCK // 16, body, 0, unroll=2)
-    write_row_sums(sums, sums_ref, rows, step)
-
-
-def coupling(parts, noise_scale, k):
+    def block(p_ref):
+        def body(g, _):
+            at = pl.ds(pl.multiple_of(g * 16, 16), 16)
+            scale = column[pl.ds(pl.multiple_of(base + g * 16, 16), 16), :]
+            summed = jnp.zeros((16, 128), F32)
+            for t in range(tiles):
+                here = slice(128 * t, 128 * (t + 1))
+                value = k_ref[at, here] * (scale * lanes[:, here])
+                p_ref[at, here] = value.astype(BF16)
+                summed += value
+            sums[at, :] = summed
+            return 0
+
+        lax.fori_loop(0, ROW_BLOCK // 16, body, 0, unroll=2)
+
+    @pl.when(step < 2)
+    def _():
+        block(pa_ref)
+
+    @pl.when(step >= 2)
+    def _():
+        block(pb_ref)
+
+    per = ROW_BLOCK // 128
+    for a in range(per):
+        piece = sums[128 * a : 128 * (a + 1), :].T
+        sums_ref[pl.ds(step * per + a, 1), :] = jnp.sum(piece, axis=0, keepdims=True)
+
+
+def coupling(parts, noise_scale, noise_first, noise_sq, data_first, data_sq, k):
+    half = jax.ShapeDtypeStruct((HALF, COLS), BF16)
     return pass_call(
         coupling_kernel,
-        (parts, noise_scale, k),
-        [FROM_ROW, NOISE, BLOCK],
-        [jax.ShapeDtypeStruct((ROWS, COLS), BF16), FROM_COL_SHAPE, DATA_SHAPE],
-        [BLOCK, FROM_COL, DATA],
+        (parts, noise_scale, noise_first, noise_sq, data_first, data_sq, k),
+        [FROM_ROW, NOISE, NOISE, NOISE, DATA, vmem((8, 2, 128)), BLOCK],
+        [half, half, NOISE_SHAPE, NOISE_SHAPE, DATA_SHAPE],
+        [
+            vmem((ROW_BLOCK, COLS), lambda i: (jnp.minimum(i, 1), 0)),
+            vmem((ROW_BLOCK, COLS), lambda i: (jnp.maximum(i - 2, 0), 0)),
+            NOISE,
+            NOISE,
+            DATA,
+        ],
         [
             pltpu.VMEM((ROWS, 128), F32),
             pltpu.VMEM((16, COLS), F32),
             pltpu.VMEM((ROW_BLOCK, 128), F32),
-            pltpu.VMEM((8, 128), F32),
         ],
         "coupling",
     )
 
 
-def target_kernel(p_ref, data_ref, out_ref):
-    for r in range(ROWS // 256):
-        at = slice(256 * r, 256 * (r + 1))
-        summed = jnp.dot(p_ref[at, :], data_ref[0], preferred_element_type=F32)
-        out_ref[0, at, :] = summed[:, :128].astype(BF16)
-        out_ref[1, at, :] = summed[:, 128:].astype(BF16)
-
-
-def targets(p, data):
+EXTRA = 16
+
+
+def split(value):
+    high = value.astype(BF16)
+    return high, (value - high.astype(F32)).astype(BF16)
+
+
+def target_kernel(side, d, info_ref, p_ref, sums_ref, *refs):
+    data_refs, out_ref = refs[:-1], refs[-1]
+    if side == 0:
+        lanes = pl.ds(pl.multiple_of(lax.rem(info_ref[19] + d, 2) * 128, 128), 128)
+        data = jnp.concatenate([ref[0, :, lanes] for ref in data_refs], axis=1)
+    else:
+        data = data_refs[0][0]
+    summed = jnp.dot(p_ref[...], data, preferred_element_type=F32).astype(BF16)
+    high, low = split(sums_ref[4 * side : 4 * side + 4, :])
+    tail = jnp.concatenate([high, low, high, low], axis=0)
+    for b in range(2):
+        out_ref[b, :HALF, :] = summed[:, 128 * b : 128 * (b + 1)]
+        out_ref[b, HALF:, :] = tail
+
+
+def message(side, d, info, p, sums, data):
+    if side == 0:
+        chunks = [
+            vmem((1, COLS, 256), lambda g, f, b=b: (4 * g + 2 * b + lax.rem(f[19] + d, 4) // 2, 0, 0)) for b in (0, 1)
+        ]
+    else:
+        chunks = [vmem((1, COLS, 256), lambda g, f: (2 * lax.rem(f[18] + d, 4) + g, 0, 0))]
     return pl.pallas_call(
-        target_kernel,
-        grid=(N_ROW,),
-        in_specs=[vmem((ROWS, COLS)), vmem((1, COLS, 256), lambda k: (k, 0, 0))],
-        out_specs=vmem((2, ROWS, 128), lambda k: (k, 0, 0)),
-        out_shape=jax.ShapeDtypeStruct((N_COL, ROWS, 128), BF16),
-        compiler_params=params(32),
-        cost_estimate=pl.CostEstimate(flops=2 * ROWS * COLS * WIDTH, bytes_accessed=16 * MIB, transcendentals=0),
+        functools.partial(target_kernel, side, d),
+        grid_spec=pltpu.PrefetchScalarGridSpec(
+            num_scalar_prefetch=1,
+            grid=(2,),
+            in_specs=[vmem((HALF, COLS)), NOISE] + chunks,
+            out_specs=vmem((2, HALF + EXTRA, 128), lambda g, f: (g, 0, 0)),
+        ),
+        out_shape=jax.ShapeDtypeStruct((4, HALF + EXTRA, 128), BF16),
+        compiler_params=params(24),
+        cost_estimate=pl.CostEstimate(flops=ROWS * COLS * WIDTH // 4, bytes_accessed=4 * MIB, transcendentals=0),
         name="targets",
-    )(p, data)
-
-
-def finish_kernel(parts_ref, sums_ref, noise_ref, out_ref):
-    inverse = merge_scale(sums_ref)
-    for a, piece in enumerate(to_column(inverse)):
-        at = slice(128 * a, 128 * (a + 1))
-        summed = parts_ref[0, at, :].astype(F32)
-        for k in range(1, N_COL):
-            summed += parts_ref[k, at, :].astype(F32)
-        out_ref[at, :] = summed * piece - noise_ref[at, :].astype(F32)
-
-
-def finish(parts, sums, noise):
+    )(info, p, sums, *[data] * len(chunks))
+
+
+def row_sums_of(ref, index=None):
+    high, low = (ref[HALF + 4 * i : HALF + 4 * i + 4, :] if index is None else ref[index, HALF + 4 * i : HALF + 4 * i + 4, :] for i in (0, 1))
+    return high.astype(F32) + low.astype(F32)
+
+
+def combine_kernel(side, info_ref, own, r1, r2, r3, keep_ref, s1, s2, s3):
+    place = info_ref[18 + side]
+    sums = (row_sums_of(own, 0) + row_sums_of(r1, 0)) + (row_sums_of(r2, 0) + row_sums_of(r3, 0))
+    high, low = split(sums)
+    tail = jnp.concatenate([high, low, high, low], axis=0)
+
+    def summed(index):
+        at = slice(0, HALF)
+        return (own[index, at, :].astype(F32) + r1[index, at, :].astype(F32)) + (
+            r2[index, at, :].astype(F32) + r3[index, at, :].astype(F32)
+        )
+
+    for d, out_ref in ((1, s1), (2, s2), (3, s3)):
+        out_ref[:HALF, :] = summed(lax.rem(place + d, 4)).astype(BF16)
+        out_ref[HALF:, :] = tail
+    keep_ref[:HALF, :] = summed(place)
+    keep_ref[HALF:, :] = jnp.concatenate([sums, jnp.zeros((EXTRA - 4, 128), F32)], axis=0)
+
+
+def combine(side, info, parts):
+    return pl.pallas_call(
+        functools.partial(combine_kernel, side),
+        in_specs=[pl.BlockSpec(memory_space=pltpu.SMEM)] + [pl.BlockSpec(memory_space=pltpu.VMEM)] * 4,
+        out_shape=[jax.ShapeDtypeStruct((HALF + EXTRA, 128), F32)] + [jax.ShapeDtypeStruct((HALF + EXTRA, 128), BF16)] * 3,
+        compiler_params=pltpu.CompilerParams(vmem_limit_bytes=16 * MIB),
+        cost_estimate=pl.CostEstimate(flops=1 << 20, bytes_accessed=3 * MIB, transcendentals=0),
+        name="combine",
+    )(info, *parts)
+
+
+def finish_kernel(noise_ref, *refs):
+    out_ref = refs[-1]
+    for half in range(2):
+        own, *others = refs[4 * half : 4 * half + 4]
+        sums = own[HALF : HALF + 4, :]
+        for other in others:
+            sums += row_sums_of(other)
+        for a, inverse in enumerate(to_column(1.0 / sums)):
+            here = slice(128 * a, 128 * (a + 1))
+            at = slice(HALF * half + 128 * a, HALF * half + 128 * (a + 1))
+            summed = own[here, :]
+            for other in others:
+                summed += other[here, :].astype(F32)
+            out_ref[at, :] = summed * inverse - noise_ref[at, :].astype(F32)
+
+
+def finish(noise, parts):
     return pl.pallas_call(
         finish_kernel,
         out_shape=jax.ShapeDtypeStruct((ROWS, 128), F32),
-        compiler_params=pltpu.CompilerParams(vmem_limit_bytes=24 * MIB),
+        compiler_params=pltpu.CompilerParams(vmem_limit_bytes=16 * MIB),
         name="finish",
-    )(parts, sums, noise)
+    )(noise, *parts)
 
 
 def swap(x, axis):
@@ -474,22 +612,31 @@
 
 
 def per_device(noise_latents, data_latents, noise_sizes, data_sizes):
-    places = jnp.stack([lax.axis_index("row") * ROWS, lax.axis_index("col") * COLS]).astype(jnp.int32)
+    row, col = lax.axis_index("row"), lax.axis_index("col")
+    places = jnp.stack([row * ROWS, col * COLS, col // 4, col % 4]).astype(jnp.int32)
     info = jnp.concatenate([noise_sizes, data_sizes, places])
     data = lax.all_gather(data_latents, "row")
-    noise = lax.all_gather(noise_latents, "col")
-    score, lse, noise_sq, data_sq = scores(info, noise, data)
+    noise, noise_sq = arrange(info, gather_noise(noise_latents))
+    score, lse, data_sq = scores(info, noise, data)
     lse, noise_first = first_columns(swap(lse, "col"), score)
     k, sums, data_first = kernel_matrix(swap(lse, "row"), noise_first, score)
     sums, _ = column_sums(swap(sums, "col"), k)
     sums = row_sums(swap(sums, "row"), k)
     sums, noise_scale = column_sums(swap(sums, "col"), k)
-    p, sums, data_scale = coupling(swap(sums, "row"), noise_scale, k)
-    sums = swap(sums, "col")
-    parts = swap(targets(p, data), "col")
-    velocity = finish(parts, sums, noise_latents)
-    noise_potential = (EPS * LN2) * (noise_first + jnp.log2(noise_scale)) + noise_sq / WIDTH
-    data_potential = (EPS * LN2) * (data_first + jnp.log2(data_scale)) + data_sq.reshape(16, 128) / WIDTH
+    *p, sums, noise_potential, data_potential = coupling(
+        swap(sums, "row"), noise_scale, noise_first, noise_sq, data_first, data_sq, k
+    )
+    way = (over_x, over_z)
+    parts = [[None] * 4, [None] * 4]
+    for d in (2, 1, 3, 0):
+        for side in (0, 1):
+            made = message(side, d, info, p[side], sums, data)
+            parts[side][d] = way[side](made, d) if d else made
+    ends = []
+    for side in (0, 1):
+        keep, *others = combine(side, info, parts[side])
+        ends += [keep] + [way[1 - side](v, d) for d, v in zip((1, 2, 3), others)]
+    velocity = finish(noise_latents, ends)
     return velocity, noise_potential.reshape(ROWS), data_potential.reshape(COLS)
 
 

time: 310 us -> 217 us (0.70)
  waiting for transfers between devices: 168 us -> 42.8 us
  starting transfers between devices: 10.9 us -> 38.7 us
  Pallas kernels: 42.2 us -> 50.6 us
    all_to_all x2 -> x0, waiting for transfers between devices: 60.8 us -> none  [swap(): return lax.all_to_all(x, axis, 0, 0, tiled=True)]
    all_gather x1 -> x0, waiting for transfers between devices: 54.9 us -> none  [per_device(): noise = lax.all_gather(noise_latents, 'col')]
    all_gather x1, waiting for transfers between devices: 51.1 us -> 4.38 us  [per_device(): data = lax.all_gather(data_latents, 'row')]
    ppermute x0 -> x26, starting transfers between devices: none -> 38.6 us  [the longest x13 20.5 us: over_z(): lax.ppermute(v, 'col', [(4 * z + x, 4 * ((z + d) % 4) + x) for z in range...]
    ppermute x0 -> x26, waiting for transfers between devices: none -> 37.8 us  [the longest x13 21.4 us: over_x(): lax.ppermute(v, 'col', [(4 * z + x, 4 * z + (x + d) % 4) for z in range(4...]
    all_to_all x2 -> x0, starting transfers between devices: 10.8 us -> none  [swap(): return lax.all_to_all(x, axis, 0, 0, tiled=True)]
    pallas_call x1 -> x11, Pallas kernels: 10.1 us -> 20.9 us  [the longest x8 16.2 us: message(): pl.pallas_call(functools.partial(target_kernel, side, d), grid_spec=pltpu...]
    unnamed x12 -> x10, local copies, waits for them, and re-layouts: 11.7 us -> 4.23 us
  transfers between devices with their start and end apart: 4 -> 27, of which waited for: 3 -> 12; matrix products, arithmetic and copies ran while one was open for 1% -> 2% of each run, Pallas kernels for 3% -> 9%
where the time goes in v2:
time: 217 us; the launch traced here: 216 us
  blocking collectives  60.9 us (28%)
  Pallas kernels  50.6 us (23%)
  waiting for transfers between devices  42.8 us (20%)
  starting transfers between devices  38.7 us (18%)
  between operations  14.2 us (7%)
  local copies, waits for them, and re-layouts  8.91 us (4%)
    all_to_all x6, blocking collectives, swap(): return lax.all_to_all(x, axis, 0, 0, tiled=True)  60.9 us
    ppermute x13, waiting for transfers between devices, over_x(): lax.ppermute(v, 'col', [(4 * z + x, 4 * z + (x + d) % 4) for z in range(4...  21.4 us
    ppermute x13, starting transfers between devices, over_z(): lax.ppermute(v, 'col', [(4 * z + x, 4 * ((z + d) % 4) + x) for z in range...  20.5 us
    ppermute x13, starting transfers between devices, over_x(): lax.ppermute(v, 'col', [(4 * z + x, 4 * z + (x + d) % 4) for z in range(4...  18.1 us
    ppermute x13, waiting for transfers between devices, over_z(): lax.ppermute(v, 'col', [(4 * z + x, 4 * ((z + d) % 4) + x) for z in range...  16.4 us
    pallas_call x8, Pallas kernels, message(): pl.pallas_call(functools.partial(target_kernel, side, d), grid_spec=pltpu...  16.2 us
    pallas_call x1, Pallas kernels, scores(): pl.pallas_call(score_kernel, grid=(COLS // COL_BLOCK,), in_specs=[pl.Bloc...  15.6 us
    pallas_call x6, Pallas kernels, pass_call(): pl.pallas_call(kernel, grid=(ROWS // ROW_BLOCK,), in_specs=in_specs, out_...  13 us
  transfers between devices with their start and end apart: 27, of which 12 were waited for; matrix products, arithmetic and copies ran while one was open for 2% of the time, Pallas kernels for 9%

profile of v2, /device:TPU:0, one launch (start us, length us, event | category | flops | bytes accessed | tf_op | source)
XLA Modules:
  0.0 216.2 jit_solution(18265214484918942239)
XLA Ops:
  8.9 4.0 %collective-permute-start.8 = (bf16[512,128]{1,0:T(8,128)(2,1)S(1)}, bf16[512,128]{1,0:T(8,128)(2,1)S(1)}, u32[]{:S(2)}, u32[]{:S(2)}) collective-permute-start(bf16[512,128]{1,0:T(8,128)(2,1)S(1)} %get-tuple-element.58), channel_id=1, source_target_pairs={{0,8},{1,9},{2,10},{3,11},{4,12},{5,13},{6,14},{7,15},{8,0},{9,1},... | collective-permute-start | bytes 393224 | tf_op jit(solution)/shard_map/ppermute | solution.py:98
  14.0 2.2 %collective-permute-start.9 = (bf16[512,128]{1,0:T(8,128)(2,1)S(1)}, bf16[512,128]{1,0:T(8,128)(2,1)S(1)}, u32[]{:S(2)}, u32[]{:S(2)}) collective-permute-start(bf16[512,128]{1,0:T(8,128)(2,1)S(1)} %get-tuple-element.58), channel_id=1, source_target_pairs={{0,12},{1,13},{2,14},{3,15},{4,0},{5,1},{6,2},{7,3},{8,4},{9,5},{1... | collective-permute-start | bytes 393224 | tf_op jit(solution)/shard_map/ppermute | solution.py:98
  16.2 3.0 %collective-permute-start.1 = (bf16[512,128]{1,0:T(8,128)(2,1)S(1)}, bf16[512,128]{1,0:T(8,128)(2,1)S(1)}, u32[]{:S(2)}, u32[]{:S(2)}) collective-permute-start(bf16[512,128]{1,0:T(8,128)(2,1)S(1)} %get-tuple-element.57), channel_id=1, source_target_pairs={{0,2},{1,3},{2,0},{3,1},{4,6},{5,7},{6,4},{7,5},{8,10},{9,11},{10,... | collective-permute-start | bytes 393224 | tf_op jit(solution)/shard_map/ppermute | solution.py:94
  19.8 2.6 %collective-permute-start.2 = (bf16[512,128]{1,0:T(8,128)(2,1)S(1)}, bf16[512,128]{1,0:T(8,128)(2,1)S(1)}, u32[]{:S(2)}, u32[]{:S(2)}) collective-permute-start(bf16[512,128]{1,0:T(8,128)(2,1)S(1)} %get-tuple-element.57), channel_id=1, source_target_pairs={{0,3},{1,0},{2,1},{3,2},{4,7},{5,4},{6,5},{7,6},{8,11},{9,8},{10,9... | collective-permute-start | bytes 393224 | tf_op jit(solution)/shard_map/ppermute | solution.py:94
  22.9 1.7 collective-permute-start.10
  24.7 1.3 collective-permute-done
  27.5 1.4 collective-permute-start.3
  28.9 7.4 %collective-permute-done.11.refs_7_ = bf16[4,512,128]{2,1,0:T(8,128)(2,1)S(1)} collective-permute-done((bf16[4,512,128]{2,1,0:T(8,128)(2,1)S(1)}, bf16[4,512,128]{2,1,0:T(8,128)(2,1)S(1)}, u32[]{:S(2)}, u32[]{:S(2)}) %collective-permute-start.11) | collective-permute-done | bytes 524320 | tf_op jit(solution)/shard_map/ppermute | solution.py:94
  37.0 3.5 %collective-permute-start.13 = (bf16[2,512,128]{2,1,0:T(8,128)(2,1)}, bf16[2,512,128]{2,1,0:T(8,128)(2,1)S(1)}, u32[]{:S(2)}, u32[]{:S(2)}) collective-permute-start(bf16[2,512,128]{2,1,0:T(8,128)(2,1)} %slice.27), channel_id=1, source_target_pairs={{0,3},{1,0},{2,1},{3,2},{4,7},{5,4},{6,5},{7,6},{8,11},{9,8},{10,9... | collective-permute-start | bytes 786440 | tf_op jit(solution)/shard_map/ppermute | solution.py:94
  42.0 1.4 collective-permute-start.6
  45.5 3.9 %collective-permute-done.12.refs_8_ = bf16[2,512,128]{2,1,0:T(8,128)(2,1)} collective-permute-done((bf16[2,512,128]{2,1,0:T(8,128)(2,1)}, bf16[2,512,128]{2,1,0:T(8,128)(2,1)}, u32[]{:S(2)}, u32[]{:S(2)}) %collective-permute-start.12) | collective-permute-done | bytes 262176 | tf_op jit(solution)/shard_map/ppermute | solution.py:94
  49.4 3.1 %collective-permute-done.5.refs_3_ = bf16[2,512,128]{2,1,0:T(8,128)(2,1)} collective-permute-done((bf16[2,512,128]{2,1,0:T(8,128)(2,1)}, bf16[2,512,128]{2,1,0:T(8,128)(2,1)}, u32[]{:S(2)}, u32[]{:S(2)}) %collective-permute-start.5) | collective-permute-done | bytes 262176 | tf_op jit(solution)/shard_map/ppermute | solution.py:98
  52.4 3.1 %arrange.1 = (bf16[1024,2048]{1,0:T(8,128)(2,1)S(1)}, f32[8,128]{1,0:T(8,128)S(1)}) custom-call(s32[20]{0:T(128)S(1)} %concatenate.3.info_ref, bf16[4,512,128]{2,1,0:T(8,128)(2,1)S(1)} %pad_maximum_fusion.refs_0_, bf16[4,512,128]{2,1,0:T(8,128)(2,1)S(1)} %collective-permute-done.3.refs_1_, bf16[4,512,128]{2,1,0:T(8,128)(2,1)S(1)} %collective-permute-done.4.refs_2_, ...), custom_call_target="tpu_custom_call" | custom-call | flops 4194304 | bytes 8388608 | tf_op jit(solution)/shard_map/arrange/pallas_call | solution.py:83
  55.5 2.0 copy-done.1
  57.6 4.4 %all-gather.3.cloned.1.call-done = bf16[16384,256]{1,0:T(8,128)(2,1)} async-done(((bf16[2048,256]{1,0:T(8,128)(2,1)}), bf16[16384,256]{1,0:T(8,128)(2,1)}) %all-gather.3.cloned.1.call-update) | async-done | bytes 8388624 | tf_op jit(solution)/shard_map/all_gather | solution.py:618
  61.9 2.2 %copy-done.2 = bf16[1024,2048]{1,0:T(8,128)(2,1)S(1)} copy-done((bf16[1024,2048]{1,0:T(8,128)(2,1)S(1)}, bf16[1024,2048]{1,0:T(8,128)(2,1)}, u32[]{:S(2)}) %copy-start.2) | copy-done | bytes 4194328
  64.1 15.6 %scores.1 = (f32[1024,2048]{1,0:T(8,128)S(1)}, f32[16,8,128]{2,1,0:T(8,128)S(1)}, f32[8,2,128]{2,1,0:T(2,128)S(1)}) custom-call(s32[20]{0:T(128)S(1)} %concatenate.3.info_ref, bf16[1024,2048]{1,0:T(8,128)(2,1)S(1)} %copy-done.2, bf16[8,2048,256]{2,1,0:T(8,128)(2,1)} %bitcast.17), custom_call_target="tpu_custom_call" | custom-call | flops 8589934592 | bytes 20971520 | tf_op jit(solution)/shard_map/scores/pallas_call | solution.py:177
  79.8 14.4 %all_to_all.30.parts_ref = f32[16,8,128]{2,1,0:T(8,128)S(1)} all-to-all(f32[16,8,128]{2,1,0:T(8,128)S(1)} %get-tuple-element.30), channel_id=1, replica_groups=mesh['row'=8,'col'=16] {'col'}, dimensions={0} | all-to-all | bytes 131072 | tf_op jit(solution)/shard_map/all_to_all | solution.py:611
  94.2 3.3 %first_columns.1 = (f32[8,16,128]{2,1,0:T(8,128)S(1)}, f32[8,128]{1,0:T(8,128)S(1)}) custom-call(f32[16,8,128]{2,1,0:T(8,128)S(1)} %all_to_all.30.parts_ref, f32[1024,2048]{1,0:T(8,128)S(1)} %get-tuple-element.31.score_ref), custom_call_target="tpu_custom_call" | custom-call | flops 8388608 | bytes 8388608 | tf_op jit(solution)/shard_map/first_columns/pallas_call | solution.py:259
  97.5 8.6 %all_to_all.31.parts_ref = f32[8,16,128]{2,1,0:T(8,128)S(1)} all-to-all(f32[8,16,128]{2,1,0:T(8,128)S(1)} %get-tuple-element.32), channel_id=1, replica_groups=mesh['row'=8,'col'=16] {'row'}, dimensions={0} | all-to-all | bytes 131072 | tf_op jit(solution)/shard_map/all_to_all | solution.py:611
  106.1 3.0 %kernel_matrix.1 = (f32[1024,2048]{1,0:T(8,128)S(1)}, f32[16,8,128]{2,1,0:T(8,128)S(1)}, f32[16,128]{1,0:T(8,128)S(1)}) custom-call(f32[8,16,128]{2,1,0:T(8,128)S(1)} %all_to_all.31.parts_ref, f32[8,128]{1,0:T(8,128)S(1)} %get-tuple-element.33.noise_ref.noise_first, f32[1024,2048]{1,0:T(8,128)S(1)} %get-tuple-element.31.score_ref), custom_call_target="tpu_custom_call" | custom-call | flops 8388608 | bytes 8388608 | tf_op jit(solution)/shard_map/kernel_matrix/pallas_call | solution.py:259
  109.1 10.8 %all_to_all.32.parts_ref = f32[16,8,128]{2,1,0:T(8,128)S(1)} all-to-all(f32[16,8,128]{2,1,0:T(8,128)S(1)} %get-tuple-element.34), channel_id=1, replica_groups=mesh['row'=8,'col'=16] {'col'}, dimensions={0} | all-to-all | bytes 131072 | tf_op jit(solution)/shard_map/all_to_all | solution.py:611
  119.9 1.6 column_sums.2
  121.5 8.0 %all_to_all.33.parts_ref = f32[8,16,128]{2,1,0:T(8,128)S(1)} all-to-all(f32[8,16,128]{2,1,0:T(8,128)S(1)} %get-tuple-element.36), channel_id=1, replica_groups=mesh['row'=8,'col'=16] {'row'}, dimensions={0} | all-to-all | bytes 131072 | tf_op jit(solution)/shard_map/all_to_all | solution.py:611
  129.5 1.2 row_sums.1
  130.8 10.8 %all_to_all.34.parts_ref = f32[16,8,128]{2,1,0:T(8,128)S(1)} all-to-all(f32[16,8,128]{2,1,0:T(8,128)S(1)} %row_sums.1), channel_id=1, replica_groups=mesh['row'=8,'col'=16] {'col'}, dimensions={0} | all-to-all | bytes 131072 | tf_op jit(solution)/shard_map/all_to_all | solution.py:611
  142.6 8.3 %all_to_all.35.parts_ref = f32[8,16,128]{2,1,0:T(8,128)S(1)} all-to-all(f32[8,16,128]{2,1,0:T(8,128)S(1)} %get-tuple-element.37), channel_id=1, replica_groups=mesh['row'=8,'col'=16] {'row'}, dimensions={0} | all-to-all | bytes 131072 | tf_op jit(solution)/shard_map/all_to_all | solution.py:611
  150.9 2.8 %coupling.1 = (bf16[512,2048]{1,0:T(8,128)(2,1)S(1)}, bf16[512,2048]{1,0:T(8,128)(2,1)S(1)}, f32[8,128]{1,0:T(8,128)S(1)}, f32[8,128]{1,0:T(8,128)}, f32[16,128]{1,0:T(8,128)}) custom-call(f32[8,16,128]{2,1,0:T(8,128)S(1)} %all_to_all.35.parts_ref, f32[8,128]{1,0:T(8,128)S(1)} %get-tuple-element.38.scale_ref, ...), custom_call_target="tpu_custom_call" | custom-call | flops 8388608 | bytes 8388608 | tf_op jit(solution)/shard_map/coupling/pallas_call | solution.py:259
  153.7 2.0 targets.13
  156.3 2.0 targets.14
  158.3 2.1 collective-permute-start.21
  160.5 2.0 targets.15
  162.5 1.3 collective-permute-start.22
  163.8 2.0 targets.11
  165.8 2.0 targets.9
  168.5 2.0 targets.10
  170.6 2.2 %collective-permute-start.15 = (bf16[4,528,128]{2,1,0:T(8,128)(2,1)S(1)}, bf16[4,528,128]{2,1,0:T(8,128)(2,1)S(1)}, u32[]{:S(2)}, u32[]{:S(2)}) collective-permute-start(bf16[4,528,128]{2,1,0:T(8,128)(2,1)S(1)} %targets.10), channel_id=1, source_target_pairs={{0,2},{1,3},{2,0},{3,1},{4,6},{5,7},{6,4},{7,5},{8,10},{9,11},{10,... | collective-permute-start | bytes 1622024 | tf_op jit(solution)/shard_map/ppermute | solution.py:94
  172.7 9.8 %collective-permute-done.20.r1 = bf16[4,528,128]{2,1,0:T(8,128)(2,1)S(1)} collective-permute-done((bf16[4,528,128]{2,1,0:T(8,128)(2,1)S(1)}, bf16[4,528,128]{2,1,0:T(8,128)(2,1)S(1)}, u32[]{:S(2)}, u32[]{:S(2)}) %collective-permute-start.20) | collective-permute-done | bytes 540704 | tf_op jit(solution)/shard_map/ppermute | solution.py:98
  182.5 1.2 collective-permute-start.16
  183.7 2.0 targets.12.own
  187.5 2.0 targets.8.own
  189.5 1.4 collective-permute-start.24
  190.9 2.0 collective-permute-done.14.r1
  192.9 2.6 %collective-permute-done.15.r2 = bf16[4,528,128]{2,1,0:T(8,128)(2,1)S(1)} collective-permute-done((bf16[4,528,128]{2,1,0:T(8,128)(2,1)S(1)}, bf16[4,528,128]{2,1,0:T(8,128)(2,1)S(1)}, u32[]{:S(2)}, u32[]{:S(2)}) %collective-permute-start.15) | collective-permute-done | bytes 540704 | tf_op jit(solution)/shard_map/ppermute | solution.py:94
  195.5 3.4 %collective-permute-done.16.r3 = bf16[4,528,128]{2,1,0:T(8,128)(2,1)S(1)} collective-permute-done((bf16[4,528,128]{2,1,0:T(8,128)(2,1)S(1)}, bf16[4,528,128]{2,1,0:T(8,128)(2,1)S(1)}, u32[]{:S(2)}, u32[]{:S(2)}) %collective-permute-start.16) | collective-permute-done | bytes 540704 | tf_op jit(solution)/shard_map/ppermute | solution.py:94
  200.6 1.6 collective-permute-start.18
  202.3 2.5 %collective-permute-start.19 = (bf16[528,128]{1,0:T(8,128)(2,1)S(1)}, bf16[528,128]{1,0:T(8,128)(2,1)S(1)}, u32[]{:S(2)}, u32[]{:S(2)}) collective-permute-start(bf16[528,128]{1,0:T(8,128)(2,1)S(1)} %get-tuple-element.47), channel_id=1, source_target_pairs={{0,12},{1,13},{2,14},{3,15},{4,0},{5,1},{6,2},{7,3},{8,4},{9,5},{1... | collective-permute-start | bytes 405512 | tf_op jit(solution)/shard_map/ppermute | solution.py:98
  204.8 2.7 %collective-permute-done.17.refs_1_ = bf16[528,128]{1,0:T(8,128)(2,1)S(1)} collective-permute-done((bf16[528,128]{1,0:T(8,128)(2,1)S(1)}, bf16[528,128]{1,0:T(8,128)(2,1)S(1)}, u32[]{:S(2)}, u32[]{:S(2)}) %collective-permute-start.17) | collective-permute-done | bytes 135200 | tf_op jit(solution)/shard_map/ppermute | solution.py:98
  (51 shorter events, 17.2 us)
Async XLA Ops:
  7.2 54.8 %all-gather.3.cloned.1.call-start = ((), (), s32[]{:S(2)}) async-start(), calls=%async_computation.6 | async-start | bytes 9437184 | tf_op jit(solution)/shard_map/all_gather | solution.py:618
  8.9 10.9 %collective-permute-start.8 = (bf16[512,128]{1,0:T(8,128)(2,1)S(1)}, bf16[512,128]{1,0:T(8,128)(2,1)S(1)}, u32[]{:S(2)}, u32[]{:S(2)}) collective-permute-start(bf16[512,128]{1,0:T(8,128)(2,1)S(1)} %get-tuple-element.58), channel_id=1, source_target_pairs={{0,8},{1,9},{2,10},{3,11},{4,12},{5,13},{6,14},{7,15},{8,0},{9,1},... | collective-permute-start | bytes 393224 | tf_op jit(solution)/shard_map/ppermute | solution.py:98
  13.0 9.5 %collective-permute-start.7 = (bf16[512,128]{1,0:T(8,128)(2,1)S(1)}, bf16[512,128]{1,0:T(8,128)(2,1)S(1)}, u32[]{:S(2)}, u32[]{:S(2)}) collective-permute-start(bf16[512,128]{1,0:T(8,128)(2,1)S(1)} %get-tuple-element.58), channel_id=1, source_target_pairs={{0,4},{1,5},{2,6},{3,7},{4,8},{5,9},{6,10},{7,11},{8,12},{9,13},{1... | collective-permute-start | bytes 393224 | tf_op jit(solution)/shard_map/ppermute | solution.py:98
  14.0 8.5 %collective-permute-start.9 = (bf16[512,128]{1,0:T(8,128)(2,1)S(1)}, bf16[512,128]{1,0:T(8,128)(2,1)S(1)}, u32[]{:S(2)}, u32[]{:S(2)}) collective-permute-start(bf16[512,128]{1,0:T(8,128)(2,1)S(1)} %get-tuple-element.58), channel_id=1, source_target_pairs={{0,12},{1,13},{2,14},{3,15},{4,0},{5,1},{6,2},{7,3},{8,4},{9,5},{1... | collective-permute-start | bytes 393224 | tf_op jit(solution)/shard_map/ppermute | solution.py:98
  16.2 8.4 %collective-permute-start.1 = (bf16[512,128]{1,0:T(8,128)(2,1)S(1)}, bf16[512,128]{1,0:T(8,128)(2,1)S(1)}, u32[]{:S(2)}, u32[]{:S(2)}) collective-permute-start(bf16[512,128]{1,0:T(8,128)(2,1)S(1)} %get-tuple-element.57), channel_id=1, source_target_pairs={{0,2},{1,3},{2,0},{3,1},{4,6},{5,7},{6,4},{7,5},{8,10},{9,11},{10,... | collective-permute-start | bytes 393224 | tf_op jit(solution)/shard_map/ppermute | solution.py:94
  19.2 6.8 %collective-permute-start = (bf16[512,128]{1,0:T(8,128)(2,1)S(1)}, bf16[512,128]{1,0:T(8,128)(2,1)S(1)}, u32[]{:S(2)}, u32[]{:S(2)}) collective-permute-start(bf16[512,128]{1,0:T(8,128)(2,1)S(1)} %get-tuple-element.57), channel_id=1, source_target_pairs={{0,1},{1,2},{2,3},{3,0},{4,5},{5,6},{6,7},{7,4},{8,9},{9,10},{10,1... | collective-permute-start | bytes 393224 | tf_op jit(solution)/shard_map/ppermute | solution.py:94
  19.8 6.9 %collective-permute-start.2 = (bf16[512,128]{1,0:T(8,128)(2,1)S(1)}, bf16[512,128]{1,0:T(8,128)(2,1)S(1)}, u32[]{:S(2)}, u32[]{:S(2)}) collective-permute-start(bf16[512,128]{1,0:T(8,128)(2,1)S(1)} %get-tuple-element.57), channel_id=1, source_target_pairs={{0,3},{1,0},{2,1},{3,2},{4,7},{5,4},{6,5},{7,6},{8,11},{9,8},{10,9... | collective-permute-start | bytes 393224 | tf_op jit(solution)/shard_map/ppermute | solution.py:94
  22.6 13.8 %collective-permute-start.11 = (bf16[4,512,128]{2,1,0:T(8,128)(2,1)S(1)}, bf16[4,512,128]{2,1,0:T(8,128)(2,1)S(1)}, u32[]{:S(2)}, u32[]{:S(2)}) collective-permute-start(bf16[4,512,128]{2,1,0:T(8,128)(2,1)S(1)} %pad_maximum_fusion.1.refs_5_), channel_id=1, source_target_pairs={{0,3},{1,0},{2,1},{3,2},{4,7},{5,4},{6,5},{7,6},{8,11},{9,8},{10,9... | collective-permute-start | bytes 1572872 | tf_op jit(solution)/shard_map/ppermute | solution.py:94
  22.9 17.6 %collective-permute-start.10 = (bf16[4,512,128]{2,1,0:T(8,128)(2,1)S(1)}, bf16[4,512,128]{2,1,0:T(8,128)(2,1)S(1)}, u32[]{:S(2)}, u32[]{:S(2)}) collective-permute-start(bf16[4,512,128]{2,1,0:T(8,128)(2,1)S(1)} %pad_maximum_fusion.1.refs_5_), channel_id=1, source_target_pairs={{0,1},{1,2},{2,3},{3,0},{4,5},{5,6},{6,7},{7,4},{8,9},{9,10},{10,1... | collective-permute-start | bytes 1572872 | tf_op jit(solution)/shard_map/ppermute | solution.py:94
  26.8 14.5 %collective-permute-start.4 = (bf16[4,512,128]{2,1,0:T(8,128)(2,1)S(1)}, bf16[4,512,128]{2,1,0:T(8,128)(2,1)S(1)}, u32[]{:S(2)}, u32[]{:S(2)}) collective-permute-start(bf16[4,512,128]{2,1,0:T(8,128)(2,1)S(1)} %pad_maximum_fusion.refs_0_), channel_id=1, source_target_pairs={{0,12},{1,13},{2,14},{3,15},{4,0},{5,1},{6,2},{7,3},{8,4},{9,5},{1... | collective-permute-start | bytes 1572872 | tf_op jit(solution)/shard_map/ppermute | solution.py:98
  27.5 15.9 %collective-permute-start.3 = (bf16[4,512,128]{2,1,0:T(8,128)(2,1)S(1)}, bf16[4,512,128]{2,1,0:T(8,128)(2,1)S(1)}, u32[]{:S(2)}, u32[]{:S(2)}) collective-permute-start(bf16[4,512,128]{2,1,0:T(8,128)(2,1)S(1)} %pad_maximum_fusion.refs_0_), channel_id=1, source_target_pairs={{0,4},{1,5},{2,6},{3,7},{4,8},{5,9},{6,10},{7,11},{8,12},{9,13},{1... | collective-permute-start | bytes 1572872 | tf_op jit(solution)/shard_map/ppermute | solution.py:98
  37.0 8.4 %collective-permute-start.13 = (bf16[2,512,128]{2,1,0:T(8,128)(2,1)}, bf16[2,512,128]{2,1,0:T(8,128)(2,1)S(1)}, u32[]{:S(2)}, u32[]{:S(2)}) collective-permute-start(bf16[2,512,128]{2,1,0:T(8,128)(2,1)} %slice.27), channel_id=1, source_target_pairs={{0,3},{1,0},{2,1},{3,2},{4,7},{5,4},{6,5},{7,6},{8,11},{9,8},{10,9... | collective-permute-start | bytes 786440 | tf_op jit(solution)/shard_map/ppermute | solution.py:94
  41.2 8.1 %collective-permute-start.12 = (bf16[2,512,128]{2,1,0:T(8,128)(2,1)}, bf16[2,512,128]{2,1,0:T(8,128)(2,1)}, u32[]{:S(2)}, u32[]{:S(2)}) collective-permute-start(bf16[2,512,128]{2,1,0:T(8,128)(2,1)} %slice.26), channel_id=1, source_target_pairs={{0,1},{1,2},{2,3},{3,0},{4,5},{5,6},{6,7},{7,4},{8,9},{9,10},{10,1... | collective-permute-start | bytes 786440 | tf_op jit(solution)/shard_map/ppermute | solution.py:94
  42.0 7.4 %collective-permute-start.6 = (bf16[2,512,128]{2,1,0:T(8,128)(2,1)}, bf16[2,512,128]{2,1,0:T(8,128)(2,1)}, u32[]{:S(2)}, u32[]{:S(2)}) collective-permute-start(bf16[2,512,128]{2,1,0:T(8,128)(2,1)} %slice.25), channel_id=1, source_target_pairs={{0,12},{1,13},{2,14},{3,15},{4,0},{5,1},{6,2},{7,3},{8,4},{9,5},{1... | collective-permute-start | bytes 786440 | tf_op jit(solution)/shard_map/ppermute | solution.py:98
  44.1 8.3 %collective-permute-start.5 = (bf16[2,512,128]{2,1,0:T(8,128)(2,1)}, bf16[2,512,128]{2,1,0:T(8,128)(2,1)}, u32[]{:S(2)}, u32[]{:S(2)}) collective-permute-start(bf16[2,512,128]{2,1,0:T(8,128)(2,1)} %slice.24), channel_id=1, source_target_pairs={{0,4},{1,5},{2,6},{3,7},{4,8},{5,9},{6,10},{7,11},{8,12},{9,13},{1... | collective-permute-start | bytes 786440 | tf_op jit(solution)/shard_map/ppermute | solution.py:98
  55.5 2.0 copy-start.1
  61.9 2.2 %copy-start.2 = (bf16[1024,2048]{1,0:T(8,128)(2,1)S(1)}, bf16[1024,2048]{1,0:T(8,128)(2,1)}, u32[]{:S(2)}) copy-start(bf16[1024,2048]{1,0:T(8,128)(2,1)} %copy-done.1) | copy-start | bytes 12582916
  141.6 12.1 %slice-start = ((s8[8388608]{0:T(1024)(128)(4,1)}), s8[4194304]{0:T(1024)(128)(4,1)S(1)}, s32[]{:S(2)}) async-start(s8[8388608]{0:T(1024)(128)(4,1)} %bitcast.18), calls=%async_computation.7 | async-start | bytes 8388608
  142.6 11.1 %slice-start.1 = ((s8[8388608]{0:T(1024)(128)(4,1)}), s8[4194304]{0:T(1024)(128)(4,1)S(1)}, s32[]{:S(2)}) async-start(s8[8388608]{0:T(1024)(128)(4,1)} %bitcast.18), calls=%async_computation.8 | async-start | bytes 8388608
  155.7 26.8 %collective-permute-start.20 = (bf16[4,528,128]{2,1,0:T(8,128)(2,1)S(1)}, bf16[4,528,128]{2,1,0:T(8,128)(2,1)S(1)}, u32[]{:S(2)}, u32[]{:S(2)}) collective-permute-start(bf16[4,528,128]{2,1,0:T(8,128)(2,1)S(1)} %targets.13), channel_id=1, source_target_pairs={{0,4},{1,5},{2,6},{3,7},{4,8},{5,9},{6,10},{7,11},{8,12},{9,13},{1... | collective-permute-start | bytes 1622024 | tf_op jit(solution)/shard_map/ppermute | solution.py:98
  158.3 27.4 %collective-permute-start.21 = (bf16[4,528,128]{2,1,0:T(8,128)(2,1)S(1)}, bf16[4,528,128]{2,1,0:T(8,128)(2,1)S(1)}, u32[]{:S(2)}, u32[]{:S(2)}) collective-permute-start(bf16[4,528,128]{2,1,0:T(8,128)(2,1)S(1)} %targets.14), channel_id=1, source_target_pairs={{0,8},{1,9},{2,10},{3,11},{4,12},{5,13},{6,14},{7,15},{8,0},{9,1},... | collective-permute-start | bytes 1622024 | tf_op jit(solution)/shard_map/ppermute | solution.py:98
  162.5 23.2 %collective-permute-start.22 = (bf16[4,528,128]{2,1,0:T(8,128)(2,1)S(1)}, bf16[4,528,128]{2,1,0:T(8,128)(2,1)S(1)}, u32[]{:S(2)}, u32[]{:S(2)}) collective-permute-start(bf16[4,528,128]{2,1,0:T(8,128)(2,1)S(1)} %targets.15), channel_id=1, source_target_pairs={{0,12},{1,13},{2,14},{3,15},{4,0},{5,1},{6,2},{7,3},{8,4},{9,5},{1... | collective-permute-start | bytes 1622024 | tf_op jit(solution)/shard_map/ppermute | solution.py:98
  167.9 25.1 %collective-permute-start.14 = (bf16[4,528,128]{2,1,0:T(8,128)(2,1)S(1)}, bf16[4,528,128]{2,1,0:T(8,128)(2,1)S(1)}, u32[]{:S(2)}, u32[]{:S(2)}) collective-permute-start(bf16[4,528,128]{2,1,0:T(8,128)(2,1)S(1)} %targets.9), channel_id=1, source_target_pairs={{0,1},{1,2},{2,3},{3,0},{4,5},{5,6},{6,7},{7,4},{8,9},{9,10},{10,1... | collective-permute-start | bytes 1622024 | tf_op jit(solution)/shard_map/ppermute | solution.py:94
  170.6 24.9 %collective-permute-start.15 = (bf16[4,528,128]{2,1,0:T(8,128)(2,1)S(1)}, bf16[4,528,128]{2,1,0:T(8,128)(2,1)S(1)}, u32[]{:S(2)}, u32[]{:S(2)}) collective-permute-start(bf16[4,528,128]{2,1,0:T(8,128)(2,1)S(1)} %targets.10), channel_id=1, source_target_pairs={{0,2},{1,3},{2,0},{3,1},{4,6},{5,7},{6,4},{7,5},{8,10},{9,11},{10,... | collective-permute-start | bytes 1622024 | tf_op jit(solution)/shard_map/ppermute | solution.py:94
  182.5 16.4 %collective-permute-start.16 = (bf16[4,528,128]{2,1,0:T(8,128)(2,1)S(1)}, bf16[4,528,128]{2,1,0:T(8,128)(2,1)S(1)}, u32[]{:S(2)}, u32[]{:S(2)}) collective-permute-start(bf16[4,528,128]{2,1,0:T(8,128)(2,1)S(1)} %targets.11), channel_id=1, source_target_pairs={{0,3},{1,0},{2,1},{3,2},{4,7},{5,4},{6,5},{7,6},{8,11},{9,8},{10,9... | collective-permute-start | bytes 1622024 | tf_op jit(solution)/shard_map/ppermute | solution.py:94
  186.5 21.8 %copy-start = (bf16[1024,128]{1,0:T(8,128)(2,1)S(1)}, bf16[1024,128]{1,0:T(8,128)(2,1)}, u32[]{:S(2)}) copy-start(bf16[1024,128]{1,0:T(8,128)(2,1)} %noise_ref.1) | copy-start | bytes 786436
  186.5 15.7 %collective-permute-start.23 = (bf16[528,128]{1,0:T(8,128)(2,1)S(1)}, bf16[528,128]{1,0:T(8,128)(2,1)S(1)}, u32[]{:S(2)}, u32[]{:S(2)}) collective-permute-start(bf16[528,128]{1,0:T(8,128)(2,1)S(1)} %get-tuple-element.50), channel_id=1, source_target_pairs={{0,1},{1,2},{2,3},{3,0},{4,5},{5,6},{6,7},{7,4},{8,9},{9,10},{10,1... | collective-permute-start | bytes 405512 | tf_op jit(solution)/shard_map/ppermute | solution.py:94
  189.5 15.3 %collective-permute-start.24 = (bf16[528,128]{1,0:T(8,128)(2,1)S(1)}, bf16[528,128]{1,0:T(8,128)(2,1)S(1)}, u32[]{:S(2)}, u32[]{:S(2)}) collective-permute-start(bf16[528,128]{1,0:T(8,128)(2,1)S(1)} %get-tuple-element.51), channel_id=1, source_target_pairs={{0,2},{1,3},{2,0},{3,1},{4,6},{5,7},{6,4},{7,5},{8,10},{9,11},{10,... | collective-permute-start | bytes 405512 | tf_op jit(solution)/shard_map/ppermute | solution.py:94
  192.9 11.9 %collective-permute-start.25 = (bf16[528,128]{1,0:T(8,128)(2,1)S(1)}, bf16[528,128]{1,0:T(8,128)(2,1)S(1)}, u32[]{:S(2)}, u32[]{:S(2)}) collective-permute-start(bf16[528,128]{1,0:T(8,128)(2,1)S(1)} %get-tuple-element.52), channel_id=1, source_target_pairs={{0,3},{1,0},{2,1},{3,2},{4,7},{5,4},{6,5},{7,6},{8,11},{9,8},{10,9... | collective-permute-start | bytes 405512 | tf_op jit(solution)/shard_map/ppermute | solution.py:94
  199.8 7.7 %collective-permute-start.17 = (bf16[528,128]{1,0:T(8,128)(2,1)S(1)}, bf16[528,128]{1,0:T(8,128)(2,1)S(1)}, u32[]{:S(2)}, u32[]{:S(2)}) collective-permute-start(bf16[528,128]{1,0:T(8,128)(2,1)S(1)} %get-tuple-element.45), channel_id=1, source_target_pairs={{0,4},{1,5},{2,6},{3,7},{4,8},{5,9},{6,10},{7,11},{8,12},{9,13},{1... | collective-permute-start | bytes 405512 | tf_op jit(solution)/shard_map/ppermute | solution.py:98
  200.6 6.9 %collective-permute-start.18 = (bf16[528,128]{1,0:T(8,128)(2,1)S(1)}, bf16[528,128]{1,0:T(8,128)(2,1)S(1)}, u32[]{:S(2)}, u32[]{:S(2)}) collective-permute-start(bf16[528,128]{1,0:T(8,128)(2,1)S(1)} %get-tuple-element.46), channel_id=1, source_target_pairs={{0,8},{1,9},{2,10},{3,11},{4,12},{5,13},{6,14},{7,15},{8,0},{9,1},... | collective-permute-start | bytes 405512 | tf_op jit(solution)/shard_map/ppermute | solution.py:98
  202.3 6.1 %collective-permute-start.19 = (bf16[528,128]{1,0:T(8,128)(2,1)S(1)}, bf16[528,128]{1,0:T(8,128)(2,1)S(1)}, u32[]{:S(2)}, u32[]{:S(2)}) collective-permute-start(bf16[528,128]{1,0:T(8,128)(2,1)S(1)} %get-tuple-element.47), channel_id=1, source_target_pairs={{0,12},{1,13},{2,14},{3,15},{4,0},{5,1},{6,2},{7,3},{8,4},{9,5},{1... | collective-permute-start | bytes 405512 | tf_op jit(solution)/shard_map/ppermute | solution.py:98
Sparse Core Ops, SparseCore 0:
  9.7 52.1 all-gather.2

commit v3 on v2

--- a/solution.py
+++ b/solution.py
@@ -510,59 +510,110 @@
     return high, (value - high.astype(F32)).astype(BF16)
 
 
-def target_kernel(side, d, info_ref, p_ref, sums_ref, *refs):
-    data_refs, out_ref = refs[:-1], refs[-1]
+def row_sum_rows(sums):
+    high, low = split(sums)
+    return jnp.concatenate([high, low, high, low], axis=0)
+
+
+def target_kernel(side, ways, info_ref, p_ref, sums_ref, *refs):
+    chunks = 2 - side
+    data_refs, out_refs = refs[:chunks], refs[chunks:]
+    step = pl.program_id(0)
     if side == 0:
-        lanes = pl.ds(pl.multiple_of(lax.rem(info_ref[19] + d, 2) * 128, 128), 128)
+        way = ways[0] if len(ways) == 1 else jnp.where(step < 2, ways[0], ways[1])
+        lanes = pl.ds(pl.multiple_of(lax.rem(info_ref[19] + way, 2) * 128, 128), 128)
         data = jnp.concatenate([ref[0, :, lanes] for ref in data_refs], axis=1)
     else:
         data = data_refs[0][0]
     summed = jnp.dot(p_ref[...], data, preferred_element_type=F32).astype(BF16)
-    high, low = split(sums_ref[4 * side : 4 * side + 4, :])
-    tail = jnp.concatenate([high, low, high, low], axis=0)
-    for b in range(2):
-        out_ref[b, :HALF, :] = summed[:, 128 * b : 128 * (b + 1)]
-        out_ref[b, HALF:, :] = tail
-
-
-def message(side, d, info, p, sums, data):
+    tail = row_sum_rows(sums_ref[4 * side : 4 * side + 4, :])
+    if ways == (2,):
+        for half, out_ref in enumerate(out_refs):
+            for b in range(2):
+                out_ref[b, : HALF // 2, :] = summed[HALF // 2 * half : HALF // 2 * (half + 1), 128 * b : 128 * (b + 1)]
+                out_ref[b, HALF // 2 :, :] = tail
+    else:
+        for n, out_ref in enumerate(out_refs):
+
+            @pl.when(step // 2 == n)
+            def _(out_ref=out_ref):
+                for b in range(2):
+                    out_ref[b, :HALF, :] = summed[:, 128 * b : 128 * (b + 1)]
+                    out_ref[b, HALF:, :] = tail
+
+
+def messages(side, ways, info, p, sums, data):
+    def place(g, f):
+        way = ways[0] if len(ways) == 1 else jnp.where(g < 2, ways[0], ways[1])
+        return lax.rem(f[19 - side] + way, 4)
+
     if side == 0:
         chunks = [
-            vmem((1, COLS, 256), lambda g, f, b=b: (4 * g + 2 * b + lax.rem(f[19] + d, 4) // 2, 0, 0)) for b in (0, 1)
+            vmem((1, COLS, 256), lambda g, f, b=b: (4 * lax.rem(g, 2) + 2 * b + place(g, f) // 2, 0, 0)) for b in (0, 1)
         ]
     else:
-        chunks = [vmem((1, COLS, 256), lambda g, f: (2 * lax.rem(f[18] + d, 4) + g, 0, 0))]
+        chunks = [vmem((1, COLS, 256), lambda g, f: (2 * place(g, f) + lax.rem(g, 2), 0, 0))]
+    if ways == (2,):
+        outs = [vmem((2, HALF // 2 + EXTRA, 128), lambda g, f: (g, 0, 0))] * 2
+        shapes = [jax.ShapeDtypeStruct((4, HALF // 2 + EXTRA, 128), BF16)] * 2
+    else:
+        outs = [
+            vmem((2, HALF + EXTRA, 128), lambda g, f, n=n: (jnp.clip(g - 2 * n, 0, 1), 0, 0)) for n in range(len(ways))
+        ]
+        shapes = [jax.ShapeDtypeStruct((4, HALF + EXTRA, 128), BF16)] * len(ways)
     return pl.pallas_call(
-        functools.partial(target_kernel, side, d),
+        functools.partial(target_kernel, side, ways),
         grid_spec=pltpu.PrefetchScalarGridSpec(
             num_scalar_prefetch=1,
-            grid=(2,),
+            grid=(2 * len(ways),),
             in_specs=[vmem((HALF, COLS)), NOISE] + chunks,
-            out_specs=vmem((2, HALF + EXTRA, 128), lambda g, f: (g, 0, 0)),
+            out_specs=outs,
         ),
-        out_shape=jax.ShapeDtypeStruct((4, HALF + EXTRA, 128), BF16),
+        out_shape=shapes,
         compiler_params=params(24),
-        cost_estimate=pl.CostEstimate(flops=ROWS * COLS * WIDTH // 4, bytes_accessed=4 * MIB, transcendentals=0),
+        cost_estimate=pl.CostEstimate(
+            flops=ROWS * COLS * WIDTH // 4 * len(ways), bytes_accessed=4 * MIB, transcendentals=0
+        ),
         name="targets",
     )(info, p, sums, *[data] * len(chunks))
 
 
-def row_sums_of(ref, index=None):
-    high, low = (ref[HALF + 4 * i : HALF + 4 * i + 4, :] if index is None else ref[index, HALF + 4 * i : HALF + 4 * i + 4, :] for i in (0, 1))
+def forward_kernel(next_ref, last_ref, from_left, from_right, out_next, out_last):
+    half = HALF // 2
+    low, high, rest = slice(0, half), slice(half, HALF), slice(HALF, HALF + EXTRA)
+    for b in range(4):
+        out_next[b, low, :] = (next_ref[b, low, :].astype(F32) + from_left[b, low, :].astype(F32)).astype(BF16)
+        out_next[b, high, :] = next_ref[b, high, :]
+        out_last[b, low, :] = last_ref[b, low, :]
+        out_last[b, high, :] = (last_ref[b, high, :].astype(F32) + from_right[b, low, :].astype(F32)).astype(BF16)
+        out_next[b, rest, :] = row_sum_rows(row_sums_of(next_ref, 0, HALF) + row_sums_of(from_left, 0, half))
+        out_last[b, rest, :] = last_ref[b, rest, :]
+
+
+def forward(following, preceding, from_left, from_right):
+    return pl.pallas_call(
+        forward_kernel,
+        out_shape=[jax.ShapeDtypeStruct((4, HALF + EXTRA, 128), BF16)] * 2,
+        compiler_params=pltpu.CompilerParams(vmem_limit_bytes=16 * MIB),
+        cost_estimate=pl.CostEstimate(flops=1 << 20, bytes_accessed=3 * MIB, transcendentals=0),
+        name="forward",
+    )(following, preceding, from_left, from_right)
+
+
+def row_sums_of(ref, index=None, start=HALF):
+    at = [slice(start + 4 * i, start + 4 * i + 4) for i in (0, 1)]
+    high, low = (ref[i, :] if index is None else ref[index, i, :] for i in at)
     return high.astype(F32) + low.astype(F32)
 
 
-def combine_kernel(side, info_ref, own, r1, r2, r3, keep_ref, s1, s2, s3):
+def combine_kernel(side, info_ref, own, left, right, keep_ref, s1, s2, s3):
     place = info_ref[18 + side]
-    sums = (row_sums_of(own, 0) + row_sums_of(r1, 0)) + (row_sums_of(r2, 0) + row_sums_of(r3, 0))
-    high, low = split(sums)
-    tail = jnp.concatenate([high, low, high, low], axis=0)
+    sums = row_sums_of(own, 0) + (row_sums_of(left, 0) + row_sums_of(right, 0))
+    tail = row_sum_rows(sums)
 
     def summed(index):
         at = slice(0, HALF)
-        return (own[index, at, :].astype(F32) + r1[index, at, :].astype(F32)) + (
-            r2[index, at, :].astype(F32) + r3[index, at, :].astype(F32)
-        )
+        return own[index, at, :].astype(F32) + (left[index, at, :].astype(F32) + right[index, at, :].astype(F32))
 
     for d, out_ref in ((1, s1), (2, s2), (3, s3)):
         out_ref[:HALF, :] = summed(lax.rem(place + d, 4)).astype(BF16)
@@ -574,7 +625,7 @@
 def combine(side, info, parts):
     return pl.pallas_call(
         functools.partial(combine_kernel, side),
-        in_specs=[pl.BlockSpec(memory_space=pltpu.SMEM)] + [pl.BlockSpec(memory_space=pltpu.VMEM)] * 4,
+        in_specs=[pl.BlockSpec(memory_space=pltpu.SMEM)] + [pl.BlockSpec(memory_space=pltpu.VMEM)] * 3,
         out_shape=[jax.ShapeDtypeStruct((HALF + EXTRA, 128), F32)] + [jax.ShapeDtypeStruct((HALF + EXTRA, 128), BF16)] * 3,
         compiler_params=pltpu.CompilerParams(vmem_limit_bytes=16 * MIB),
         cost_estimate=pl.CostEstimate(flops=1 << 20, bytes_accessed=3 * MIB, transcendentals=0),
@@ -627,14 +678,25 @@
         swap(sums, "row"), noise_scale, noise_first, noise_sq, data_first, data_sq, k
     )
     way = (over_x, over_z)
-    parts = [[None] * 4, [None] * 4]
-    for d in (2, 1, 3, 0):
-        for side in (0, 1):
-            made = message(side, d, info, p[side], sums, data)
-            parts[side][d] = way[side](made, d) if d else made
+    moved = []
+    for side in (0, 1):
+        to_right, to_left = messages(side, (2,), info, p[side], sums, data)
+        moved.append((way[side](to_right, 1), way[side](to_left, 3)))
+        sums, _, _ = lax.optimization_barrier((sums, to_right, to_left))
+    made = []
+    for side in (0, 1):
+        made.append(messages(side, (1, 3), info, p[side], sums, data))
+        sums, _ = lax.optimization_barrier((sums, made[side]))
+    got = []
+    for side in (0, 1):
+        following, preceding = forward(*made[side], *moved[side])
+        got.append((way[side](following, 1), way[side](preceding, 3)))
+        sums, _ = lax.optimization_barrier((sums, following))
     ends = []
     for side in (0, 1):
-        keep, *others = combine(side, info, parts[side])
+        own = messages(side, (0,), info, p[side], sums, data)[0]
+        sums, _ = lax.optimization_barrier((sums, own))
+        keep, *others = combine(side, info, (own, *got[side]))
         ends += [keep] + [way[1 - side](v, d) for d, v in zip((1, 2, 3), others)]
     velocity = finish(noise_latents, ends)
     return velocity, noise_potential.reshape(ROWS), data_potential.reshape(COLS)

time: 217 us -> 208 us (0.959)
  waiting for transfers between devices: 42.8 us -> 31.6 us
  starting transfers between devices: 38.7 us -> 42.1 us
    ppermute x13 -> x14, waiting for transfers between devices: 16.4 us -> 4.68 us  [over_z(): lax.ppermute(v, 'col', [(4 * z + x, 4 * ((z + d) % 4) + x) for z in range...]
    ppermute x13 -> x14, starting transfers between devices: 18.1 us -> 21.5 us  [over_x(): lax.ppermute(v, 'col', [(4 * z + x, 4 * z + (x + d) % 4) for z in range(4...]
    ppermute x13 -> x14, waiting for transfers between devices: 21.4 us -> 21.9 us  [over_x(): lax.ppermute(v, 'col', [(4 * z + x, 4 * z + (x + d) % 4) for z in range(4...]
    ppermute x13 -> x14, starting transfers between devices: 20.5 us -> 20.5 us  [over_z(): lax.ppermute(v, 'col', [(4 * z + x, 4 * ((z + d) % 4) + x) for z in range...]
  transfers between devices with their start and end apart: 27 -> 29, of which waited for: 12 -> 12; matrix products, arithmetic and copies ran while one was open for 2% -> 2% of each run, Pallas kernels for 9% -> 9%
where the time goes in v3:
time: 208 us
  blocking collectives  60.9 us (29%)
  Pallas kernels  49.9 us (24%)
  starting transfers between devices  42.1 us (20%)
  waiting for transfers between devices  31.6 us (15%)
  between operations  14.3 us (7%)
  local copies, waits for them, and re-layouts  8.9 us (4%)
    all_to_all x6, blocking collectives, swap(): return lax.all_to_all(x, axis, 0, 0, tiled=True)  60.9 us
    ppermute x14, waiting for transfers between devices, over_x(): lax.ppermute(v, 'col', [(4 * z + x, 4 * z + (x + d) % 4) for z in range(4...  21.9 us
    ppermute x14, starting transfers between devices, over_x(): lax.ppermute(v, 'col', [(4 * z + x, 4 * z + (x + d) % 4) for z in range(4...  21.5 us
    ppermute x14, starting transfers between devices, over_z(): lax.ppermute(v, 'col', [(4 * z + x, 4 * ((z + d) % 4) + x) for z in range...  20.5 us
    pallas_call x1, Pallas kernels, scores(): pl.pallas_call(score_kernel, grid=(COLS // COL_BLOCK,), in_specs=[pl.Bloc...  15.6 us
    pallas_call x6, Pallas kernels, messages(): pl.pallas_call(functools.partial(target_kernel, side, ways), grid_spec=pl...  15.4 us
    pallas_call x6, Pallas kernels, pass_call(): pl.pallas_call(kernel, grid=(ROWS // ROW_BLOCK,), in_specs=in_specs, out_...  13 us
    ppermute x14, waiting for transfers between devices, over_z(): lax.ppermute(v, 'col', [(4 * z + x, 4 * ((z + d) % 4) + x) for z in range...  4.68 us
  transfers between devices with their start and end apart: 29, of which 12 were waited for; matrix products, arithmetic and copies ran while one was open for 2% of the time, Pallas kernels for 9%

profile of v3, /device:TPU:0, one launch (start us, length us, event | category | flops | bytes accessed | tf_op | source)
XLA Modules:
  0.0 207.8 jit_solution(13370820715852969807)
XLA Ops:
  7.9 1.0 slice_bitcast_fusion
  8.9 4.0 %collective-permute-start.8 = (bf16[512,128]{1,0:T(8,128)(2,1)S(1)}, bf16[512,128]{1,0:T(8,128)(2,1)S(1)}, u32[]{:S(2)}, u32[]{:S(2)}) collective-permute-start(bf16[512,128]{1,0:T(8,128)(2,1)S(1)} %get-tuple-element.96), channel_id=1, source_target_pairs={{0,8},{1,9},{2,10},{3,11},{4,12},{5,13},{6,14},{7,15},{8,0},{9,1},... | collective-permute-start | bytes 393224 | tf_op jit(solution)/shard_map/ppermute | solution.py:98
  14.0 2.2 %collective-permute-start.9 = (bf16[512,128]{1,0:T(8,128)(2,1)S(1)}, bf16[512,128]{1,0:T(8,128)(2,1)S(1)}, u32[]{:S(2)}, u32[]{:S(2)}) collective-permute-start(bf16[512,128]{1,0:T(8,128)(2,1)S(1)} %get-tuple-element.96), channel_id=1, source_target_pairs={{0,12},{1,13},{2,14},{3,15},{4,0},{5,1},{6,2},{7,3},{8,4},{9,5},{1... | collective-permute-start | bytes 393224 | tf_op jit(solution)/shard_map/ppermute | solution.py:98
  16.2 3.0 %collective-permute-start.1 = (bf16[512,128]{1,0:T(8,128)(2,1)S(1)}, bf16[512,128]{1,0:T(8,128)(2,1)S(1)}, u32[]{:S(2)}, u32[]{:S(2)}) collective-permute-start(bf16[512,128]{1,0:T(8,128)(2,1)S(1)} %get-tuple-element.95), channel_id=1, source_target_pairs={{0,2},{1,3},{2,0},{3,1},{4,6},{5,7},{6,4},{7,5},{8,10},{9,11},{10,... | collective-permute-start | bytes 393224 | tf_op jit(solution)/shard_map/ppermute | solution.py:94
  19.8 2.6 %collective-permute-start.2 = (bf16[512,128]{1,0:T(8,128)(2,1)S(1)}, bf16[512,128]{1,0:T(8,128)(2,1)S(1)}, u32[]{:S(2)}, u32[]{:S(2)}) collective-permute-start(bf16[512,128]{1,0:T(8,128)(2,1)S(1)} %get-tuple-element.95), channel_id=1, source_target_pairs={{0,3},{1,0},{2,1},{3,2},{4,7},{5,4},{6,5},{7,6},{8,11},{9,8},{10,9... | collective-permute-start | bytes 393224 | tf_op jit(solution)/shard_map/ppermute | solution.py:94
  22.9 1.7 collective-permute-start.10
  24.7 1.3 collective-permute-done
  27.5 1.4 collective-permute-start.3
  28.9 7.4 %collective-permute-done.11.refs_7_ = bf16[4,512,128]{2,1,0:T(8,128)(2,1)S(1)} collective-permute-done((bf16[4,512,128]{2,1,0:T(8,128)(2,1)S(1)}, bf16[4,512,128]{2,1,0:T(8,128)(2,1)S(1)}, u32[]{:S(2)}, u32[]{:S(2)}) %collective-permute-start.11) | collective-permute-done | bytes 524320 | tf_op jit(solution)/shard_map/ppermute | solution.py:94
  37.0 3.5 %collective-permute-start.13 = (bf16[2,512,128]{2,1,0:T(8,128)(2,1)}, bf16[2,512,128]{2,1,0:T(8,128)(2,1)S(1)}, u32[]{:S(2)}, u32[]{:S(2)}) collective-permute-start(bf16[2,512,128]{2,1,0:T(8,128)(2,1)} %slice.27), channel_id=1, source_target_pairs={{0,3},{1,0},{2,1},{3,2},{4,7},{5,4},{6,5},{7,6},{8,11},{9,8},{10,9... | collective-permute-start | bytes 786440 | tf_op jit(solution)/shard_map/ppermute | solution.py:94
  41.9 1.4 collective-permute-start.6
  45.4 3.9 %collective-permute-done.12.refs_8_ = bf16[2,512,128]{2,1,0:T(8,128)(2,1)} collective-permute-done((bf16[2,512,128]{2,1,0:T(8,128)(2,1)}, bf16[2,512,128]{2,1,0:T(8,128)(2,1)}, u32[]{:S(2)}, u32[]{:S(2)}) %collective-permute-start.12) | collective-permute-done | bytes 262176 | tf_op jit(solution)/shard_map/ppermute | solution.py:94
  49.3 3.0 %collective-permute-done.5.refs_3_ = bf16[2,512,128]{2,1,0:T(8,128)(2,1)} collective-permute-done((bf16[2,512,128]{2,1,0:T(8,128)(2,1)}, bf16[2,512,128]{2,1,0:T(8,128)(2,1)}, u32[]{:S(2)}, u32[]{:S(2)}) %collective-permute-start.5) | collective-permute-done | bytes 262176 | tf_op jit(solution)/shard_map/ppermute | solution.py:98
  52.4 3.1 %arrange.1 = (bf16[1024,2048]{1,0:T(8,128)(2,1)S(1)}, f32[8,128]{1,0:T(8,128)S(1)}) custom-call(s32[20]{0:T(128)S(1)} %concatenate.3.info_ref, bf16[4,512,128]{2,1,0:T(8,128)(2,1)S(1)} %pad_maximum_fusion.refs_0_, bf16[4,512,128]{2,1,0:T(8,128)(2,1)S(1)} %collective-permute-done.3.refs_1_, bf16[4,512,128]{2,1,0:T(8,128)(2,1)S(1)} %collective-permute-done.4.refs_2_, ...), custom_call_target="tpu_custom_call" | custom-call | flops 4194304 | bytes 8388608 | tf_op jit(solution)/shard_map/arrange/pallas_call | solution.py:83
  55.5 2.1 copy-done.1
  57.6 4.4 %all-gather.3.cloned.1.call-done = bf16[16384,256]{1,0:T(8,128)(2,1)} async-done(((bf16[2048,256]{1,0:T(8,128)(2,1)}), bf16[16384,256]{1,0:T(8,128)(2,1)}) %all-gather.3.cloned.1.call-update) | async-done | bytes 8388624 | tf_op jit(solution)/shard_map/all_gather | solution.py:669
  61.9 2.2 %copy-done.2 = bf16[1024,2048]{1,0:T(8,128)(2,1)S(1)} copy-done((bf16[1024,2048]{1,0:T(8,128)(2,1)S(1)}, bf16[1024,2048]{1,0:T(8,128)(2,1)}, u32[]{:S(2)}) %copy-start.2) | copy-done | bytes 4194328
  64.1 15.6 %scores.1 = (f32[1024,2048]{1,0:T(8,128)S(1)}, f32[16,8,128]{2,1,0:T(8,128)S(1)}, f32[8,2,128]{2,1,0:T(2,128)S(1)}) custom-call(s32[20]{0:T(128)S(1)} %concatenate.3.info_ref, bf16[1024,2048]{1,0:T(8,128)(2,1)S(1)} %copy-done.2, bf16[8,2048,256]{2,1,0:T(8,128)(2,1)} %bitcast.17), custom_call_target="tpu_custom_call" | custom-call | flops 8589934592 | bytes 20971520 | tf_op jit(solution)/shard_map/scores/pallas_call | solution.py:177
  79.8 14.4 %all_to_all.30.parts_ref = f32[16,8,128]{2,1,0:T(8,128)S(1)} all-to-all(f32[16,8,128]{2,1,0:T(8,128)S(1)} %get-tuple-element.49), channel_id=1, replica_groups=mesh['row'=8,'col'=16] {'col'}, dimensions={0} | all-to-all | bytes 131072 | tf_op jit(solution)/shard_map/all_to_all | solution.py:662
  94.2 3.3 %first_columns.1 = (f32[8,16,128]{2,1,0:T(8,128)S(1)}, f32[8,128]{1,0:T(8,128)S(1)}) custom-call(f32[16,8,128]{2,1,0:T(8,128)S(1)} %all_to_all.30.parts_ref, f32[1024,2048]{1,0:T(8,128)S(1)} %get-tuple-element.50.score_ref), custom_call_target="tpu_custom_call" | custom-call | flops 8388608 | bytes 8388608 | tf_op jit(solution)/shard_map/first_columns/pallas_call | solution.py:259
  97.5 8.6 %all_to_all.31.parts_ref = f32[8,16,128]{2,1,0:T(8,128)S(1)} all-to-all(f32[8,16,128]{2,1,0:T(8,128)S(1)} %get-tuple-element.51), channel_id=1, replica_groups=mesh['row'=8,'col'=16] {'row'}, dimensions={0} | all-to-all | bytes 131072 | tf_op jit(solution)/shard_map/all_to_all | solution.py:662
  106.1 3.0 %kernel_matrix.1 = (f32[1024,2048]{1,0:T(8,128)S(1)}, f32[16,8,128]{2,1,0:T(8,128)S(1)}, f32[16,128]{1,0:T(8,128)S(1)}) custom-call(f32[8,16,128]{2,1,0:T(8,128)S(1)} %all_to_all.31.parts_ref, f32[8,128]{1,0:T(8,128)S(1)} %get-tuple-element.52.noise_ref.noise_first, f32[1024,2048]{1,0:T(8,128)S(1)} %get-tuple-element.50.score_ref), custom_call_target="tpu_custom_call" | custom-call | flops 8388608 | bytes 8388608 | tf_op jit(solution)/shard_map/kernel_matrix/pallas_call | solution.py:259
  109.1 10.8 %all_to_all.32.parts_ref = f32[16,8,128]{2,1,0:T(8,128)S(1)} all-to-all(f32[16,8,128]{2,1,0:T(8,128)S(1)} %get-tuple-element.53), channel_id=1, replica_groups=mesh['row'=8,'col'=16] {'col'}, dimensions={0} | all-to-all | bytes 131072 | tf_op jit(solution)/shard_map/all_to_all | solution.py:662
  119.9 1.6 column_sums.2
  121.5 8.0 %all_to_all.33.parts_ref = f32[8,16,128]{2,1,0:T(8,128)S(1)} all-to-all(f32[8,16,128]{2,1,0:T(8,128)S(1)} %get-tuple-element.55), channel_id=1, replica_groups=mesh['row'=8,'col'=16] {'row'}, dimensions={0} | all-to-all | bytes 131072 | tf_op jit(solution)/shard_map/all_to_all | solution.py:662
  129.5 1.2 row_sums.1
  130.8 10.8 %all_to_all.34.parts_ref = f32[16,8,128]{2,1,0:T(8,128)S(1)} all-to-all(f32[16,8,128]{2,1,0:T(8,128)S(1)} %row_sums.1), channel_id=1, replica_groups=mesh['row'=8,'col'=16] {'col'}, dimensions={0} | all-to-all | bytes 131072 | tf_op jit(solution)/shard_map/all_to_all | solution.py:662
  141.6 1.0 column_sums.3
  142.6 8.3 %all_to_all.35.parts_ref = f32[8,16,128]{2,1,0:T(8,128)S(1)} all-to-all(f32[8,16,128]{2,1,0:T(8,128)S(1)} %get-tuple-element.56), channel_id=1, replica_groups=mesh['row'=8,'col'=16] {'row'}, dimensions={0} | all-to-all | bytes 131072 | tf_op jit(solution)/shard_map/all_to_all | solution.py:662
  150.9 2.8 %coupling.1 = (bf16[512,2048]{1,0:T(8,128)(2,1)S(1)}, bf16[512,2048]{1,0:T(8,128)(2,1)S(1)}, f32[8,128]{1,0:T(8,128)S(1)}, f32[8,128]{1,0:T(8,128)}, f32[16,128]{1,0:T(8,128)}) custom-call(f32[8,16,128]{2,1,0:T(8,128)S(1)} %all_to_all.35.parts_ref, f32[8,128]{1,0:T(8,128)S(1)} %get-tuple-element.57.scale_ref, ...), custom_call_target="tpu_custom_call" | custom-call | flops 8388608 | bytes 8388608 | tf_op jit(solution)/shard_map/coupling/pallas_call | solution.py:259
  153.7 2.0 targets.6
  156.4 2.7 %collective-permute-start.15 = (bf16[4,272,128]{2,1,0:T(8,128)(2,1)S(1)}, bf16[4,272,128]{2,1,0:T(8,128)(2,1)S(1)}, u32[]{:S(2)}, u32[]{:S(2)}) collective-permute-start(bf16[4,272,128]{2,1,0:T(8,128)(2,1)S(1)} %get-tuple-element.64), channel_id=1, source_target_pairs={{0,3},{1,0},{2,1},{3,2},{4,7},{5,4},{6,5},{7,6},{8,11},{9,8},{10,9... | collective-permute-start | bytes 835592 | tf_op jit(solution)/shard_map/ppermute | solution.py:94
  159.1 2.0 targets.7
  161.7 2.7 %collective-permute-start.17 = (bf16[4,272,128]{2,1,0:T(8,128)(2,1)S(1)}, bf16[4,272,128]{2,1,0:T(8,128)(2,1)S(1)}, u32[]{:S(2)}, u32[]{:S(2)}) collective-permute-start(bf16[4,272,128]{2,1,0:T(8,128)(2,1)S(1)} %get-tuple-element.68), channel_id=1, source_target_pairs={{0,12},{1,13},{2,14},{3,15},{4,0},{5,1},{6,2},{7,3},{8,4},{9,5},{1... | collective-permute-start | bytes 835592 | tf_op jit(solution)/shard_map/ppermute | solution.py:98
  164.4 3.6 %targets.8 = (bf16[4,528,128]{2,1,0:T(8,128)(2,1)S(1)}, bf16[4,528,128]{2,1,0:T(8,128)(2,1)S(1)}) custom-call(s32[20]{0:T(128)S(1)} %concatenate.3.info_ref, bf16[512,2048]{1,0:T(8,128)(2,1)S(1)} %get-tuple-element.61.p_ref, f32[8,128]{1,0:T(8,128)S(1)} %get-tuple-element.85.sums_ref, bf16[8,2048,256]{2,1,0:T(8,128)(2,1)S(1)} %bitcast.23, ...), custom_call_target="tpu_custom_call" | custom-call | flops 2147483648 | bytes 4194304 | tf_op jit(solution)/shard_map/targets/pallas_call | solution.py:564
  168.5 1.8 collective-permute-start.18
  170.3 3.6 %targets.9 = (bf16[4,528,128]{2,1,0:T(8,128)(2,1)S(1)}, bf16[4,528,128]{2,1,0:T(8,128)(2,1)S(1)}) custom-call(s32[20]{0:T(128)S(1)} %concatenate.3.info_ref, bf16[512,2048]{1,0:T(8,128)(2,1)S(1)} %get-tuple-element.66.p_ref, f32[8,128]{1,0:T(8,128)S(1)} %get-tuple-element.85.sums_ref, bf16[8,2048,256]{2,1,0:T(8,128)(2,1)S(1)} %bitcast.25), custom_call_target="tpu_custom_call" | custom-call | flops 2147483648 | bytes 4194304 | tf_op jit(solution)/shard_map/targets/pallas_call | solution.py:564
  174.1 2.0 collective-permute-start.23
  176.1 2.1 targets.10.own
  178.2 2.8 %collective-permute-done.19.right = bf16[4,528,128]{2,1,0:T(8,128)(2,1)S(1)} collective-permute-done((bf16[4,528,128]{2,1,0:T(8,128)(2,1)S(1)}, bf16[4,528,128]{2,1,0:T(8,128)(2,1)S(1)}, u32[]{:S(2)}, u32[]{:S(2)}) %collective-permute-start.19) | collective-permute-done | bytes 540704 | tf_op jit(solution)/shard_map/ppermute | solution.py:94
  181.0 1.3 collective-permute-done.18.left
  183.5 2.0 targets.11.own
  185.5 2.1 %collective-permute-start.21 = (bf16[528,128]{1,0:T(8,128)(2,1)S(1)}, bf16[528,128]{1,0:T(8,128)(2,1)S(1)}, u32[]{:S(2)}, u32[]{:S(2)}) collective-permute-start(bf16[528,128]{1,0:T(8,128)(2,1)S(1)} %get-tuple-element.83), channel_id=1, source_target_pairs={{0,8},{1,9},{2,10},{3,11},{4,12},{5,13},{6,14},{7,15},{8,0},{9,1},... | collective-permute-start | bytes 405512 | tf_op jit(solution)/shard_map/ppermute | solution.py:98
  187.7 1.2 collective-permute-start.22
  188.9 1.6 collective-permute-done.23.left
  191.6 3.3 %collective-permute-start.26 = (bf16[528,128]{1,0:T(8,128)(2,1)S(1)}, bf16[528,128]{1,0:T(8,128)(2,1)S(1)}, u32[]{:S(2)}, u32[]{:S(2)}) collective-permute-start(bf16[528,128]{1,0:T(8,128)(2,1)S(1)} %get-tuple-element.89), channel_id=1, source_target_pairs={{0,2},{1,3},{2,0},{3,1},{4,6},{5,7},{6,4},{7,5},{8,10},{9,11},{10,... | collective-permute-start | bytes 405512 | tf_op jit(solution)/shard_map/ppermute | solution.py:94
  195.5 2.0 collective-permute-done.25.refs_5_
  197.5 1.8 collective-permute-done.26.refs_6_
  (55 shorter events, 14.8 us)
Async XLA Ops:
  7.2 54.8 %all-gather.3.cloned.1.call-start = ((), (), s32[]{:S(2)}) async-start(), calls=%async_computation.6 | async-start | bytes 9437184 | tf_op jit(solution)/shard_map/all_gather | solution.py:669
  8.9 10.9 %collective-permute-start.8 = (bf16[512,128]{1,0:T(8,128)(2,1)S(1)}, bf16[512,128]{1,0:T(8,128)(2,1)S(1)}, u32[]{:S(2)}, u32[]{:S(2)}) collective-permute-start(bf16[512,128]{1,0:T(8,128)(2,1)S(1)} %get-tuple-element.96), channel_id=1, source_target_pairs={{0,8},{1,9},{2,10},{3,11},{4,12},{5,13},{6,14},{7,15},{8,0},{9,1},... | collective-permute-start | bytes 393224 | tf_op jit(solution)/shard_map/ppermute | solution.py:98
  13.0 9.5 %collective-permute-start.7 = (bf16[512,128]{1,0:T(8,128)(2,1)S(1)}, bf16[512,128]{1,0:T(8,128)(2,1)S(1)}, u32[]{:S(2)}, u32[]{:S(2)}) collective-permute-start(bf16[512,128]{1,0:T(8,128)(2,1)S(1)} %get-tuple-element.96), channel_id=1, source_target_pairs={{0,4},{1,5},{2,6},{3,7},{4,8},{5,9},{6,10},{7,11},{8,12},{9,13},{1... | collective-permute-start | bytes 393224 | tf_op jit(solution)/shard_map/ppermute | solution.py:98
  14.0 8.5 %collective-permute-start.9 = (bf16[512,128]{1,0:T(8,128)(2,1)S(1)}, bf16[512,128]{1,0:T(8,128)(2,1)S(1)}, u32[]{:S(2)}, u32[]{:S(2)}) collective-permute-start(bf16[512,128]{1,0:T(8,128)(2,1)S(1)} %get-tuple-element.96), channel_id=1, source_target_pairs={{0,12},{1,13},{2,14},{3,15},{4,0},{5,1},{6,2},{7,3},{8,4},{9,5},{1... | collective-permute-start | bytes 393224 | tf_op jit(solution)/shard_map/ppermute | solution.py:98
  16.2 8.4 %collective-permute-start.1 = (bf16[512,128]{1,0:T(8,128)(2,1)S(1)}, bf16[512,128]{1,0:T(8,128)(2,1)S(1)}, u32[]{:S(2)}, u32[]{:S(2)}) collective-permute-start(bf16[512,128]{1,0:T(8,128)(2,1)S(1)} %get-tuple-element.95), channel_id=1, source_target_pairs={{0,2},{1,3},{2,0},{3,1},{4,6},{5,7},{6,4},{7,5},{8,10},{9,11},{10,... | collective-permute-start | bytes 393224 | tf_op jit(solution)/shard_map/ppermute | solution.py:94
  19.2 6.8 %collective-permute-start = (bf16[512,128]{1,0:T(8,128)(2,1)S(1)}, bf16[512,128]{1,0:T(8,128)(2,1)S(1)}, u32[]{:S(2)}, u32[]{:S(2)}) collective-permute-start(bf16[512,128]{1,0:T(8,128)(2,1)S(1)} %get-tuple-element.95), channel_id=1, source_target_pairs={{0,1},{1,2},{2,3},{3,0},{4,5},{5,6},{6,7},{7,4},{8,9},{9,10},{10,1... | collective-permute-start | bytes 393224 | tf_op jit(solution)/shard_map/ppermute | solution.py:94
  19.8 6.9 %collective-permute-start.2 = (bf16[512,128]{1,0:T(8,128)(2,1)S(1)}, bf16[512,128]{1,0:T(8,128)(2,1)S(1)}, u32[]{:S(2)}, u32[]{:S(2)}) collective-permute-start(bf16[512,128]{1,0:T(8,128)(2,1)S(1)} %get-tuple-element.95), channel_id=1, source_target_pairs={{0,3},{1,0},{2,1},{3,2},{4,7},{5,4},{6,5},{7,6},{8,11},{9,8},{10,9... | collective-permute-start | bytes 393224 | tf_op jit(solution)/shard_map/ppermute | solution.py:94
  22.6 13.8 %collective-permute-start.11 = (bf16[4,512,128]{2,1,0:T(8,128)(2,1)S(1)}, bf16[4,512,128]{2,1,0:T(8,128)(2,1)S(1)}, u32[]{:S(2)}, u32[]{:S(2)}) collective-permute-start(bf16[4,512,128]{2,1,0:T(8,128)(2,1)S(1)} %pad_maximum_fusion.1.refs_5_), channel_id=1, source_target_pairs={{0,3},{1,0},{2,1},{3,2},{4,7},{5,4},{6,5},{7,6},{8,11},{9,8},{10,9... | collective-permute-start | bytes 1572872 | tf_op jit(solution)/shard_map/ppermute | solution.py:94
  22.9 17.6 %collective-permute-start.10 = (bf16[4,512,128]{2,1,0:T(8,128)(2,1)S(1)}, bf16[4,512,128]{2,1,0:T(8,128)(2,1)S(1)}, u32[]{:S(2)}, u32[]{:S(2)}) collective-permute-start(bf16[4,512,128]{2,1,0:T(8,128)(2,1)S(1)} %pad_maximum_fusion.1.refs_5_), channel_id=1, source_target_pairs={{0,1},{1,2},{2,3},{3,0},{4,5},{5,6},{6,7},{7,4},{8,9},{9,10},{10,1... | collective-permute-start | bytes 1572872 | tf_op jit(solution)/shard_map/ppermute | solution.py:94
  26.8 14.4 %collective-permute-start.4 = (bf16[4,512,128]{2,1,0:T(8,128)(2,1)S(1)}, bf16[4,512,128]{2,1,0:T(8,128)(2,1)S(1)}, u32[]{:S(2)}, u32[]{:S(2)}) collective-permute-start(bf16[4,512,128]{2,1,0:T(8,128)(2,1)S(1)} %pad_maximum_fusion.refs_0_), channel_id=1, source_target_pairs={{0,12},{1,13},{2,14},{3,15},{4,0},{5,1},{6,2},{7,3},{8,4},{9,5},{1... | collective-permute-start | bytes 1572872 | tf_op jit(solution)/shard_map/ppermute | solution.py:98
  27.5 15.8 %collective-permute-start.3 = (bf16[4,512,128]{2,1,0:T(8,128)(2,1)S(1)}, bf16[4,512,128]{2,1,0:T(8,128)(2,1)S(1)}, u32[]{:S(2)}, u32[]{:S(2)}) collective-permute-start(bf16[4,512,128]{2,1,0:T(8,128)(2,1)S(1)} %pad_maximum_fusion.refs_0_), channel_id=1, source_target_pairs={{0,4},{1,5},{2,6},{3,7},{4,8},{5,9},{6,10},{7,11},{8,12},{9,13},{1... | collective-permute-start | bytes 1572872 | tf_op jit(solution)/shard_map/ppermute | solution.py:98
  37.0 8.4 %collective-permute-start.13 = (bf16[2,512,128]{2,1,0:T(8,128)(2,1)}, bf16[2,512,128]{2,1,0:T(8,128)(2,1)S(1)}, u32[]{:S(2)}, u32[]{:S(2)}) collective-permute-start(bf16[2,512,128]{2,1,0:T(8,128)(2,1)} %slice.27), channel_id=1, source_target_pairs={{0,3},{1,0},{2,1},{3,2},{4,7},{5,4},{6,5},{7,6},{8,11},{9,8},{10,9... | collective-permute-start | bytes 786440 | tf_op jit(solution)/shard_map/ppermute | solution.py:94
  41.2 8.1 %collective-permute-start.12 = (bf16[2,512,128]{2,1,0:T(8,128)(2,1)}, bf16[2,512,128]{2,1,0:T(8,128)(2,1)}, u32[]{:S(2)}, u32[]{:S(2)}) collective-permute-start(bf16[2,512,128]{2,1,0:T(8,128)(2,1)} %slice.26), channel_id=1, source_target_pairs={{0,1},{1,2},{2,3},{3,0},{4,5},{5,6},{6,7},{7,4},{8,9},{9,10},{10,1... | collective-permute-start | bytes 786440 | tf_op jit(solution)/shard_map/ppermute | solution.py:94
  41.9 7.4 %collective-permute-start.6 = (bf16[2,512,128]{2,1,0:T(8,128)(2,1)}, bf16[2,512,128]{2,1,0:T(8,128)(2,1)}, u32[]{:S(2)}, u32[]{:S(2)}) collective-permute-start(bf16[2,512,128]{2,1,0:T(8,128)(2,1)} %slice.25), channel_id=1, source_target_pairs={{0,12},{1,13},{2,14},{3,15},{4,0},{5,1},{6,2},{7,3},{8,4},{9,5},{1... | collective-permute-start | bytes 786440 | tf_op jit(solution)/shard_map/ppermute | solution.py:98
  44.1 8.3 %collective-permute-start.5 = (bf16[2,512,128]{2,1,0:T(8,128)(2,1)}, bf16[2,512,128]{2,1,0:T(8,128)(2,1)}, u32[]{:S(2)}, u32[]{:S(2)}) collective-permute-start(bf16[2,512,128]{2,1,0:T(8,128)(2,1)} %slice.24), channel_id=1, source_target_pairs={{0,4},{1,5},{2,6},{3,7},{4,8},{5,9},{6,10},{7,11},{8,12},{9,13},{1... | collective-permute-start | bytes 786440 | tf_op jit(solution)/shard_map/ppermute | solution.py:98
  55.5 2.1 copy-start.1
  61.9 2.2 %copy-start.2 = (bf16[1024,2048]{1,0:T(8,128)(2,1)S(1)}, bf16[1024,2048]{1,0:T(8,128)(2,1)}, u32[]{:S(2)}) copy-start(bf16[1024,2048]{1,0:T(8,128)(2,1)} %copy-done.1) | copy-start | bytes 12582916
  141.6 12.1 %slice-start = ((s8[8388608]{0:T(1024)(128)(4,1)}), s8[4194304]{0:T(1024)(128)(4,1)S(1)}, s32[]{:S(2)}) async-start(s8[8388608]{0:T(1024)(128)(4,1)} %bitcast.18), calls=%async_computation.7 | async-start | bytes 8388608
  142.6 11.1 %slice-start.1 = ((s8[8388608]{0:T(1024)(128)(4,1)}), s8[4194304]{0:T(1024)(128)(4,1)S(1)}, s32[]{:S(2)}) async-start(s8[8388608]{0:T(1024)(128)(4,1)} %bitcast.18), calls=%async_computation.8 | async-start | bytes 8388608
  155.7 12.3 %collective-permute-start.14 = (bf16[4,272,128]{2,1,0:T(8,128)(2,1)S(1)}, bf16[4,272,128]{2,1,0:T(8,128)(2,1)S(1)}, u32[]{:S(2)}, u32[]{:S(2)}) collective-permute-start(bf16[4,272,128]{2,1,0:T(8,128)(2,1)S(1)} %get-tuple-element.63), channel_id=1, source_target_pairs={{0,1},{1,2},{2,3},{3,0},{4,5},{5,6},{6,7},{7,4},{8,9},{9,10},{10,1... | collective-permute-start | bytes 835592 | tf_op jit(solution)/shard_map/ppermute | solution.py:94
  156.4 11.7 %collective-permute-start.15 = (bf16[4,272,128]{2,1,0:T(8,128)(2,1)S(1)}, bf16[4,272,128]{2,1,0:T(8,128)(2,1)S(1)}, u32[]{:S(2)}, u32[]{:S(2)}) collective-permute-start(bf16[4,272,128]{2,1,0:T(8,128)(2,1)S(1)} %get-tuple-element.64), channel_id=1, source_target_pairs={{0,3},{1,0},{2,1},{3,2},{4,7},{5,4},{6,5},{7,6},{8,11},{9,8},{10,9... | collective-permute-start | bytes 835592 | tf_op jit(solution)/shard_map/ppermute | solution.py:94
  161.1 12.8 %collective-permute-start.16 = (bf16[4,272,128]{2,1,0:T(8,128)(2,1)S(1)}, bf16[4,272,128]{2,1,0:T(8,128)(2,1)S(1)}, u32[]{:S(2)}, u32[]{:S(2)}) collective-permute-start(bf16[4,272,128]{2,1,0:T(8,128)(2,1)S(1)} %get-tuple-element.67), channel_id=1, source_target_pairs={{0,4},{1,5},{2,6},{3,7},{4,8},{5,9},{6,10},{7,11},{8,12},{9,13},{1... | collective-permute-start | bytes 835592 | tf_op jit(solution)/shard_map/ppermute | solution.py:98
  161.7 12.2 %collective-permute-start.17 = (bf16[4,272,128]{2,1,0:T(8,128)(2,1)S(1)}, bf16[4,272,128]{2,1,0:T(8,128)(2,1)S(1)}, u32[]{:S(2)}, u32[]{:S(2)}) collective-permute-start(bf16[4,272,128]{2,1,0:T(8,128)(2,1)S(1)} %get-tuple-element.68), channel_id=1, source_target_pairs={{0,12},{1,13},{2,14},{3,15},{4,0},{5,1},{6,2},{7,3},{8,4},{9,5},{1... | collective-permute-start | bytes 835592 | tf_op jit(solution)/shard_map/ppermute | solution.py:98
  168.2 12.9 %collective-permute-start.19 = (bf16[4,528,128]{2,1,0:T(8,128)(2,1)S(1)}, bf16[4,528,128]{2,1,0:T(8,128)(2,1)S(1)}, u32[]{:S(2)}, u32[]{:S(2)}) collective-permute-start(bf16[4,528,128]{2,1,0:T(8,128)(2,1)S(1)} %get-tuple-element.80), channel_id=1, source_target_pairs={{0,3},{1,0},{2,1},{3,2},{4,7},{5,4},{6,5},{7,6},{8,11},{9,8},{10,9... | collective-permute-start | bytes 1622024 | tf_op jit(solution)/shard_map/ppermute | solution.py:94
  168.5 13.8 %collective-permute-start.18 = (bf16[4,528,128]{2,1,0:T(8,128)(2,1)S(1)}, bf16[4,528,128]{2,1,0:T(8,128)(2,1)S(1)}, u32[]{:S(2)}, u32[]{:S(2)}) collective-permute-start(bf16[4,528,128]{2,1,0:T(8,128)(2,1)S(1)} %get-tuple-element.76), channel_id=1, source_target_pairs={{0,1},{1,2},{2,3},{3,0},{4,5},{5,6},{6,7},{7,4},{8,9},{9,10},{10,1... | collective-permute-start | bytes 1622024 | tf_op jit(solution)/shard_map/ppermute | solution.py:94
  174.0 14.9 %collective-permute-start.24 = (bf16[4,528,128]{2,1,0:T(8,128)(2,1)S(1)}, bf16[4,528,128]{2,1,0:T(8,128)(2,1)S(1)}, u32[]{:S(2)}, u32[]{:S(2)}) collective-permute-start(bf16[4,528,128]{2,1,0:T(8,128)(2,1)S(1)} %get-tuple-element.86), channel_id=1, source_target_pairs={{0,12},{1,13},{2,14},{3,15},{4,0},{5,1},{6,2},{7,3},{8,4},{9,5},{1... | collective-permute-start | bytes 1622024 | tf_op jit(solution)/shard_map/ppermute | solution.py:98
  174.1 16.4 %collective-permute-start.23 = (bf16[4,528,128]{2,1,0:T(8,128)(2,1)S(1)}, bf16[4,528,128]{2,1,0:T(8,128)(2,1)S(1)}, u32[]{:S(2)}, u32[]{:S(2)}) collective-permute-start(bf16[4,528,128]{2,1,0:T(8,128)(2,1)S(1)} %get-tuple-element.78), channel_id=1, source_target_pairs={{0,4},{1,5},{2,6},{3,7},{4,8},{5,9},{6,10},{7,11},{8,12},{9,13},{1... | collective-permute-start | bytes 1622024 | tf_op jit(solution)/shard_map/ppermute | solution.py:98
  178.2 21.7 %copy-start = (bf16[1024,128]{1,0:T(8,128)(2,1)S(1)}, bf16[1024,128]{1,0:T(8,128)(2,1)}, u32[]{:S(2)}) copy-start(bf16[1024,128]{1,0:T(8,128)(2,1)} %noise_ref.1) | copy-start | bytes 786436
  183.1 11.8 %collective-permute-start.20 = (bf16[528,128]{1,0:T(8,128)(2,1)S(1)}, bf16[528,128]{1,0:T(8,128)(2,1)S(1)}, u32[]{:S(2)}, u32[]{:S(2)}) collective-permute-start(bf16[528,128]{1,0:T(8,128)(2,1)S(1)} %get-tuple-element.82), channel_id=1, source_target_pairs={{0,4},{1,5},{2,6},{3,7},{4,8},{5,9},{6,10},{7,11},{8,12},{9,13},{1... | collective-permute-start | bytes 405512 | tf_op jit(solution)/shard_map/ppermute | solution.py:98
  185.5 10.0 %collective-permute-start.21 = (bf16[528,128]{1,0:T(8,128)(2,1)S(1)}, bf16[528,128]{1,0:T(8,128)(2,1)S(1)}, u32[]{:S(2)}, u32[]{:S(2)}) collective-permute-start(bf16[528,128]{1,0:T(8,128)(2,1)S(1)} %get-tuple-element.83), channel_id=1, source_target_pairs={{0,8},{1,9},{2,10},{3,11},{4,12},{5,13},{6,14},{7,15},{8,0},{9,1},... | collective-permute-start | bytes 405512 | tf_op jit(solution)/shard_map/ppermute | solution.py:98
  187.7 7.9 %collective-permute-start.22 = (bf16[528,128]{1,0:T(8,128)(2,1)S(1)}, bf16[528,128]{1,0:T(8,128)(2,1)S(1)}, u32[]{:S(2)}, u32[]{:S(2)}) collective-permute-start(bf16[528,128]{1,0:T(8,128)(2,1)S(1)} %get-tuple-element.84), channel_id=1, source_target_pairs={{0,12},{1,13},{2,14},{3,15},{4,0},{5,1},{6,2},{7,3},{8,4},{9,5},{1... | collective-permute-start | bytes 405512 | tf_op jit(solution)/shard_map/ppermute | solution.py:98
  191.2 6.3 %collective-permute-start.25 = (bf16[528,128]{1,0:T(8,128)(2,1)S(1)}, bf16[528,128]{1,0:T(8,128)(2,1)S(1)}, u32[]{:S(2)}, u32[]{:S(2)}) collective-permute-start(bf16[528,128]{1,0:T(8,128)(2,1)S(1)} %get-tuple-element.88), channel_id=1, source_target_pairs={{0,1},{1,2},{2,3},{3,0},{4,5},{5,6},{6,7},{7,4},{8,9},{9,10},{10,1... | collective-permute-start | bytes 405512 | tf_op jit(solution)/shard_map/ppermute | solution.py:94
  191.6 7.7 %collective-permute-start.26 = (bf16[528,128]{1,0:T(8,128)(2,1)S(1)}, bf16[528,128]{1,0:T(8,128)(2,1)S(1)}, u32[]{:S(2)}, u32[]{:S(2)}) collective-permute-start(bf16[528,128]{1,0:T(8,128)(2,1)S(1)} %get-tuple-element.89), channel_id=1, source_target_pairs={{0,2},{1,3},{2,0},{3,1},{4,6},{5,7},{6,4},{7,5},{8,10},{9,11},{10,... | collective-permute-start | bytes 405512 | tf_op jit(solution)/shard_map/ppermute | solution.py:94
  194.9 5.0 %collective-permute-start.27 = (bf16[528,128]{1,0:T(8,128)(2,1)S(1)}, bf16[528,128]{1,0:T(8,128)(2,1)S(1)}, u32[]{:S(2)}, u32[]{:S(2)}) collective-permute-start(bf16[528,128]{1,0:T(8,128)(2,1)S(1)} %get-tuple-element.90), channel_id=1, source_target_pairs={{0,3},{1,0},{2,1},{3,2},{4,7},{5,4},{6,5},{7,6},{8,11},{9,8},{10,9... | collective-permute-start | bytes 405512 | tf_op jit(solution)/shard_map/ppermute | solution.py:94
Sparse Core Ops, SparseCore 0:
  9.7 52.1 all-gather.2

commit v4 on v3

--- a/solution.py
+++ b/solution.py
@@ -19,7 +19,8 @@
 ROWS = 1024
 COLS = 2048
 WIDTH = 2048
-COL_BLOCK = 256
+COL_BLOCK = 512
+SCORE_ROWS = 512
 ROW_BLOCK = 256
 HALF = 512
 N_ROW = 8
@@ -146,18 +147,19 @@
     low = low - info_ref[16]
     high = high - info_ref[16]
 
-    half = 256
+    half = SCORE_ROWS
     for r in range(ROWS // half):
         inner = lax.dot_general(noise_ref[half * r : half * (r + 1), :], data, (((1,), (1,)), ((), ())), preferred_element_type=F32)
         i = half * r + lax.broadcasted_iota(jnp.int32, (half, COL_BLOCK), 0)
         score = jnp.where((i >= low) & (i < high), inner * (2.0 * KAPPA), MASKED)
         score_ref[half * r : half * (r + 1), :] = score
-        lo = score[:, :128] - KAPPA * data_sq[0]
-        hi = score[:, 128:] - KAPPA * data_sq[1]
+        parts = [score[:, 128 * t : 128 * (t + 1)] - KAPPA * data_sq[t] for t in range(COL_BLOCK // 128)]
         at = slice(half * r, half * (r + 1))
         old = big[at, :]
-        new = jnp.maximum(old, jnp.maximum(lo, hi))
-        total[at, :] = total[at, :] * jnp.exp2(old - new) + (jnp.exp2(lo - new) + jnp.exp2(hi - new))
+        new = functools.reduce(jnp.maximum, parts, old)
+        total[at, :] = total[at, :] * jnp.exp2(old - new) + functools.reduce(
+            jnp.add, [jnp.exp2(part - new) for part in parts]
+        )
         big[at, :] = new
 
     @pl.when(step == pl.num_programs(0) - 1)
@@ -185,12 +187,12 @@
         out_specs=[
             vmem((ROWS, COL_BLOCK), lambda j: (0, j)),
             vmem((N_COL, 8, 128)),
-            vmem((1, 2, 128), lambda j: (j, 0, 0)),
+            vmem((1, COL_BLOCK // 128, 128), lambda j: (j, 0, 0)),
         ],
         out_shape=[
             jax.ShapeDtypeStruct((ROWS, COLS), F32),
             jax.ShapeDtypeStruct((N_COL, 8, 128), F32),
-            jax.ShapeDtypeStruct((COLS // COL_BLOCK, 2, 128), F32),
+            jax.ShapeDtypeStruct((COLS // COL_BLOCK, COL_BLOCK // 128, 128), F32),
         ],
         scratch_shapes=[pltpu.VMEM((ROWS, 128), F32), pltpu.VMEM((ROWS, 128), F32)],
         compiler_params=params(40),
@@ -444,8 +446,10 @@
             column[128 * a : 128 * (a + 1), :] = piece
         noise_ref[...] = (EPS * LN2) * (noise_first[...] + jnp.log2(scale_ref[...])) + noise_sq[...] * (1.0 / WIDTH)
         potential = (EPS * LN2) * (data_first[...] + jnp.log2(scale))
-        for k in range(8):
-            data_ref[2 * k : 2 * k + 2, :] = potential[2 * k : 2 * k + 2, :] + data_sq[k] * (1.0 / WIDTH)
+        per = COL_BLOCK // 128
+        for k in range(COLS // COL_BLOCK):
+            at = slice(per * k, per * (k + 1))
+            data_ref[at, :] = potential[at, :] + data_sq[k] * (1.0 / WIDTH)
 
     base = step * ROW_BLOCK
     tiles = COLS // 128
@@ -457,9 +461,9 @@
             summed = jnp.zeros((16, 128), F32)
             for t in range(tiles):
                 here = slice(128 * t, 128 * (t + 1))
-                value = k_ref[at, here] * (scale * lanes[:, here])
-                p_ref[at, here] = value.astype(BF16)
-                summed += value
+                value = (k_ref[at, here] * (scale * lanes[:, here])).astype(BF16)
+                p_ref[at, here] = value
+                summed += value.astype(F32)
             sums[at, :] = summed
             return 0
 
@@ -484,7 +488,7 @@
     return pass_call(
         coupling_kernel,
         (parts, noise_scale, noise_first, noise_sq, data_first, data_sq, k),
-        [FROM_ROW, NOISE, NOISE, NOISE, DATA, vmem((8, 2, 128)), BLOCK],
+        [FROM_ROW, NOISE, NOISE, NOISE, DATA, vmem((COLS // COL_BLOCK, COL_BLOCK // 128, 128)), BLOCK],
         [half, half, NOISE_SHAPE, NOISE_SHAPE, DATA_SHAPE],
         [
             vmem((ROW_BLOCK, COLS), lambda i: (jnp.minimum(i, 1), 0)),
@@ -515,67 +519,44 @@
     return jnp.concatenate([high, low, high, low], axis=0)
 
 
-def target_kernel(side, ways, info_ref, p_ref, sums_ref, *refs):
-    chunks = 2 - side
-    data_refs, out_refs = refs[:chunks], refs[chunks:]
-    step = pl.program_id(0)
-    if side == 0:
-        way = ways[0] if len(ways) == 1 else jnp.where(step < 2, ways[0], ways[1])
-        lanes = pl.ds(pl.multiple_of(lax.rem(info_ref[19] + way, 2) * 128, 128), 128)
-        data = jnp.concatenate([ref[0, :, lanes] for ref in data_refs], axis=1)
-    else:
-        data = data_refs[0][0]
-    summed = jnp.dot(p_ref[...], data, preferred_element_type=F32).astype(BF16)
-    tail = row_sum_rows(sums_ref[4 * side : 4 * side + 4, :])
-    if ways == (2,):
-        for half, out_ref in enumerate(out_refs):
-            for b in range(2):
-                out_ref[b, : HALF // 2, :] = summed[HALF // 2 * half : HALF // 2 * (half + 1), 128 * b : 128 * (b + 1)]
-                out_ref[b, HALF // 2 :, :] = tail
-    else:
-        for n, out_ref in enumerate(out_refs):
-
-            @pl.when(step // 2 == n)
-            def _(out_ref=out_ref):
-                for b in range(2):
-                    out_ref[b, :HALF, :] = summed[:, 128 * b : 128 * (b + 1)]
-                    out_ref[b, HALF:, :] = tail
-
-
-def messages(side, ways, info, p, sums, data):
-    def place(g, f):
-        way = ways[0] if len(ways) == 1 else jnp.where(g < 2, ways[0], ways[1])
-        return lax.rem(f[19 - side] + way, 4)
-
-    if side == 0:
-        chunks = [
-            vmem((1, COLS, 256), lambda g, f, b=b: (4 * lax.rem(g, 2) + 2 * b + place(g, f) // 2, 0, 0)) for b in (0, 1)
-        ]
-    else:
-        chunks = [vmem((1, COLS, 256), lambda g, f: (2 * place(g, f) + lax.rem(g, 2), 0, 0))]
-    if ways == (2,):
-        outs = [vmem((2, HALF // 2 + EXTRA, 128), lambda g, f: (g, 0, 0))] * 2
-        shapes = [jax.ShapeDtypeStruct((4, HALF // 2 + EXTRA, 128), BF16)] * 2
-    else:
-        outs = [
-            vmem((2, HALF + EXTRA, 128), lambda g, f, n=n: (jnp.clip(g - 2 * n, 0, 1), 0, 0)) for n in range(len(ways))
-        ]
-        shapes = [jax.ShapeDtypeStruct((4, HALF + EXTRA, 128), BF16)] * len(ways)
-    return pl.pallas_call(
-        functools.partial(target_kernel, side, ways),
-        grid_spec=pltpu.PrefetchScalarGridSpec(
-            num_scalar_prefetch=1,
-            grid=(2 * len(ways),),
-            in_specs=[vmem((HALF, COLS)), NOISE] + chunks,
-            out_specs=outs,
-        ),
-        out_shape=shapes,
-        compiler_params=params(24),
+def target_kernel(ways, info_ref, pa_ref, pb_ref, sums_ref, data_ref, *out_refs):
+    z, x = info_ref[18], info_ref[19]
+    out_refs = list(out_refs)
+    for side in (0, 1):
+        tail = row_sum_rows(sums_ref[4 * side : 4 * side + 4, :])
+        for way in ways:
+            if side == 0:
+                block = lax.rem(x + way, 4)
+                lanes = pl.ds(pl.multiple_of(lax.rem(block, 2) * 128, 128), 128)
+                data = [data_ref[2 * k + block // 2, :, lanes] for k in range(4)]
+                values = pa_ref[...]
+            else:
+                block = lax.rem(z + way, 4)
+                data = [data_ref[2 * block + k] for k in range(2)]
+                values = pb_ref[...]
+            summed = jnp.dot(values, jnp.concatenate(data, axis=1), preferred_element_type=F32).astype(BF16)
+            parts = 2 if way == 2 else 1
+            rows = HALF // parts
+            for part in range(parts):
+                out_ref = out_refs.pop(0)
+                for b in range(4):
+                    out_ref[b, :rows, :] = summed[rows * part : rows * (part + 1), 128 * b : 128 * (b + 1)]
+                    out_ref[b, rows:, :] = tail
+
+
+def messages(ways, info, p, sums, data):
+    rows = [HALF // 2] * 2 if ways == (2,) else [HALF] * len(ways)
+    made = pl.pallas_call(
+        functools.partial(target_kernel, ways),
+        in_specs=[pl.BlockSpec(memory_space=pltpu.SMEM)] + [pl.BlockSpec(memory_space=pltpu.VMEM)] * 4,
+        out_shape=[jax.ShapeDtypeStruct((4, n + EXTRA, 128), BF16) for n in rows * 2],
+        compiler_params=pltpu.CompilerParams(vmem_limit_bytes=28 * MIB),
         cost_estimate=pl.CostEstimate(
-            flops=ROWS * COLS * WIDTH // 4 * len(ways), bytes_accessed=4 * MIB, transcendentals=0
+            flops=ROWS * COLS * WIDTH // 2 * len(ways), bytes_accessed=8 * MIB, transcendentals=0
         ),
         name="targets",
-    )(info, p, sums, *[data] * len(chunks))
+    )(info, *p, sums, data)
+    return made[: len(rows)], made[len(rows) :]
 
 
 def forward_kernel(next_ref, last_ref, from_left, from_right, out_next, out_last):
@@ -678,25 +659,20 @@
         swap(sums, "row"), noise_scale, noise_first, noise_sq, data_first, data_sq, k
     )
     way = (over_x, over_z)
-    moved = []
-    for side in (0, 1):
-        to_right, to_left = messages(side, (2,), info, p[side], sums, data)
-        moved.append((way[side](to_right, 1), way[side](to_left, 3)))
-        sums, _, _ = lax.optimization_barrier((sums, to_right, to_left))
-    made = []
-    for side in (0, 1):
-        made.append(messages(side, (1, 3), info, p[side], sums, data))
-        sums, _ = lax.optimization_barrier((sums, made[side]))
+    made = messages((2,), info, p, sums, data)
+    moved = [(way[side](made[side][0], 1), way[side](made[side][1], 3)) for side in (0, 1)]
+    sums, _ = lax.optimization_barrier((sums, made))
+    made = messages((1, 3), info, p, sums, data)
+    sums, _ = lax.optimization_barrier((sums, made))
     got = []
     for side in (0, 1):
         following, preceding = forward(*made[side], *moved[side])
         got.append((way[side](following, 1), way[side](preceding, 3)))
         sums, _ = lax.optimization_barrier((sums, following))
+    own = messages((0,), info, p, sums, data)
     ends = []
     for side in (0, 1):
-        own = messages(side, (0,), info, p[side], sums, data)[0]
-        sums, _ = lax.optimization_barrier((sums, own))
-        keep, *others = combine(side, info, (own, *got[side]))
+        keep, *others = combine(side, info, (own[side][0], *got[side]))
         ends += [keep] + [way[1 - side](v, d) for d, v in zip((1, 2, 3), others)]
     velocity = finish(noise_latents, ends)
     return velocity, noise_potential.reshape(ROWS), data_potential.reshape(COLS)

time: 208 us -> 206 us (level)
  Pallas kernels: 49.9 us -> 44.6 us
  waiting for transfers between devices: 31.6 us -> 34.5 us
    ppermute x14, waiting for transfers between devices: 4.68 us -> 15.9 us  [over_z(): lax.ppermute(v, 'col', [(4 * z + x, 4 * ((z + d) % 4) + x) for z in range...]
    ppermute x14, waiting for transfers between devices: 21.9 us -> 13.5 us  [over_x(): lax.ppermute(v, 'col', [(4 * z + x, 4 * z + (x + d) % 4) for z in range(4...]
    pallas_call x6 -> x3, Pallas kernels: 15.4 us -> 10.8 us  [messages(): pl.pallas_call(functools.partial(target_kernel, ways), in_specs=[pl.Block...]
  transfers between devices with their start and end apart: 29 -> 29, of which waited for: 12 -> 13; matrix products, arithmetic and copies ran while one was open for 2% -> 2% of each run, Pallas kernels for 9% -> 6%
where the time goes in v4:
time: 206 us
  blocking collectives  61.1 us (30%)
  Pallas kernels  44.6 us (22%)
  starting transfers between devices  42.7 us (21%)
  waiting for transfers between devices  34.5 us (17%)
  between operations  14.2 us (7%)
  local copies, waits for them, and re-layouts  8.92 us (4%)
    all_to_all x6, blocking collectives, swap(): return lax.all_to_all(x, axis, 0, 0, tiled=True)  61.1 us
    ppermute x14, starting transfers between devices, over_z(): lax.ppermute(v, 'col', [(4 * z + x, 4 * ((z + d) % 4) + x) for z in range...  22.1 us
    ppermute x14, starting transfers between devices, over_x(): lax.ppermute(v, 'col', [(4 * z + x, 4 * z + (x + d) % 4) for z in range(4...  20.5 us
    ppermute x14, waiting for transfers between devices, over_z(): lax.ppermute(v, 'col', [(4 * z + x, 4 * ((z + d) % 4) + x) for z in range...  15.9 us
    pallas_call x1, Pallas kernels, scores(): pl.pallas_call(score_kernel, grid=(COLS // COL_BLOCK,), in_specs=[pl.Bloc...  14.5 us
    ppermute x14, waiting for transfers between devices, over_x(): lax.ppermute(v, 'col', [(4 * z + x, 4 * z + (x + d) % 4) for z in range(4...  13.5 us
    pallas_call x6, Pallas kernels, pass_call(): pl.pallas_call(kernel, grid=(ROWS // ROW_BLOCK,), in_specs=in_specs, out_...  13.3 us
    pallas_call x3, Pallas kernels, messages(): pl.pallas_call(functools.partial(target_kernel, ways), in_specs=[pl.Block...  10.8 us
  transfers between devices with their start and end apart: 29, of which 13 were waited for; matrix products, arithmetic and copies ran while one was open for 2% of the time, Pallas kernels for 6%

profile of v4, /device:TPU:0, one launch (start us, length us, event | category | flops | bytes accessed | tf_op | source)
XLA Modules:
  0.0 206.1 jit_solution(9142071873961683973)
XLA Ops:
  7.9 1.0 slice_bitcast_fusion
  8.9 4.0 %collective-permute-start.8 = (bf16[512,128]{1,0:T(8,128)(2,1)S(1)}, bf16[512,128]{1,0:T(8,128)(2,1)S(1)}, u32[]{:S(2)}, u32[]{:S(2)}) collective-permute-start(bf16[512,128]{1,0:T(8,128)(2,1)S(1)} %get-tuple-element.94), channel_id=1, source_target_pairs={{0,8},{1,9},{2,10},{3,11},{4,12},{5,13},{6,14},{7,15},{8,0},{9,1},... | collective-permute-start | bytes 393224 | tf_op jit(solution)/shard_map/ppermute | solution.py:99
  13.0 1.0 collective-permute-start.7
  14.0 2.2 %collective-permute-start.9 = (bf16[512,128]{1,0:T(8,128)(2,1)S(1)}, bf16[512,128]{1,0:T(8,128)(2,1)S(1)}, u32[]{:S(2)}, u32[]{:S(2)}) collective-permute-start(bf16[512,128]{1,0:T(8,128)(2,1)S(1)} %get-tuple-element.94), channel_id=1, source_target_pairs={{0,12},{1,13},{2,14},{3,15},{4,0},{5,1},{6,2},{7,3},{8,4},{9,5},{1... | collective-permute-start | bytes 393224 | tf_op jit(solution)/shard_map/ppermute | solution.py:99
  16.2 3.0 %collective-permute-start.1 = (bf16[512,128]{1,0:T(8,128)(2,1)S(1)}, bf16[512,128]{1,0:T(8,128)(2,1)S(1)}, u32[]{:S(2)}, u32[]{:S(2)}) collective-permute-start(bf16[512,128]{1,0:T(8,128)(2,1)S(1)} %get-tuple-element.93), channel_id=1, source_target_pairs={{0,2},{1,3},{2,0},{3,1},{4,6},{5,7},{6,4},{7,5},{8,10},{9,11},{10,... | collective-permute-start | bytes 393224 | tf_op jit(solution)/shard_map/ppermute | solution.py:95
  19.8 2.6 %collective-permute-start.2 = (bf16[512,128]{1,0:T(8,128)(2,1)S(1)}, bf16[512,128]{1,0:T(8,128)(2,1)S(1)}, u32[]{:S(2)}, u32[]{:S(2)}) collective-permute-start(bf16[512,128]{1,0:T(8,128)(2,1)S(1)} %get-tuple-element.93), channel_id=1, source_target_pairs={{0,3},{1,0},{2,1},{3,2},{4,7},{5,4},{6,5},{7,6},{8,11},{9,8},{10,9... | collective-permute-start | bytes 393224 | tf_op jit(solution)/shard_map/ppermute | solution.py:95
  22.9 1.7 collective-permute-start.10
  24.7 1.3 collective-permute-done
  27.5 1.4 collective-permute-start.3
  28.9 7.4 %collective-permute-done.11.refs_7_ = bf16[4,512,128]{2,1,0:T(8,128)(2,1)S(1)} collective-permute-done((bf16[4,512,128]{2,1,0:T(8,128)(2,1)S(1)}, bf16[4,512,128]{2,1,0:T(8,128)(2,1)S(1)}, u32[]{:S(2)}, u32[]{:S(2)}) %collective-permute-start.11) | collective-permute-done | bytes 524320 | tf_op jit(solution)/shard_map/ppermute | solution.py:95
  37.0 3.5 %collective-permute-start.13 = (bf16[2,512,128]{2,1,0:T(8,128)(2,1)}, bf16[2,512,128]{2,1,0:T(8,128)(2,1)S(1)}, u32[]{:S(2)}, u32[]{:S(2)}) collective-permute-start(bf16[2,512,128]{2,1,0:T(8,128)(2,1)} %slice.27), channel_id=1, source_target_pairs={{0,3},{1,0},{2,1},{3,2},{4,7},{5,4},{6,5},{7,6},{8,11},{9,8},{10,9... | collective-permute-start | bytes 786440 | tf_op jit(solution)/shard_map/ppermute | solution.py:95
  42.0 1.4 collective-permute-start.6
  44.7 0.7 concatenate.3.info_ref
  45.5 3.9 %collective-permute-done.12.refs_8_ = bf16[2,512,128]{2,1,0:T(8,128)(2,1)} collective-permute-done((bf16[2,512,128]{2,1,0:T(8,128)(2,1)}, bf16[2,512,128]{2,1,0:T(8,128)(2,1)}, u32[]{:S(2)}, u32[]{:S(2)}) %collective-permute-start.12) | collective-permute-done | bytes 262176 | tf_op jit(solution)/shard_map/ppermute | solution.py:95
  49.3 3.0 %collective-permute-done.5.refs_3_ = bf16[2,512,128]{2,1,0:T(8,128)(2,1)} collective-permute-done((bf16[2,512,128]{2,1,0:T(8,128)(2,1)}, bf16[2,512,128]{2,1,0:T(8,128)(2,1)}, u32[]{:S(2)}, u32[]{:S(2)}) %collective-permute-start.5) | collective-permute-done | bytes 262176 | tf_op jit(solution)/shard_map/ppermute | solution.py:99
  52.4 3.1 %arrange.1 = (bf16[1024,2048]{1,0:T(8,128)(2,1)S(1)}, f32[8,128]{1,0:T(8,128)S(1)}) custom-call(s32[20]{0:T(128)S(1)} %concatenate.3.info_ref, bf16[4,512,128]{2,1,0:T(8,128)(2,1)S(1)} %pad_maximum_fusion.refs_0_, bf16[4,512,128]{2,1,0:T(8,128)(2,1)S(1)} %collective-permute-done.3.refs_1_, bf16[4,512,128]{2,1,0:T(8,128)(2,1)S(1)} %collective-permute-done.4.refs_2_, ...), custom_call_target="tpu_custom_call" | custom-call | flops 4194304 | bytes 8388608 | tf_op jit(solution)/shard_map/arrange/pallas_call | solution.py:84
  55.5 2.0 copy-done.1
  57.6 4.4 %all-gather.3.cloned.1.call-done = bf16[16384,256]{1,0:T(8,128)(2,1)} async-done(((bf16[2048,256]{1,0:T(8,128)(2,1)}), bf16[16384,256]{1,0:T(8,128)(2,1)}) %all-gather.3.cloned.1.call-update) | async-done | bytes 8388624 | tf_op jit(solution)/shard_map/all_gather | solution.py:650
  61.9 2.2 %copy-done.2 = bf16[1024,2048]{1,0:T(8,128)(2,1)S(1)} copy-done((bf16[1024,2048]{1,0:T(8,128)(2,1)S(1)}, bf16[1024,2048]{1,0:T(8,128)(2,1)}, u32[]{:S(2)}) %copy-start.2) | copy-done | bytes 4194328
  64.1 14.5 %scores.1 = (f32[1024,2048]{1,0:T(8,128)S(1)}, f32[16,8,128]{2,1,0:T(8,128)S(1)}, f32[4,4,128]{2,1,0:T(4,128)S(1)}) custom-call(s32[20]{0:T(128)S(1)} %concatenate.3.info_ref, bf16[1024,2048]{1,0:T(8,128)(2,1)S(1)} %copy-done.2, bf16[8,2048,256]{2,1,0:T(8,128)(2,1)} %bitcast.17), custom_call_target="tpu_custom_call" | custom-call | flops 8589934592 | bytes 20971520 | tf_op jit(solution)/shard_map/scores/pallas_call | solution.py:179
  78.7 14.4 %all_to_all.30.parts_ref = f32[16,8,128]{2,1,0:T(8,128)S(1)} all-to-all(f32[16,8,128]{2,1,0:T(8,128)S(1)} %get-tuple-element.48), channel_id=1, replica_groups=mesh['row'=8,'col'=16] {'col'}, dimensions={0} | all-to-all | bytes 131072 | tf_op jit(solution)/shard_map/all_to_all | solution.py:643
  93.1 3.3 %first_columns.1 = (f32[8,16,128]{2,1,0:T(8,128)S(1)}, f32[8,128]{1,0:T(8,128)S(1)}) custom-call(f32[16,8,128]{2,1,0:T(8,128)S(1)} %all_to_all.30.parts_ref, f32[1024,2048]{1,0:T(8,128)S(1)} %get-tuple-element.49.score_ref), custom_call_target="tpu_custom_call" | custom-call | flops 8388608 | bytes 8388608 | tf_op jit(solution)/shard_map/first_columns/pallas_call | solution.py:261
  96.4 8.6 %all_to_all.31.parts_ref = f32[8,16,128]{2,1,0:T(8,128)S(1)} all-to-all(f32[8,16,128]{2,1,0:T(8,128)S(1)} %get-tuple-element.50), channel_id=1, replica_groups=mesh['row'=8,'col'=16] {'row'}, dimensions={0} | all-to-all | bytes 131072 | tf_op jit(solution)/shard_map/all_to_all | solution.py:643
  105.0 3.0 %kernel_matrix.1 = (f32[1024,2048]{1,0:T(8,128)S(1)}, f32[16,8,128]{2,1,0:T(8,128)S(1)}, f32[16,128]{1,0:T(8,128)S(1)}) custom-call(f32[8,16,128]{2,1,0:T(8,128)S(1)} %all_to_all.31.parts_ref, f32[8,128]{1,0:T(8,128)S(1)} %get-tuple-element.51.noise_ref.noise_first, f32[1024,2048]{1,0:T(8,128)S(1)} %get-tuple-element.49.score_ref), custom_call_target="tpu_custom_call" | custom-call | flops 8388608 | bytes 8388608 | tf_op jit(solution)/shard_map/kernel_matrix/pallas_call | solution.py:261
  108.0 10.8 %all_to_all.32.parts_ref = f32[16,8,128]{2,1,0:T(8,128)S(1)} all-to-all(f32[16,8,128]{2,1,0:T(8,128)S(1)} %get-tuple-element.52), channel_id=1, replica_groups=mesh['row'=8,'col'=16] {'col'}, dimensions={0} | all-to-all | bytes 131072 | tf_op jit(solution)/shard_map/all_to_all | solution.py:643
  118.8 1.6 column_sums.2
  120.4 8.0 %all_to_all.33.parts_ref = f32[8,16,128]{2,1,0:T(8,128)S(1)} all-to-all(f32[8,16,128]{2,1,0:T(8,128)S(1)} %get-tuple-element.54), channel_id=1, replica_groups=mesh['row'=8,'col'=16] {'row'}, dimensions={0} | all-to-all | bytes 131072 | tf_op jit(solution)/shard_map/all_to_all | solution.py:643
  128.4 1.2 row_sums.1
  129.7 10.8 %all_to_all.34.parts_ref = f32[16,8,128]{2,1,0:T(8,128)S(1)} all-to-all(f32[16,8,128]{2,1,0:T(8,128)S(1)} %row_sums.1), channel_id=1, replica_groups=mesh['row'=8,'col'=16] {'col'}, dimensions={0} | all-to-all | bytes 131072 | tf_op jit(solution)/shard_map/all_to_all | solution.py:643
  140.5 1.0 column_sums.3
  141.5 8.4 %all_to_all.35.parts_ref = f32[8,16,128]{2,1,0:T(8,128)S(1)} all-to-all(f32[8,16,128]{2,1,0:T(8,128)S(1)} %get-tuple-element.55), channel_id=1, replica_groups=mesh['row'=8,'col'=16] {'row'}, dimensions={0} | all-to-all | bytes 131072 | tf_op jit(solution)/shard_map/all_to_all | solution.py:643
  150.0 3.1 %coupling.1 = (bf16[512,2048]{1,0:T(8,128)(2,1)S(1)}, bf16[512,2048]{1,0:T(8,128)(2,1)S(1)}, f32[8,128]{1,0:T(8,128)S(1)}, f32[8,128]{1,0:T(8,128)}, f32[16,128]{1,0:T(8,128)}) custom-call(f32[8,16,128]{2,1,0:T(8,128)S(1)} %all_to_all.35.parts_ref, f32[8,128]{1,0:T(8,128)S(1)} %get-tuple-element.56.scale_ref, ...), custom_call_target="tpu_custom_call" | custom-call | flops 8388608 | bytes 8388608 | tf_op jit(solution)/shard_map/coupling/pallas_call | solution.py:261
  153.1 2.9 %targets.3 = (bf16[4,272,128]{2,1,0:T(8,128)(2,1)S(1)}, bf16[4,272,128]{2,1,0:T(8,128)(2,1)S(1)}, bf16[4,272,128]{2,1,0:T(8,128)(2,1)S(1)}, bf16[4,272,128]{2,1,0:T(8,128)(2,1)S(1)}) custom-call(s32[20]{0:T(128)S(1)} %concatenate.3.info_ref, bf16[512,2048]{1,0:T(8,128)(2,1)S(1)} %get-tuple-element.60.pa_ref, bf16[512,2048]{1,0:T(8,128)(2,1)S(1)} %get-tuple-element.61.pb_ref, ...), custom_call_target="tpu_custom_call" | custom-call | flops 2147483648 | bytes 8388608 | tf_op jit(solution)/shard_map/targets/pallas_call | solution.py:549
  156.6 2.7 %collective-permute-start.15 = (bf16[4,272,128]{2,1,0:T(8,128)(2,1)S(1)}, bf16[4,272,128]{2,1,0:T(8,128)(2,1)S(1)}, u32[]{:S(2)}, u32[]{:S(2)}) collective-permute-start(bf16[4,272,128]{2,1,0:T(8,128)(2,1)S(1)} %get-tuple-element.64), channel_id=1, source_target_pairs={{0,3},{1,0},{2,1},{3,2},{4,7},{5,4},{6,5},{7,6},{8,11},{9,8},{10,9... | collective-permute-start | bytes 835592 | tf_op jit(solution)/shard_map/ppermute | solution.py:95
  159.8 2.7 %collective-permute-start.17 = (bf16[4,272,128]{2,1,0:T(8,128)(2,1)S(1)}, bf16[4,272,128]{2,1,0:T(8,128)(2,1)S(1)}, u32[]{:S(2)}, u32[]{:S(2)}) collective-permute-start(bf16[4,272,128]{2,1,0:T(8,128)(2,1)S(1)} %get-tuple-element.66), channel_id=1, source_target_pairs={{0,12},{1,13},{2,14},{3,15},{4,0},{5,1},{6,2},{7,3},{8,4},{9,5},{1... | collective-permute-start | bytes 835592 | tf_op jit(solution)/shard_map/ppermute | solution.py:99
  162.6 5.0 %targets.4 = (bf16[4,528,128]{2,1,0:T(8,128)(2,1)S(1)}, bf16[4,528,128]{2,1,0:T(8,128)(2,1)S(1)}, bf16[4,528,128]{2,1,0:T(8,128)(2,1)S(1)}, bf16[4,528,128]{2,1,0:T(8,128)(2,1)S(1)}) custom-call(s32[20]{0:T(128)S(1)} %concatenate.3.info_ref, bf16[512,2048]{1,0:T(8,128)(2,1)S(1)} %get-tuple-element.60.pa_ref, bf16[512,2048]{1,0:T(8,128)(2,1)S(1)} %get-tuple-element.61.pb_ref, ...), custom_call_target="tpu_custom_call" | custom-call | flops 4294967296 | bytes 8388608 | tf_op jit(solution)/shard_map/targets/pallas_call | solution.py:549
  168.4 3.0 %collective-permute-start.24 = (bf16[4,528,128]{2,1,0:T(8,128)(2,1)S(1)}, bf16[4,528,128]{2,1,0:T(8,128)(2,1)S(1)}, u32[]{:S(2)}, u32[]{:S(2)}) collective-permute-start(bf16[4,528,128]{2,1,0:T(8,128)(2,1)S(1)} %get-tuple-element.84), channel_id=1, source_target_pairs={{0,12},{1,13},{2,14},{3,15},{4,0},{5,1},{6,2},{7,3},{8,4},{9,5},{1... | collective-permute-start | bytes 1622024 | tf_op jit(solution)/shard_map/ppermute | solution.py:99
  172.0 1.7 collective-permute-start.18
  173.7 2.9 %targets.5 = (bf16[4,528,128]{2,1,0:T(8,128)(2,1)S(1)}, bf16[4,528,128]{2,1,0:T(8,128)(2,1)S(1)}) custom-call(s32[20]{0:T(128)S(1)} %concatenate.3.info_ref, bf16[512,2048]{1,0:T(8,128)(2,1)S(1)} %get-tuple-element.60.pa_ref, bf16[512,2048]{1,0:T(8,128)(2,1)S(1)} %get-tuple-element.61.pb_ref, f32[8,128]{1,0:T(8,128)S(1)} %get-tuple-element.76.sums_ref, ...), custom_call_target="tpu_custom_call" | custom-call | flops 2147483648 | bytes 8388608 | tf_op jit(solution)/shard_map/targets/pallas_call | solution.py:549
  176.6 4.5 %collective-permute-done.24.right = bf16[4,528,128]{2,1,0:T(8,128)(2,1)S(1)} collective-permute-done((bf16[4,528,128]{2,1,0:T(8,128)(2,1)S(1)}, bf16[4,528,128]{2,1,0:T(8,128)(2,1)S(1)}, u32[]{:S(2)}, u32[]{:S(2)}) %collective-permute-start.24) | collective-permute-done | bytes 540704 | tf_op jit(solution)/shard_map/ppermute | solution.py:99
  181.1 3.4 %collective-permute-done.23.left = bf16[4,528,128]{2,1,0:T(8,128)(2,1)S(1)} collective-permute-done((bf16[4,528,128]{2,1,0:T(8,128)(2,1)S(1)}, bf16[4,528,128]{2,1,0:T(8,128)(2,1)S(1)}, u32[]{:S(2)}, u32[]{:S(2)}) %collective-permute-start.23) | collective-permute-done | bytes 540704 | tf_op jit(solution)/shard_map/ppermute | solution.py:99
  185.3 2.0 collective-permute-start.26
  187.4 1.2 collective-permute-start.27
  188.6 0.8 combine.2
  189.4 3.8 %collective-permute-start.21 = (bf16[528,128]{1,0:T(8,128)(2,1)S(1)}, bf16[528,128]{1,0:T(8,128)(2,1)S(1)}, u32[]{:S(2)}, u32[]{:S(2)}) collective-permute-start(bf16[528,128]{1,0:T(8,128)(2,1)S(1)} %get-tuple-element.81), channel_id=1, source_target_pairs={{0,8},{1,9},{2,10},{3,11},{4,12},{5,13},{6,14},{7,15},{8,0},{9,1},... | collective-permute-start | bytes 405512 | tf_op jit(solution)/shard_map/ppermute | solution.py:99
  193.9 1.7 collective-permute-done.20.refs_1_
  195.6 2.0 collective-permute-done.21.refs_2_
  198.2 1.0 finish.1
  (52 shorter events, 11.4 us)
Async XLA Ops:
  7.2 54.8 %all-gather.3.cloned.1.call-start = ((), (), s32[]{:S(2)}) async-start(), calls=%async_computation.6 | async-start | bytes 9437184 | tf_op jit(solution)/shard_map/all_gather | solution.py:650
  8.9 10.9 %collective-permute-start.8 = (bf16[512,128]{1,0:T(8,128)(2,1)S(1)}, bf16[512,128]{1,0:T(8,128)(2,1)S(1)}, u32[]{:S(2)}, u32[]{:S(2)}) collective-permute-start(bf16[512,128]{1,0:T(8,128)(2,1)S(1)} %get-tuple-element.94), channel_id=1, source_target_pairs={{0,8},{1,9},{2,10},{3,11},{4,12},{5,13},{6,14},{7,15},{8,0},{9,1},... | collective-permute-start | bytes 393224 | tf_op jit(solution)/shard_map/ppermute | solution.py:99
  13.0 9.5 %collective-permute-start.7 = (bf16[512,128]{1,0:T(8,128)(2,1)S(1)}, bf16[512,128]{1,0:T(8,128)(2,1)S(1)}, u32[]{:S(2)}, u32[]{:S(2)}) collective-permute-start(bf16[512,128]{1,0:T(8,128)(2,1)S(1)} %get-tuple-element.94), channel_id=1, source_target_pairs={{0,4},{1,5},{2,6},{3,7},{4,8},{5,9},{6,10},{7,11},{8,12},{9,13},{1... | collective-permute-start | bytes 393224 | tf_op jit(solution)/shard_map/ppermute | solution.py:99
  14.0 8.5 %collective-permute-start.9 = (bf16[512,128]{1,0:T(8,128)(2,1)S(1)}, bf16[512,128]{1,0:T(8,128)(2,1)S(1)}, u32[]{:S(2)}, u32[]{:S(2)}) collective-permute-start(bf16[512,128]{1,0:T(8,128)(2,1)S(1)} %get-tuple-element.94), channel_id=1, source_target_pairs={{0,12},{1,13},{2,14},{3,15},{4,0},{5,1},{6,2},{7,3},{8,4},{9,5},{1... | collective-permute-start | bytes 393224 | tf_op jit(solution)/shard_map/ppermute | solution.py:99
  16.2 8.4 %collective-permute-start.1 = (bf16[512,128]{1,0:T(8,128)(2,1)S(1)}, bf16[512,128]{1,0:T(8,128)(2,1)S(1)}, u32[]{:S(2)}, u32[]{:S(2)}) collective-permute-start(bf16[512,128]{1,0:T(8,128)(2,1)S(1)} %get-tuple-element.93), channel_id=1, source_target_pairs={{0,2},{1,3},{2,0},{3,1},{4,6},{5,7},{6,4},{7,5},{8,10},{9,11},{10,... | collective-permute-start | bytes 393224 | tf_op jit(solution)/shard_map/ppermute | solution.py:95
  19.2 6.8 %collective-permute-start = (bf16[512,128]{1,0:T(8,128)(2,1)S(1)}, bf16[512,128]{1,0:T(8,128)(2,1)S(1)}, u32[]{:S(2)}, u32[]{:S(2)}) collective-permute-start(bf16[512,128]{1,0:T(8,128)(2,1)S(1)} %get-tuple-element.93), channel_id=1, source_target_pairs={{0,1},{1,2},{2,3},{3,0},{4,5},{5,6},{6,7},{7,4},{8,9},{9,10},{10,1... | collective-permute-start | bytes 393224 | tf_op jit(solution)/shard_map/ppermute | solution.py:95
  19.8 6.9 %collective-permute-start.2 = (bf16[512,128]{1,0:T(8,128)(2,1)S(1)}, bf16[512,128]{1,0:T(8,128)(2,1)S(1)}, u32[]{:S(2)}, u32[]{:S(2)}) collective-permute-start(bf16[512,128]{1,0:T(8,128)(2,1)S(1)} %get-tuple-element.93), channel_id=1, source_target_pairs={{0,3},{1,0},{2,1},{3,2},{4,7},{5,4},{6,5},{7,6},{8,11},{9,8},{10,9... | collective-permute-start | bytes 393224 | tf_op jit(solution)/shard_map/ppermute | solution.py:95
  22.6 13.8 %collective-permute-start.11 = (bf16[4,512,128]{2,1,0:T(8,128)(2,1)S(1)}, bf16[4,512,128]{2,1,0:T(8,128)(2,1)S(1)}, u32[]{:S(2)}, u32[]{:S(2)}) collective-permute-start(bf16[4,512,128]{2,1,0:T(8,128)(2,1)S(1)} %pad_maximum_fusion.1.refs_5_), channel_id=1, source_target_pairs={{0,3},{1,0},{2,1},{3,2},{4,7},{5,4},{6,5},{7,6},{8,11},{9,8},{10,9... | collective-permute-start | bytes 1572872 | tf_op jit(solution)/shard_map/ppermute | solution.py:95
  22.9 17.6 %collective-permute-start.10 = (bf16[4,512,128]{2,1,0:T(8,128)(2,1)S(1)}, bf16[4,512,128]{2,1,0:T(8,128)(2,1)S(1)}, u32[]{:S(2)}, u32[]{:S(2)}) collective-permute-start(bf16[4,512,128]{2,1,0:T(8,128)(2,1)S(1)} %pad_maximum_fusion.1.refs_5_), channel_id=1, source_target_pairs={{0,1},{1,2},{2,3},{3,0},{4,5},{5,6},{6,7},{7,4},{8,9},{9,10},{10,1... | collective-permute-start | bytes 1572872 | tf_op jit(solution)/shard_map/ppermute | solution.py:95
  26.8 14.5 %collective-permute-start.4 = (bf16[4,512,128]{2,1,0:T(8,128)(2,1)S(1)}, bf16[4,512,128]{2,1,0:T(8,128)(2,1)S(1)}, u32[]{:S(2)}, u32[]{:S(2)}) collective-permute-start(bf16[4,512,128]{2,1,0:T(8,128)(2,1)S(1)} %pad_maximum_fusion.refs_0_), channel_id=1, source_target_pairs={{0,12},{1,13},{2,14},{3,15},{4,0},{5,1},{6,2},{7,3},{8,4},{9,5},{1... | collective-permute-start | bytes 1572872 | tf_op jit(solution)/shard_map/ppermute | solution.py:99
  27.5 15.9 %collective-permute-start.3 = (bf16[4,512,128]{2,1,0:T(8,128)(2,1)S(1)}, bf16[4,512,128]{2,1,0:T(8,128)(2,1)S(1)}, u32[]{:S(2)}, u32[]{:S(2)}) collective-permute-start(bf16[4,512,128]{2,1,0:T(8,128)(2,1)S(1)} %pad_maximum_fusion.refs_0_), channel_id=1, source_target_pairs={{0,4},{1,5},{2,6},{3,7},{4,8},{5,9},{6,10},{7,11},{8,12},{9,13},{1... | collective-permute-start | bytes 1572872 | tf_op jit(solution)/shard_map/ppermute | solution.py:99
  37.0 8.4 %collective-permute-start.13 = (bf16[2,512,128]{2,1,0:T(8,128)(2,1)}, bf16[2,512,128]{2,1,0:T(8,128)(2,1)S(1)}, u32[]{:S(2)}, u32[]{:S(2)}) collective-permute-start(bf16[2,512,128]{2,1,0:T(8,128)(2,1)} %slice.27), channel_id=1, source_target_pairs={{0,3},{1,0},{2,1},{3,2},{4,7},{5,4},{6,5},{7,6},{8,11},{9,8},{10,9... | collective-permute-start | bytes 786440 | tf_op jit(solution)/shard_map/ppermute | solution.py:95
  41.2 8.1 %collective-permute-start.12 = (bf16[2,512,128]{2,1,0:T(8,128)(2,1)}, bf16[2,512,128]{2,1,0:T(8,128)(2,1)}, u32[]{:S(2)}, u32[]{:S(2)}) collective-permute-start(bf16[2,512,128]{2,1,0:T(8,128)(2,1)} %slice.26), channel_id=1, source_target_pairs={{0,1},{1,2},{2,3},{3,0},{4,5},{5,6},{6,7},{7,4},{8,9},{9,10},{10,1... | collective-permute-start | bytes 786440 | tf_op jit(solution)/shard_map/ppermute | solution.py:95
  42.0 7.4 %collective-permute-start.6 = (bf16[2,512,128]{2,1,0:T(8,128)(2,1)}, bf16[2,512,128]{2,1,0:T(8,128)(2,1)}, u32[]{:S(2)}, u32[]{:S(2)}) collective-permute-start(bf16[2,512,128]{2,1,0:T(8,128)(2,1)} %slice.25), channel_id=1, source_target_pairs={{0,12},{1,13},{2,14},{3,15},{4,0},{5,1},{6,2},{7,3},{8,4},{9,5},{1... | collective-permute-start | bytes 786440 | tf_op jit(solution)/shard_map/ppermute | solution.py:99
  44.1 8.3 %collective-permute-start.5 = (bf16[2,512,128]{2,1,0:T(8,128)(2,1)}, bf16[2,512,128]{2,1,0:T(8,128)(2,1)}, u32[]{:S(2)}, u32[]{:S(2)}) collective-permute-start(bf16[2,512,128]{2,1,0:T(8,128)(2,1)} %slice.24), channel_id=1, source_target_pairs={{0,4},{1,5},{2,6},{3,7},{4,8},{5,9},{6,10},{7,11},{8,12},{9,13},{1... | collective-permute-start | bytes 786440 | tf_op jit(solution)/shard_map/ppermute | solution.py:99
  55.5 2.1 copy-start.1
  61.9 2.2 %copy-start.2 = (bf16[1024,2048]{1,0:T(8,128)(2,1)S(1)}, bf16[1024,2048]{1,0:T(8,128)(2,1)}, u32[]{:S(2)}) copy-start(bf16[1024,2048]{1,0:T(8,128)(2,1)} %copy-done.1) | copy-start | bytes 12582916
  140.5 12.7 %slice-start = ((s8[8388608]{0:T(1024)(128)(4,1)}), s8[4194304]{0:T(1024)(128)(4,1)S(1)}, s32[]{:S(2)}) async-start(s8[8388608]{0:T(1024)(128)(4,1)} %bitcast.18), calls=%async_computation.7 | async-start | bytes 8388608
  141.5 11.6 %slice-start.1 = ((s8[8388608]{0:T(1024)(128)(4,1)}), s8[4194304]{0:T(1024)(128)(4,1)S(1)}, s32[]{:S(2)}) async-start(s8[8388608]{0:T(1024)(128)(4,1)} %bitcast.18), calls=%async_computation.8 | async-start | bytes 8388608
  156.0 15.4 %collective-permute-start.14 = (bf16[4,272,128]{2,1,0:T(8,128)(2,1)S(1)}, bf16[4,272,128]{2,1,0:T(8,128)(2,1)S(1)}, u32[]{:S(2)}, u32[]{:S(2)}) collective-permute-start(bf16[4,272,128]{2,1,0:T(8,128)(2,1)S(1)} %get-tuple-element.63), channel_id=1, source_target_pairs={{0,1},{1,2},{2,3},{3,0},{4,5},{5,6},{6,7},{7,4},{8,9},{9,10},{10,1... | collective-permute-start | bytes 835592 | tf_op jit(solution)/shard_map/ppermute | solution.py:95
  156.6 14.8 %collective-permute-start.15 = (bf16[4,272,128]{2,1,0:T(8,128)(2,1)S(1)}, bf16[4,272,128]{2,1,0:T(8,128)(2,1)S(1)}, u32[]{:S(2)}, u32[]{:S(2)}) collective-permute-start(bf16[4,272,128]{2,1,0:T(8,128)(2,1)S(1)} %get-tuple-element.64), channel_id=1, source_target_pairs={{0,3},{1,0},{2,1},{3,2},{4,7},{5,4},{6,5},{7,6},{8,11},{9,8},{10,9... | collective-permute-start | bytes 835592 | tf_op jit(solution)/shard_map/ppermute | solution.py:95
  159.3 8.9 %collective-permute-start.16 = (bf16[4,272,128]{2,1,0:T(8,128)(2,1)S(1)}, bf16[4,272,128]{2,1,0:T(8,128)(2,1)S(1)}, u32[]{:S(2)}, u32[]{:S(2)}) collective-permute-start(bf16[4,272,128]{2,1,0:T(8,128)(2,1)S(1)} %get-tuple-element.65), channel_id=1, source_target_pairs={{0,4},{1,5},{2,6},{3,7},{4,8},{5,9},{6,10},{7,11},{8,12},{9,13},{1... | collective-permute-start | bytes 835592 | tf_op jit(solution)/shard_map/ppermute | solution.py:99
  159.8 8.4 %collective-permute-start.17 = (bf16[4,272,128]{2,1,0:T(8,128)(2,1)S(1)}, bf16[4,272,128]{2,1,0:T(8,128)(2,1)S(1)}, u32[]{:S(2)}, u32[]{:S(2)}) collective-permute-start(bf16[4,272,128]{2,1,0:T(8,128)(2,1)S(1)} %get-tuple-element.66), channel_id=1, source_target_pairs={{0,12},{1,13},{2,14},{3,15},{4,0},{5,1},{6,2},{7,3},{8,4},{9,5},{1... | collective-permute-start | bytes 835592 | tf_op jit(solution)/shard_map/ppermute | solution.py:99
  168.4 12.7 %collective-permute-start.24 = (bf16[4,528,128]{2,1,0:T(8,128)(2,1)S(1)}, bf16[4,528,128]{2,1,0:T(8,128)(2,1)S(1)}, u32[]{:S(2)}, u32[]{:S(2)}) collective-permute-start(bf16[4,528,128]{2,1,0:T(8,128)(2,1)S(1)} %get-tuple-element.84), channel_id=1, source_target_pairs={{0,12},{1,13},{2,14},{3,15},{4,0},{5,1},{6,2},{7,3},{8,4},{9,5},{1... | collective-permute-start | bytes 1622024 | tf_op jit(solution)/shard_map/ppermute | solution.py:99
  171.4 13.1 %collective-permute-start.23 = (bf16[4,528,128]{2,1,0:T(8,128)(2,1)S(1)}, bf16[4,528,128]{2,1,0:T(8,128)(2,1)S(1)}, u32[]{:S(2)}, u32[]{:S(2)}) collective-permute-start(bf16[4,528,128]{2,1,0:T(8,128)(2,1)S(1)} %get-tuple-element.75), channel_id=1, source_target_pairs={{0,4},{1,5},{2,6},{3,7},{4,8},{5,9},{6,10},{7,11},{8,12},{9,13},{1... | collective-permute-start | bytes 1622024 | tf_op jit(solution)/shard_map/ppermute | solution.py:99
  171.4 26.7 %copy-start = (bf16[1024,128]{1,0:T(8,128)(2,1)S(1)}, bf16[1024,128]{1,0:T(8,128)(2,1)}, u32[]{:S(2)}) copy-start(bf16[1024,128]{1,0:T(8,128)(2,1)} %noise_ref.1) | copy-start | bytes 786436
  171.6 17.0 %collective-permute-start.19 = (bf16[4,528,128]{2,1,0:T(8,128)(2,1)S(1)}, bf16[4,528,128]{2,1,0:T(8,128)(2,1)S(1)}, u32[]{:S(2)}, u32[]{:S(2)}) collective-permute-start(bf16[4,528,128]{2,1,0:T(8,128)(2,1)S(1)} %get-tuple-element.78), channel_id=1, source_target_pairs={{0,3},{1,0},{2,1},{3,2},{4,7},{5,4},{6,5},{7,6},{8,11},{9,8},{10,9... | collective-permute-start | bytes 1622024 | tf_op jit(solution)/shard_map/ppermute | solution.py:95
  172.0 16.6 %collective-permute-start.18 = (bf16[4,528,128]{2,1,0:T(8,128)(2,1)S(1)}, bf16[4,528,128]{2,1,0:T(8,128)(2,1)S(1)}, u32[]{:S(2)}, u32[]{:S(2)}) collective-permute-start(bf16[4,528,128]{2,1,0:T(8,128)(2,1)S(1)} %get-tuple-element.73), channel_id=1, source_target_pairs={{0,1},{1,2},{2,3},{3,0},{4,5},{5,6},{6,7},{7,4},{8,9},{9,10},{10,1... | collective-permute-start | bytes 1622024 | tf_op jit(solution)/shard_map/ppermute | solution.py:95
  185.3 7.9 %collective-permute-start.25 = (bf16[528,128]{1,0:T(8,128)(2,1)S(1)}, bf16[528,128]{1,0:T(8,128)(2,1)S(1)}, u32[]{:S(2)}, u32[]{:S(2)}) collective-permute-start(bf16[528,128]{1,0:T(8,128)(2,1)S(1)} %get-tuple-element.86), channel_id=1, source_target_pairs={{0,1},{1,2},{2,3},{3,0},{4,5},{5,6},{6,7},{7,4},{8,9},{9,10},{10,1... | collective-permute-start | bytes 405512 | tf_op jit(solution)/shard_map/ppermute | solution.py:95
  185.3 8.5 %collective-permute-start.26 = (bf16[528,128]{1,0:T(8,128)(2,1)S(1)}, bf16[528,128]{1,0:T(8,128)(2,1)S(1)}, u32[]{:S(2)}, u32[]{:S(2)}) collective-permute-start(bf16[528,128]{1,0:T(8,128)(2,1)S(1)} %get-tuple-element.87), channel_id=1, source_target_pairs={{0,2},{1,3},{2,0},{3,1},{4,6},{5,7},{6,4},{7,5},{8,10},{9,11},{10,... | collective-permute-start | bytes 405512 | tf_op jit(solution)/shard_map/ppermute | solution.py:95
  187.4 6.5 %collective-permute-start.27 = (bf16[528,128]{1,0:T(8,128)(2,1)S(1)}, bf16[528,128]{1,0:T(8,128)(2,1)S(1)}, u32[]{:S(2)}, u32[]{:S(2)}) collective-permute-start(bf16[528,128]{1,0:T(8,128)(2,1)S(1)} %get-tuple-element.88), channel_id=1, source_target_pairs={{0,3},{1,0},{2,1},{3,2},{4,7},{5,4},{6,5},{7,6},{8,11},{9,8},{10,9... | collective-permute-start | bytes 405512 | tf_op jit(solution)/shard_map/ppermute | solution.py:95
  189.3 6.3 %collective-permute-start.20 = (bf16[528,128]{1,0:T(8,128)(2,1)S(1)}, bf16[528,128]{1,0:T(8,128)(2,1)S(1)}, u32[]{:S(2)}, u32[]{:S(2)}) collective-permute-start(bf16[528,128]{1,0:T(8,128)(2,1)S(1)} %get-tuple-element.80), channel_id=1, source_target_pairs={{0,4},{1,5},{2,6},{3,7},{4,8},{5,9},{6,10},{7,11},{8,12},{9,13},{1... | collective-permute-start | bytes 405512 | tf_op jit(solution)/shard_map/ppermute | solution.py:99
  189.4 8.2 %collective-permute-start.21 = (bf16[528,128]{1,0:T(8,128)(2,1)S(1)}, bf16[528,128]{1,0:T(8,128)(2,1)S(1)}, u32[]{:S(2)}, u32[]{:S(2)}) collective-permute-start(bf16[528,128]{1,0:T(8,128)(2,1)S(1)} %get-tuple-element.81), channel_id=1, source_target_pairs={{0,8},{1,9},{2,10},{3,11},{4,12},{5,13},{6,14},{7,15},{8,0},{9,1},... | collective-permute-start | bytes 405512 | tf_op jit(solution)/shard_map/ppermute | solution.py:99
  193.2 5.0 %collective-permute-start.22 = (bf16[528,128]{1,0:T(8,128)(2,1)S(1)}, bf16[528,128]{1,0:T(8,128)(2,1)S(1)}, u32[]{:S(2)}, u32[]{:S(2)}) collective-permute-start(bf16[528,128]{1,0:T(8,128)(2,1)S(1)} %get-tuple-element.82), channel_id=1, source_target_pairs={{0,12},{1,13},{2,14},{3,15},{4,0},{5,1},{6,2},{7,3},{8,4},{9,5},{1... | collective-permute-start | bytes 405512 | tf_op jit(solution)/shard_map/ppermute | solution.py:99
Sparse Core Ops, SparseCore 0:
  9.7 52.1 all-gather.2

commit v5 on v4

--- a/solution.py
+++ b/solution.py
@@ -214,8 +214,11 @@
 GROUP = 8
 
 
-def first_columns_kernel(parts_ref, score_ref, lse_ref, noise_ref, column, big, total):
+def first_columns_kernel(parts_ref, score_ref, lse_ref, noise_ref, e_ref, max_ref, column, big, total):
     step = pl.program_id(0)
+    blocks = ROWS // ROW_BLOCK
+    tiles = COLS // 128
+    base = lax.rem(step, blocks) * ROW_BLOCK
 
     @pl.when(step == 0)
     def _():
@@ -226,41 +229,54 @@
         big[...] = jnp.full(big.shape, MASKED, F32)
         total[...] = jnp.zeros(total.shape, F32)
 
-    base = step * ROW_BLOCK
-    tiles = COLS // 128
-
-    def largest(g, carry):
-        shift = column[pl.ds(pl.multiple_of(base + g * GROUP, GROUP), GROUP), :]
-        at = pl.ds(pl.multiple_of(g * GROUP, GROUP), GROUP)
-        return tuple(jnp.maximum(carry[t], score_ref[at, 128 * t : 128 * (t + 1)] + shift) for t in range(tiles))
-
-    old = tuple(big[:, 128 * t : 128 * (t + 1)] for t in range(tiles))
-    new = lax.fori_loop(0, ROW_BLOCK // GROUP, largest, old, unroll=2)
-
-    def add(g, carry):
-        shift = column[pl.ds(pl.multiple_of(base + g * GROUP, GROUP), GROUP), :]
-        at = pl.ds(pl.multiple_of(g * GROUP, GROUP), GROUP)
-        return tuple(
-            carry[t] + jnp.exp2(score_ref[at, 128 * t : 128 * (t + 1)] + (shift - new[t])) for t in range(tiles)
-        )
-
-    start = tuple(total[:, 128 * t : 128 * (t + 1)] * jnp.exp2(old[t] - new[t]) for t in range(tiles))
-    summed = lax.fori_loop(0, ROW_BLOCK // GROUP, add, start, unroll=2)
-    for t in range(tiles):
-        big[:, 128 * t : 128 * (t + 1)] = new[t]
-        total[:, 128 * t : 128 * (t + 1)] = summed[t]
-
-    @pl.when(step == pl.num_programs(0) - 1)
-    def _():
-        m = jnp.max(big[...], axis=0, keepdims=True)
-        s = jnp.sum(total[...] * jnp.exp2(big[...] - m), axis=0, keepdims=True)
-        lse_ref[...] = jnp.broadcast_to(from_lanes(m + jnp.log2(s))[None], lse_ref.shape)
-
-
-def pass_call(kernel, inputs, in_specs, outs, out_specs, scratch, name, transcendentals=0):
+    @pl.when(step < blocks)
+    def _():
+        def largest(g, carry):
+            shift = column[pl.ds(pl.multiple_of(base + g * GROUP, GROUP), GROUP), :]
+            at = pl.ds(pl.multiple_of(g * GROUP, GROUP), GROUP)
+            return tuple(jnp.maximum(carry[t], score_ref[at, 128 * t : 128 * (t + 1)] + shift) for t in range(tiles))
+
+        start = tuple(big[:, 128 * t : 128 * (t + 1)] for t in range(tiles))
+        new = lax.fori_loop(0, ROW_BLOCK // GROUP, largest, start, unroll=2)
+        for t in range(tiles):
+            big[:, 128 * t : 128 * (t + 1)] = new[t]
+
+    @pl.when(step == blocks)
+    def _():
+        big[...] = jnp.broadcast_to(jnp.max(big[...], axis=0, keepdims=True), big.shape)
+
+    @pl.when(step >= blocks)
+    def _():
+        most = [big[:, 128 * t : 128 * (t + 1)] for t in range(tiles)]
+
+        def add(g, carry):
+            shift = column[pl.ds(pl.multiple_of(base + g * GROUP, GROUP), GROUP), :]
+            at = pl.ds(pl.multiple_of(g * GROUP, GROUP), GROUP)
+            out = []
+            for t in range(tiles):
+                here = slice(128 * t, 128 * (t + 1))
+                value = jnp.exp2(score_ref[at, here] + (shift - most[t]))
+                e_ref[at, here] = value
+                out.append(carry[t] + value)
+            return tuple(out)
+
+        start = tuple(total[:, 128 * t : 128 * (t + 1)] for t in range(tiles))
+        summed = lax.fori_loop(0, ROW_BLOCK // GROUP, add, start, unroll=2)
+        for t in range(tiles):
+            total[:, 128 * t : 128 * (t + 1)] = summed[t]
+
+    @pl.when(step == 2 * blocks - 1)
+    def _():
+        most = big[0:1, :]
+        s = jnp.sum(total[...], axis=0, keepdims=True)
+        lse_ref[...] = jnp.broadcast_to(from_lanes(most + jnp.log2(s))[None], lse_ref.shape)
+        max_ref[...] = from_lanes(most)
+
+
+def pass_call(kernel, inputs, in_specs, outs, out_specs, scratch, name, transcendentals=0, sweeps=1):
     return pl.pallas_call(
         kernel,
-        grid=(ROWS // ROW_BLOCK,),
+        grid=(sweeps * (ROWS // ROW_BLOCK),),
         in_specs=in_specs,
         out_specs=out_specs,
         out_shape=outs,
@@ -284,15 +300,17 @@
 
 
 def first_columns(parts, score):
+    blocks = ROWS // ROW_BLOCK
     return pass_call(
         first_columns_kernel,
         (parts, score),
-        [FROM_COL, BLOCK],
-        [FROM_ROW_SHAPE, NOISE_SHAPE],
-        [FROM_ROW, NOISE],
+        [FROM_COL, vmem((ROW_BLOCK, COLS), lambda i: (lax.rem(i, blocks), 0))],
+        [FROM_ROW_SHAPE, NOISE_SHAPE, BLOCK_SHAPE, DATA_SHAPE],
+        [FROM_ROW, NOISE, vmem((ROW_BLOCK, COLS), lambda i: (jnp.maximum(i - blocks, 0), 0)), DATA],
         [pltpu.VMEM((ROWS, 128), F32), pltpu.VMEM((8, COLS), F32), pltpu.VMEM((8, COLS), F32)],
         "first_columns",
         ROWS * COLS,
+        2,
     )
 
 
@@ -307,56 +325,7 @@
         out_ref[...] = jnp.broadcast_to(rows[...][None], out_ref.shape)
 
 
-def kernel_matrix_kernel(parts_ref, noise_ref, score_ref, k_ref, sums_ref, data_ref, column, lanes, sums, rows):
-    step = pl.program_id(0)
-
-    @pl.when(step == 0)
-    def _():
-        potential = merge_lse(parts_ref)
-        data_ref[...] = potential
-        lanes[...] = jnp.broadcast_to(to_lanes(potential), lanes.shape)
-        for a, piece in enumerate(to_column(noise_ref[...])):
-            column[128 * a : 128 * (a + 1), :] = piece
-
-    base = step * ROW_BLOCK
-    tiles = COLS // 128
-    shifts = [lanes[:, 128 * t : 128 * (t + 1)] for t in range(tiles)]
-
-    def body(g, _):
-        shift = column[pl.ds(pl.multiple_of(base + g * GROUP, GROUP), GROUP), :]
-        at = pl.ds(pl.multiple_of(g * GROUP, GROUP), GROUP)
-        summed = jnp.zeros((GROUP, 128), F32)
-        for t in range(tiles):
-            here = slice(128 * t, 128 * (t + 1))
-            value = jnp.exp2(score_ref[at, here] + shift + shifts[t])
-            k_ref[at, here] = value
-            summed += value
-        sums[at, :] = summed
-        return 0
-
-    lax.fori_loop(0, ROW_BLOCK // GROUP, body, 0, unroll=2)
-    write_row_sums(sums, sums_ref, rows, step)
-
-
-def kernel_matrix(parts, noise_potential, score):
-    return pass_call(
-        kernel_matrix_kernel,
-        (parts, noise_potential, score),
-        [FROM_ROW, NOISE, BLOCK],
-        [BLOCK_SHAPE, FROM_COL_SHAPE, DATA_SHAPE],
-        [BLOCK, FROM_COL, DATA],
-        [
-            pltpu.VMEM((ROWS, 128), F32),
-            pltpu.VMEM((GROUP, COLS), F32),
-            pltpu.VMEM((ROW_BLOCK, 128), F32),
-            pltpu.VMEM((8, 128), F32),
-        ],
-        "kernel_matrix",
-        ROWS * COLS,
-    )
-
-
-def column_sums_kernel(parts_ref, k_ref, sums_ref, scale_ref, column, total):
+def column_sums_kernel(parts_ref, factor_ref, k_ref, sums_ref, scale_ref, column, total):
     step = pl.program_id(0)
 
     @pl.when(step == 0)
@@ -383,14 +352,14 @@
     @pl.when(step == pl.num_programs(0) - 1)
     def _():
         s = jnp.sum(total[...], axis=0, keepdims=True)
-        sums_ref[...] = jnp.broadcast_to(from_lanes(s)[None], sums_ref.shape)
-
-
-def column_sums(parts, k):
+        sums_ref[...] = jnp.broadcast_to((from_lanes(s) * factor_ref[...])[None], sums_ref.shape)
+
+
+def column_sums(parts, factor, k):
     return pass_call(
         column_sums_kernel,
-        (parts, k),
-        [FROM_COL, BLOCK],
+        (parts, factor, k),
+        [FROM_COL, DATA, BLOCK],
         [FROM_ROW_SHAPE, NOISE_SHAPE],
         [FROM_ROW, NOISE],
         [pltpu.VMEM((ROWS, 128), F32), pltpu.VMEM((GROUP, COLS), F32)],
@@ -398,12 +367,21 @@
     )
 
 
-def row_sums_kernel(parts_ref, k_ref, sums_ref, lanes, sums, rows):
+def row_sums_kernel(first, parts_ref, factor_ref, k_ref, sums_ref, *refs):
+    lanes, sums, rows = refs[-3:]
     step = pl.program_id(0)
 
     @pl.when(step == 0)
     def _():
-        lanes[...] = jnp.broadcast_to(to_lanes(merge_scale(parts_ref)), lanes.shape)
+        if first:
+            data_ref, out_ref = refs[:2]
+            potential = merge_lse(parts_ref)
+            data_ref[...] = potential
+            scale = jnp.exp2(factor_ref[...] + potential)
+            out_ref[...] = scale
+        else:
+            scale = factor_ref[...] * merge_scale(parts_ref)
+        lanes[...] = jnp.broadcast_to(to_lanes(scale), lanes.shape)
 
     tiles = COLS // 128
     scales = [lanes[:, 128 * t : 128 * (t + 1)] for t in range(tiles)]
@@ -420,20 +398,21 @@
     write_row_sums(sums, sums_ref, rows, step)
 
 
-def row_sums(parts, k):
+def row_sums(first, parts, factor, k):
+    more = 2 if first else 0
     return pass_call(
-        row_sums_kernel,
-        (parts, k),
-        [FROM_ROW, BLOCK],
-        [FROM_COL_SHAPE],
-        [FROM_COL],
+        functools.partial(row_sums_kernel, first),
+        (parts, factor, k),
+        [FROM_ROW, DATA, BLOCK],
+        [FROM_COL_SHAPE] + [DATA_SHAPE] * more,
+        [FROM_COL] + [DATA] * more,
         [pltpu.VMEM((GROUP, COLS), F32), pltpu.VMEM((ROW_BLOCK, 128), F32), pltpu.VMEM((8, 128), F32)],
         "row_sums",
-    )[0]
+    )
 
 
 def coupling_kernel(
-    parts_ref, scale_ref, noise_first, noise_sq, data_first, data_sq, k_ref,
+    parts_ref, scale_ref, noise_first, noise_sq, data_first, data_sq, factor_ref, k_ref,
     pa_ref, pb_ref, sums_ref, noise_ref, data_ref, column, lanes, sums,
 ):
     step = pl.program_id(0)
@@ -441,7 +420,7 @@
     @pl.when(step == 0)
     def _():
         scale = merge_scale(parts_ref)
-        lanes[...] = jnp.broadcast_to(to_lanes(scale), lanes.shape)
+        lanes[...] = jnp.broadcast_to(to_lanes(factor_ref[...] * scale), lanes.shape)
         for a, piece in enumerate(to_column(scale_ref[...])):
             column[128 * a : 128 * (a + 1), :] = piece
         noise_ref[...] = (EPS * LN2) * (noise_first[...] + jnp.log2(scale_ref[...])) + noise_sq[...] * (1.0 / WIDTH)
@@ -483,12 +462,12 @@
         sums_ref[pl.ds(step * per + a, 1), :] = jnp.sum(piece, axis=0, keepdims=True)
 
 
-def coupling(parts, noise_scale, noise_first, noise_sq, data_first, data_sq, k):
+def coupling(parts, noise_scale, noise_first, noise_sq, data_first, data_sq, factor, k):
     half = jax.ShapeDtypeStruct((HALF, COLS), BF16)
     return pass_call(
         coupling_kernel,
-        (parts, noise_scale, noise_first, noise_sq, data_first, data_sq, k),
-        [FROM_ROW, NOISE, NOISE, NOISE, DATA, vmem((COLS // COL_BLOCK, COL_BLOCK // 128, 128)), BLOCK],
+        (parts, noise_scale, noise_first, noise_sq, data_first, data_sq, factor, k),
+        [FROM_ROW, NOISE, NOISE, NOISE, DATA, vmem((COLS // COL_BLOCK, COL_BLOCK // 128, 128)), DATA, BLOCK],
         [half, half, NOISE_SHAPE, NOISE_SHAPE, DATA_SHAPE],
         [
             vmem((ROW_BLOCK, COLS), lambda i: (jnp.minimum(i, 1), 0)),
@@ -650,13 +629,13 @@
     data = lax.all_gather(data_latents, "row")
     noise, noise_sq = arrange(info, gather_noise(noise_latents))
     score, lse, data_sq = scores(info, noise, data)
-    lse, noise_first = first_columns(swap(lse, "col"), score)
-    k, sums, data_first = kernel_matrix(swap(lse, "row"), noise_first, score)
-    sums, _ = column_sums(swap(sums, "col"), k)
-    sums = row_sums(swap(sums, "row"), k)
-    sums, noise_scale = column_sums(swap(sums, "col"), k)
+    lse, noise_first, e, most = first_columns(swap(lse, "col"), score)
+    sums, data_first, factor = row_sums(True, swap(lse, "row"), most, e)
+    sums, _ = column_sums(swap(sums, "col"), factor, e)
+    sums = row_sums(False, swap(sums, "row"), factor, e)[0]
+    sums, noise_scale = column_sums(swap(sums, "col"), factor, e)
     *p, sums, noise_potential, data_potential = coupling(
-        swap(sums, "row"), noise_scale, noise_first, noise_sq, data_first, data_sq, k
+        swap(sums, "row"), noise_scale, noise_first, noise_sq, data_first, data_sq, factor, e
     )
     way = (over_x, over_z)
     made = messages((2,), info, p, sums, data)

time: 206 us -> 205 us (level)
  no operation moved by 1% of the time
where the time goes in v5:
time: 205 us; the launch traced here: 204 us
  blocking collectives  61.1 us (30%)
  Pallas kernels  43.1 us (21%)
  starting transfers between devices  42.7 us (21%)
  waiting for transfers between devices  34.4 us (17%)
  between operations  14.2 us (7%)
  local copies, waits for them, and re-layouts  8.92 us (4%)
    all_to_all x6, blocking collectives, swap(): return lax.all_to_all(x, axis, 0, 0, tiled=True)  61.1 us
    ppermute x14, starting transfers between devices, over_z(): lax.ppermute(v, 'col', [(4 * z + x, 4 * ((z + d) % 4) + x) for z in range...  22.1 us
    ppermute x14, starting transfers between devices, over_x(): lax.ppermute(v, 'col', [(4 * z + x, 4 * z + (x + d) % 4) for z in range(4...  20.5 us
    ppermute x14, waiting for transfers between devices, over_z(): lax.ppermute(v, 'col', [(4 * z + x, 4 * ((z + d) % 4) + x) for z in range...  15.8 us
    pallas_call x1, Pallas kernels, scores(): pl.pallas_call(score_kernel, grid=(COLS // COL_BLOCK,), in_specs=[pl.Bloc...  14.5 us
    ppermute x14, waiting for transfers between devices, over_x(): lax.ppermute(v, 'col', [(4 * z + x, 4 * z + (x + d) % 4) for z in range(4...  13.5 us
    pallas_call x6, Pallas kernels, pass_call(): pl.pallas_call(kernel, grid=(sweeps * (ROWS // ROW_BLOCK),), in_specs=in_...  11.7 us
    pallas_call x3, Pallas kernels, messages(): pl.pallas_call(functools.partial(target_kernel, ways), in_specs=[pl.Block...  11 us
  transfers between devices with their start and end apart: 29, of which 13 were waited for; matrix products, arithmetic and copies ran while one was open for 2% of the time, Pallas kernels for 6%

profile of v5, /device:TPU:0, one launch (start us, length us, event | category | flops | bytes accessed | tf_op | source)
XLA Modules:
  0.0 204.5 jit_solution(4941286232613717753)
XLA Ops:
  7.9 1.0 slice_bitcast_fusion
  8.9 4.0 %collective-permute-start.8 = (bf16[512,128]{1,0:T(8,128)(2,1)S(1)}, bf16[512,128]{1,0:T(8,128)(2,1)S(1)}, u32[]{:S(2)}, u32[]{:S(2)}) collective-permute-start(bf16[512,128]{1,0:T(8,128)(2,1)S(1)} %get-tuple-element.98), channel_id=1, source_target_pairs={{0,8},{1,9},{2,10},{3,11},{4,12},{5,13},{6,14},{7,15},{8,0},{9,1},... | collective-permute-start | bytes 393224 | tf_op jit(solution)/shard_map/ppermute | solution.py:99
  13.0 1.0 collective-permute-start.7
  14.0 2.2 %collective-permute-start.9 = (bf16[512,128]{1,0:T(8,128)(2,1)S(1)}, bf16[512,128]{1,0:T(8,128)(2,1)S(1)}, u32[]{:S(2)}, u32[]{:S(2)}) collective-permute-start(bf16[512,128]{1,0:T(8,128)(2,1)S(1)} %get-tuple-element.98), channel_id=1, source_target_pairs={{0,12},{1,13},{2,14},{3,15},{4,0},{5,1},{6,2},{7,3},{8,4},{9,5},{1... | collective-permute-start | bytes 393224 | tf_op jit(solution)/shard_map/ppermute | solution.py:99
  16.2 3.0 %collective-permute-start.1 = (bf16[512,128]{1,0:T(8,128)(2,1)S(1)}, bf16[512,128]{1,0:T(8,128)(2,1)S(1)}, u32[]{:S(2)}, u32[]{:S(2)}) collective-permute-start(bf16[512,128]{1,0:T(8,128)(2,1)S(1)} %get-tuple-element.97), channel_id=1, source_target_pairs={{0,2},{1,3},{2,0},{3,1},{4,6},{5,7},{6,4},{7,5},{8,10},{9,11},{10,... | collective-permute-start | bytes 393224 | tf_op jit(solution)/shard_map/ppermute | solution.py:95
  19.8 2.6 %collective-permute-start.2 = (bf16[512,128]{1,0:T(8,128)(2,1)S(1)}, bf16[512,128]{1,0:T(8,128)(2,1)S(1)}, u32[]{:S(2)}, u32[]{:S(2)}) collective-permute-start(bf16[512,128]{1,0:T(8,128)(2,1)S(1)} %get-tuple-element.97), channel_id=1, source_target_pairs={{0,3},{1,0},{2,1},{3,2},{4,7},{5,4},{6,5},{7,6},{8,11},{9,8},{10,9... | collective-permute-start | bytes 393224 | tf_op jit(solution)/shard_map/ppermute | solution.py:95
  22.9 1.7 collective-permute-start.10
  24.7 1.3 collective-permute-done
  27.5 1.4 collective-permute-start.3
  28.9 7.4 %collective-permute-done.11.refs_7_ = bf16[4,512,128]{2,1,0:T(8,128)(2,1)S(1)} collective-permute-done((bf16[4,512,128]{2,1,0:T(8,128)(2,1)S(1)}, bf16[4,512,128]{2,1,0:T(8,128)(2,1)S(1)}, u32[]{:S(2)}, u32[]{:S(2)}) %collective-permute-start.11) | collective-permute-done | bytes 524320 | tf_op jit(solution)/shard_map/ppermute | solution.py:95
  37.0 3.5 %collective-permute-start.13 = (bf16[2,512,128]{2,1,0:T(8,128)(2,1)}, bf16[2,512,128]{2,1,0:T(8,128)(2,1)S(1)}, u32[]{:S(2)}, u32[]{:S(2)}) collective-permute-start(bf16[2,512,128]{2,1,0:T(8,128)(2,1)} %slice.27), channel_id=1, source_target_pairs={{0,3},{1,0},{2,1},{3,2},{4,7},{5,4},{6,5},{7,6},{8,11},{9,8},{10,9... | collective-permute-start | bytes 786440 | tf_op jit(solution)/shard_map/ppermute | solution.py:95
  42.0 1.4 collective-permute-start.6
  44.7 0.7 concatenate.3.info_ref
  45.5 3.9 %collective-permute-done.12.refs_8_ = bf16[2,512,128]{2,1,0:T(8,128)(2,1)} collective-permute-done((bf16[2,512,128]{2,1,0:T(8,128)(2,1)}, bf16[2,512,128]{2,1,0:T(8,128)(2,1)}, u32[]{:S(2)}, u32[]{:S(2)}) %collective-permute-start.12) | collective-permute-done | bytes 262176 | tf_op jit(solution)/shard_map/ppermute | solution.py:95
  49.3 3.0 %collective-permute-done.5.refs_3_ = bf16[2,512,128]{2,1,0:T(8,128)(2,1)} collective-permute-done((bf16[2,512,128]{2,1,0:T(8,128)(2,1)}, bf16[2,512,128]{2,1,0:T(8,128)(2,1)}, u32[]{:S(2)}, u32[]{:S(2)}) %collective-permute-start.5) | collective-permute-done | bytes 262176 | tf_op jit(solution)/shard_map/ppermute | solution.py:99
  52.4 3.1 %arrange.1 = (bf16[1024,2048]{1,0:T(8,128)(2,1)S(1)}, f32[8,128]{1,0:T(8,128)S(1)}) custom-call(s32[20]{0:T(128)S(1)} %concatenate.3.info_ref, bf16[4,512,128]{2,1,0:T(8,128)(2,1)S(1)} %pad_maximum_fusion.refs_0_, bf16[4,512,128]{2,1,0:T(8,128)(2,1)S(1)} %collective-permute-done.3.refs_1_, bf16[4,512,128]{2,1,0:T(8,128)(2,1)S(1)} %collective-permute-done.4.refs_2_, ...), custom_call_target="tpu_custom_call" | custom-call | flops 4194304 | bytes 8388608 | tf_op jit(solution)/shard_map/arrange/pallas_call | solution.py:84
  55.5 2.0 copy-done.1
  57.6 4.4 %all-gather.3.cloned.1.call-done = bf16[16384,256]{1,0:T(8,128)(2,1)} async-done(((bf16[2048,256]{1,0:T(8,128)(2,1)}), bf16[16384,256]{1,0:T(8,128)(2,1)}) %all-gather.3.cloned.1.call-update) | async-done | bytes 8388624 | tf_op jit(solution)/shard_map/all_gather | solution.py:629
  61.9 2.2 %copy-done.2 = bf16[1024,2048]{1,0:T(8,128)(2,1)S(1)} copy-done((bf16[1024,2048]{1,0:T(8,128)(2,1)S(1)}, bf16[1024,2048]{1,0:T(8,128)(2,1)}, u32[]{:S(2)}) %copy-start.2) | copy-done | bytes 4194328
  64.1 14.5 %scores.1 = (f32[1024,2048]{1,0:T(8,128)S(1)}, f32[16,8,128]{2,1,0:T(8,128)S(1)}, f32[4,4,128]{2,1,0:T(4,128)S(1)}) custom-call(s32[20]{0:T(128)S(1)} %concatenate.3.info_ref, bf16[1024,2048]{1,0:T(8,128)(2,1)S(1)} %copy-done.2, bf16[8,2048,256]{2,1,0:T(8,128)(2,1)} %bitcast.17), custom_call_target="tpu_custom_call" | custom-call | flops 8589934592 | bytes 20971520 | tf_op jit(solution)/shard_map/scores/pallas_call | solution.py:179
  78.7 14.4 %all_to_all.30.parts_ref = f32[16,8,128]{2,1,0:T(8,128)S(1)} all-to-all(f32[16,8,128]{2,1,0:T(8,128)S(1)} %get-tuple-element.50), channel_id=1, replica_groups=mesh['row'=8,'col'=16] {'col'}, dimensions={0} | all-to-all | bytes 131072 | tf_op jit(solution)/shard_map/all_to_all | solution.py:622
  93.1 3.4 %first_columns.1 = (f32[8,16,128]{2,1,0:T(8,128)S(1)}, f32[8,128]{1,0:T(8,128)S(1)}, f32[1024,2048]{1,0:T(8,128)S(1)}, f32[16,128]{1,0:T(8,128)S(1)}) custom-call(f32[16,8,128]{2,1,0:T(8,128)S(1)} %all_to_all.30.parts_ref, f32[1024,2048]{1,0:T(8,128)S(1)} %get-tuple-element.51.score_ref), custom_call_target="tpu_custom_call" | custom-call | flops 8388608 | bytes 8388608 | tf_op jit(solution)/shard_map/first_columns/pallas_call | solution.py:277
  96.5 8.6 %all_to_all.31.parts_ref = f32[8,16,128]{2,1,0:T(8,128)S(1)} all-to-all(f32[8,16,128]{2,1,0:T(8,128)S(1)} %get-tuple-element.52), channel_id=1, replica_groups=mesh['row'=8,'col'=16] {'row'}, dimensions={0} | all-to-all | bytes 131072 | tf_op jit(solution)/shard_map/all_to_all | solution.py:622
  105.1 1.3 row_sums.2
  106.4 10.8 %all_to_all.32.parts_ref = f32[16,8,128]{2,1,0:T(8,128)S(1)} all-to-all(f32[16,8,128]{2,1,0:T(8,128)S(1)} %get-tuple-element.55), channel_id=1, replica_groups=mesh['row'=8,'col'=16] {'col'}, dimensions={0} | all-to-all | bytes 131072 | tf_op jit(solution)/shard_map/all_to_all | solution.py:622
  117.2 1.6 column_sums.2
  118.8 8.0 %all_to_all.33.parts_ref = f32[8,16,128]{2,1,0:T(8,128)S(1)} all-to-all(f32[8,16,128]{2,1,0:T(8,128)S(1)} %get-tuple-element.57), channel_id=1, replica_groups=mesh['row'=8,'col'=16] {'row'}, dimensions={0} | all-to-all | bytes 131072 | tf_op jit(solution)/shard_map/all_to_all | solution.py:622
  126.8 1.2 row_sums.3
  128.1 10.8 %all_to_all.34.parts_ref = f32[16,8,128]{2,1,0:T(8,128)S(1)} all-to-all(f32[16,8,128]{2,1,0:T(8,128)S(1)} %row_sums.3), channel_id=1, replica_groups=mesh['row'=8,'col'=16] {'col'}, dimensions={0} | all-to-all | bytes 131072 | tf_op jit(solution)/shard_map/all_to_all | solution.py:622
  138.9 1.0 column_sums.3
  139.9 8.4 %all_to_all.35.parts_ref = f32[8,16,128]{2,1,0:T(8,128)S(1)} all-to-all(f32[8,16,128]{2,1,0:T(8,128)S(1)} %get-tuple-element.58), channel_id=1, replica_groups=mesh['row'=8,'col'=16] {'row'}, dimensions={0} | all-to-all | bytes 131072 | tf_op jit(solution)/shard_map/all_to_all | solution.py:622
  148.4 3.1 %coupling.1 = (bf16[512,2048]{1,0:T(8,128)(2,1)S(1)}, bf16[512,2048]{1,0:T(8,128)(2,1)S(1)}, f32[8,128]{1,0:T(8,128)S(1)}, f32[8,128]{1,0:T(8,128)}, f32[16,128]{1,0:T(8,128)}) custom-call(f32[8,16,128]{2,1,0:T(8,128)S(1)} %all_to_all.35.parts_ref, f32[8,128]{1,0:T(8,128)S(1)} %get-tuple-element.59.scale_ref, f32[8,128]{1,0:T(8,128)S(1)} %get-tuple-element.60.noise_first, ...), custom_call_target="tpu_custom_call" | custom-call | flops 8388608 | bytes 8388608 | tf_op jit(solution)/shard_map/coupling/pallas_call | solution.py:277
  151.5 2.9 %targets.3 = (bf16[4,272,128]{2,1,0:T(8,128)(2,1)S(1)}, bf16[4,272,128]{2,1,0:T(8,128)(2,1)S(1)}, bf16[4,272,128]{2,1,0:T(8,128)(2,1)S(1)}, bf16[4,272,128]{2,1,0:T(8,128)(2,1)S(1)}) custom-call(s32[20]{0:T(128)S(1)} %concatenate.3.info_ref, bf16[512,2048]{1,0:T(8,128)(2,1)S(1)} %get-tuple-element.64.pa_ref, bf16[512,2048]{1,0:T(8,128)(2,1)S(1)} %get-tuple-element.65.pb_ref, ...), custom_call_target="tpu_custom_call" | custom-call | flops 2147483648 | bytes 8388608 | tf_op jit(solution)/shard_map/targets/pallas_call | solution.py:528
  155.1 2.7 %collective-permute-start.15 = (bf16[4,272,128]{2,1,0:T(8,128)(2,1)S(1)}, bf16[4,272,128]{2,1,0:T(8,128)(2,1)S(1)}, u32[]{:S(2)}, u32[]{:S(2)}) collective-permute-start(bf16[4,272,128]{2,1,0:T(8,128)(2,1)S(1)} %get-tuple-element.68), channel_id=1, source_target_pairs={{0,3},{1,0},{2,1},{3,2},{4,7},{5,4},{6,5},{7,6},{8,11},{9,8},{10,9... | collective-permute-start | bytes 835592 | tf_op jit(solution)/shard_map/ppermute | solution.py:95
  158.3 2.7 %collective-permute-start.17 = (bf16[4,272,128]{2,1,0:T(8,128)(2,1)S(1)}, bf16[4,272,128]{2,1,0:T(8,128)(2,1)S(1)}, u32[]{:S(2)}, u32[]{:S(2)}) collective-permute-start(bf16[4,272,128]{2,1,0:T(8,128)(2,1)S(1)} %get-tuple-element.70), channel_id=1, source_target_pairs={{0,12},{1,13},{2,14},{3,15},{4,0},{5,1},{6,2},{7,3},{8,4},{9,5},{1... | collective-permute-start | bytes 835592 | tf_op jit(solution)/shard_map/ppermute | solution.py:99
  161.0 5.1 %targets.4 = (bf16[4,528,128]{2,1,0:T(8,128)(2,1)S(1)}, bf16[4,528,128]{2,1,0:T(8,128)(2,1)S(1)}, bf16[4,528,128]{2,1,0:T(8,128)(2,1)S(1)}, bf16[4,528,128]{2,1,0:T(8,128)(2,1)S(1)}) custom-call(s32[20]{0:T(128)S(1)} %concatenate.3.info_ref, bf16[512,2048]{1,0:T(8,128)(2,1)S(1)} %get-tuple-element.64.pa_ref, bf16[512,2048]{1,0:T(8,128)(2,1)S(1)} %get-tuple-element.65.pb_ref, ...), custom_call_target="tpu_custom_call" | custom-call | flops 4294967296 | bytes 8388608 | tf_op jit(solution)/shard_map/targets/pallas_call | solution.py:528
  166.8 3.0 %collective-permute-start.24 = (bf16[4,528,128]{2,1,0:T(8,128)(2,1)S(1)}, bf16[4,528,128]{2,1,0:T(8,128)(2,1)S(1)}, u32[]{:S(2)}, u32[]{:S(2)}) collective-permute-start(bf16[4,528,128]{2,1,0:T(8,128)(2,1)S(1)} %get-tuple-element.88), channel_id=1, source_target_pairs={{0,12},{1,13},{2,14},{3,15},{4,0},{5,1},{6,2},{7,3},{8,4},{9,5},{1... | collective-permute-start | bytes 1622024 | tf_op jit(solution)/shard_map/ppermute | solution.py:99
  170.4 1.7 collective-permute-start.18
  172.1 2.9 %targets.5 = (bf16[4,528,128]{2,1,0:T(8,128)(2,1)S(1)}, bf16[4,528,128]{2,1,0:T(8,128)(2,1)S(1)}) custom-call(s32[20]{0:T(128)S(1)} %concatenate.3.info_ref, bf16[512,2048]{1,0:T(8,128)(2,1)S(1)} %get-tuple-element.64.pa_ref, bf16[512,2048]{1,0:T(8,128)(2,1)S(1)} %get-tuple-element.65.pb_ref, f32[8,128]{1,0:T(8,128)S(1)} %get-tuple-element.80.sums_ref, ...), custom_call_target="tpu_custom_call" | custom-call | flops 2147483648 | bytes 8388608 | tf_op jit(solution)/shard_map/targets/pallas_call | solution.py:528
  175.1 4.5 %collective-permute-done.24.right = bf16[4,528,128]{2,1,0:T(8,128)(2,1)S(1)} collective-permute-done((bf16[4,528,128]{2,1,0:T(8,128)(2,1)S(1)}, bf16[4,528,128]{2,1,0:T(8,128)(2,1)S(1)}, u32[]{:S(2)}, u32[]{:S(2)}) %collective-permute-start.24) | collective-permute-done | bytes 540704 | tf_op jit(solution)/shard_map/ppermute | solution.py:99
  179.5 3.4 %collective-permute-done.23.left = bf16[4,528,128]{2,1,0:T(8,128)(2,1)S(1)} collective-permute-done((bf16[4,528,128]{2,1,0:T(8,128)(2,1)S(1)}, bf16[4,528,128]{2,1,0:T(8,128)(2,1)S(1)}, u32[]{:S(2)}, u32[]{:S(2)}) %collective-permute-start.23) | collective-permute-done | bytes 540704 | tf_op jit(solution)/shard_map/ppermute | solution.py:99
  183.8 2.0 collective-permute-start.26
  185.8 1.2 collective-permute-start.27
  187.0 0.7 combine.2
  187.8 3.7 %collective-permute-start.21 = (bf16[528,128]{1,0:T(8,128)(2,1)S(1)}, bf16[528,128]{1,0:T(8,128)(2,1)S(1)}, u32[]{:S(2)}, u32[]{:S(2)}) collective-permute-start(bf16[528,128]{1,0:T(8,128)(2,1)S(1)} %get-tuple-element.85), channel_id=1, source_target_pairs={{0,8},{1,9},{2,10},{3,11},{4,12},{5,13},{6,14},{7,15},{8,0},{9,1},... | collective-permute-start | bytes 405512 | tf_op jit(solution)/shard_map/ppermute | solution.py:99
  192.3 1.7 collective-permute-done.20.refs_1_
  194.0 2.0 collective-permute-done.21.refs_2_
  196.6 1.0 finish.1
  (52 shorter events, 11.4 us)
Async XLA Ops:
  7.2 54.8 %all-gather.3.cloned.1.call-start = ((), (), s32[]{:S(2)}) async-start(), calls=%async_computation.6 | async-start | bytes 9437184 | tf_op jit(solution)/shard_map/all_gather | solution.py:629
  8.9 10.9 %collective-permute-start.8 = (bf16[512,128]{1,0:T(8,128)(2,1)S(1)}, bf16[512,128]{1,0:T(8,128)(2,1)S(1)}, u32[]{:S(2)}, u32[]{:S(2)}) collective-permute-start(bf16[512,128]{1,0:T(8,128)(2,1)S(1)} %get-tuple-element.98), channel_id=1, source_target_pairs={{0,8},{1,9},{2,10},{3,11},{4,12},{5,13},{6,14},{7,15},{8,0},{9,1},... | collective-permute-start | bytes 393224 | tf_op jit(solution)/shard_map/ppermute | solution.py:99
  13.0 9.5 %collective-permute-start.7 = (bf16[512,128]{1,0:T(8,128)(2,1)S(1)}, bf16[512,128]{1,0:T(8,128)(2,1)S(1)}, u32[]{:S(2)}, u32[]{:S(2)}) collective-permute-start(bf16[512,128]{1,0:T(8,128)(2,1)S(1)} %get-tuple-element.98), channel_id=1, source_target_pairs={{0,4},{1,5},{2,6},{3,7},{4,8},{5,9},{6,10},{7,11},{8,12},{9,13},{1... | collective-permute-start | bytes 393224 | tf_op jit(solution)/shard_map/ppermute | solution.py:99
  14.0 8.5 %collective-permute-start.9 = (bf16[512,128]{1,0:T(8,128)(2,1)S(1)}, bf16[512,128]{1,0:T(8,128)(2,1)S(1)}, u32[]{:S(2)}, u32[]{:S(2)}) collective-permute-start(bf16[512,128]{1,0:T(8,128)(2,1)S(1)} %get-tuple-element.98), channel_id=1, source_target_pairs={{0,12},{1,13},{2,14},{3,15},{4,0},{5,1},{6,2},{7,3},{8,4},{9,5},{1... | collective-permute-start | bytes 393224 | tf_op jit(solution)/shard_map/ppermute | solution.py:99
  16.2 8.4 %collective-permute-start.1 = (bf16[512,128]{1,0:T(8,128)(2,1)S(1)}, bf16[512,128]{1,0:T(8,128)(2,1)S(1)}, u32[]{:S(2)}, u32[]{:S(2)}) collective-permute-start(bf16[512,128]{1,0:T(8,128)(2,1)S(1)} %get-tuple-element.97), channel_id=1, source_target_pairs={{0,2},{1,3},{2,0},{3,1},{4,6},{5,7},{6,4},{7,5},{8,10},{9,11},{10,... | collective-permute-start | bytes 393224 | tf_op jit(solution)/shard_map/ppermute | solution.py:95
  19.2 6.8 %collective-permute-start = (bf16[512,128]{1,0:T(8,128)(2,1)S(1)}, bf16[512,128]{1,0:T(8,128)(2,1)S(1)}, u32[]{:S(2)}, u32[]{:S(2)}) collective-permute-start(bf16[512,128]{1,0:T(8,128)(2,1)S(1)} %get-tuple-element.97), channel_id=1, source_target_pairs={{0,1},{1,2},{2,3},{3,0},{4,5},{5,6},{6,7},{7,4},{8,9},{9,10},{10,1... | collective-permute-start | bytes 393224 | tf_op jit(solution)/shard_map/ppermute | solution.py:95
  19.8 6.9 %collective-permute-start.2 = (bf16[512,128]{1,0:T(8,128)(2,1)S(1)}, bf16[512,128]{1,0:T(8,128)(2,1)S(1)}, u32[]{:S(2)}, u32[]{:S(2)}) collective-permute-start(bf16[512,128]{1,0:T(8,128)(2,1)S(1)} %get-tuple-element.97), channel_id=1, source_target_pairs={{0,3},{1,0},{2,1},{3,2},{4,7},{5,4},{6,5},{7,6},{8,11},{9,8},{10,9... | collective-permute-start | bytes 393224 | tf_op jit(solution)/shard_map/ppermute | solution.py:95
  22.6 13.8 %collective-permute-start.11 = (bf16[4,512,128]{2,1,0:T(8,128)(2,1)S(1)}, bf16[4,512,128]{2,1,0:T(8,128)(2,1)S(1)}, u32[]{:S(2)}, u32[]{:S(2)}) collective-permute-start(bf16[4,512,128]{2,1,0:T(8,128)(2,1)S(1)} %pad_maximum_fusion.1.refs_5_), channel_id=1, source_target_pairs={{0,3},{1,0},{2,1},{3,2},{4,7},{5,4},{6,5},{7,6},{8,11},{9,8},{10,9... | collective-permute-start | bytes 1572872 | tf_op jit(solution)/shard_map/ppermute | solution.py:95
  22.9 17.6 %collective-permute-start.10 = (bf16[4,512,128]{2,1,0:T(8,128)(2,1)S(1)}, bf16[4,512,128]{2,1,0:T(8,128)(2,1)S(1)}, u32[]{:S(2)}, u32[]{:S(2)}) collective-permute-start(bf16[4,512,128]{2,1,0:T(8,128)(2,1)S(1)} %pad_maximum_fusion.1.refs_5_), channel_id=1, source_target_pairs={{0,1},{1,2},{2,3},{3,0},{4,5},{5,6},{6,7},{7,4},{8,9},{9,10},{10,1... | collective-permute-start | bytes 1572872 | tf_op jit(solution)/shard_map/ppermute | solution.py:95
  26.8 14.5 %collective-permute-start.4 = (bf16[4,512,128]{2,1,0:T(8,128)(2,1)S(1)}, bf16[4,512,128]{2,1,0:T(8,128)(2,1)S(1)}, u32[]{:S(2)}, u32[]{:S(2)}) collective-permute-start(bf16[4,512,128]{2,1,0:T(8,128)(2,1)S(1)} %pad_maximum_fusion.refs_0_), channel_id=1, source_target_pairs={{0,12},{1,13},{2,14},{3,15},{4,0},{5,1},{6,2},{7,3},{8,4},{9,5},{1... | collective-permute-start | bytes 1572872 | tf_op jit(solution)/shard_map/ppermute | solution.py:99
  27.5 15.9 %collective-permute-start.3 = (bf16[4,512,128]{2,1,0:T(8,128)(2,1)S(1)}, bf16[4,512,128]{2,1,0:T(8,128)(2,1)S(1)}, u32[]{:S(2)}, u32[]{:S(2)}) collective-permute-start(bf16[4,512,128]{2,1,0:T(8,128)(2,1)S(1)} %pad_maximum_fusion.refs_0_), channel_id=1, source_target_pairs={{0,4},{1,5},{2,6},{3,7},{4,8},{5,9},{6,10},{7,11},{8,12},{9,13},{1... | collective-permute-start | bytes 1572872 | tf_op jit(solution)/shard_map/ppermute | solution.py:99
  37.0 8.4 %collective-permute-start.13 = (bf16[2,512,128]{2,1,0:T(8,128)(2,1)}, bf16[2,512,128]{2,1,0:T(8,128)(2,1)S(1)}, u32[]{:S(2)}, u32[]{:S(2)}) collective-permute-start(bf16[2,512,128]{2,1,0:T(8,128)(2,1)} %slice.27), channel_id=1, source_target_pairs={{0,3},{1,0},{2,1},{3,2},{4,7},{5,4},{6,5},{7,6},{8,11},{9,8},{10,9... | collective-permute-start | bytes 786440 | tf_op jit(solution)/shard_map/ppermute | solution.py:95
  41.2 8.1 %collective-permute-start.12 = (bf16[2,512,128]{2,1,0:T(8,128)(2,1)}, bf16[2,512,128]{2,1,0:T(8,128)(2,1)}, u32[]{:S(2)}, u32[]{:S(2)}) collective-permute-start(bf16[2,512,128]{2,1,0:T(8,128)(2,1)} %slice.26), channel_id=1, source_target_pairs={{0,1},{1,2},{2,3},{3,0},{4,5},{5,6},{6,7},{7,4},{8,9},{9,10},{10,1... | collective-permute-start | bytes 786440 | tf_op jit(solution)/shard_map/ppermute | solution.py:95
  42.0 7.4 %collective-permute-start.6 = (bf16[2,512,128]{2,1,0:T(8,128)(2,1)}, bf16[2,512,128]{2,1,0:T(8,128)(2,1)}, u32[]{:S(2)}, u32[]{:S(2)}) collective-permute-start(bf16[2,512,128]{2,1,0:T(8,128)(2,1)} %slice.25), channel_id=1, source_target_pairs={{0,12},{1,13},{2,14},{3,15},{4,0},{5,1},{6,2},{7,3},{8,4},{9,5},{1... | collective-permute-start | bytes 786440 | tf_op jit(solution)/shard_map/ppermute | solution.py:99
  44.1 8.3 %collective-permute-start.5 = (bf16[2,512,128]{2,1,0:T(8,128)(2,1)}, bf16[2,512,128]{2,1,0:T(8,128)(2,1)}, u32[]{:S(2)}, u32[]{:S(2)}) collective-permute-start(bf16[2,512,128]{2,1,0:T(8,128)(2,1)} %slice.24), channel_id=1, source_target_pairs={{0,4},{1,5},{2,6},{3,7},{4,8},{5,9},{6,10},{7,11},{8,12},{9,13},{1... | collective-permute-start | bytes 786440 | tf_op jit(solution)/shard_map/ppermute | solution.py:99
  55.5 2.1 %copy-start.1 = (bf16[1024,2048]{1,0:T(8,128)(2,1)}, bf16[1024,2048]{1,0:T(8,128)(2,1)S(1)}, u32[]{:S(2)}) copy-start(bf16[1024,2048]{1,0:T(8,128)(2,1)S(1)} %get-tuple-element.49.noise_ref) | copy-start | bytes 12582916
  61.9 2.2 %copy-start.2 = (bf16[1024,2048]{1,0:T(8,128)(2,1)S(1)}, bf16[1024,2048]{1,0:T(8,128)(2,1)}, u32[]{:S(2)}) copy-start(bf16[1024,2048]{1,0:T(8,128)(2,1)} %copy-done.1) | copy-start | bytes 12582916
  138.9 12.7 %slice-start = ((s8[8388608]{0:T(1024)(128)(4,1)}), s8[4194304]{0:T(1024)(128)(4,1)S(1)}, s32[]{:S(2)}) async-start(s8[8388608]{0:T(1024)(128)(4,1)} %bitcast.18), calls=%async_computation.7 | async-start | bytes 8388608
  139.9 11.6 %slice-start.1 = ((s8[8388608]{0:T(1024)(128)(4,1)}), s8[4194304]{0:T(1024)(128)(4,1)S(1)}, s32[]{:S(2)}) async-start(s8[8388608]{0:T(1024)(128)(4,1)} %bitcast.18), calls=%async_computation.8 | async-start | bytes 8388608
  154.5 15.4 %collective-permute-start.14 = (bf16[4,272,128]{2,1,0:T(8,128)(2,1)S(1)}, bf16[4,272,128]{2,1,0:T(8,128)(2,1)S(1)}, u32[]{:S(2)}, u32[]{:S(2)}) collective-permute-start(bf16[4,272,128]{2,1,0:T(8,128)(2,1)S(1)} %get-tuple-element.67), channel_id=1, source_target_pairs={{0,1},{1,2},{2,3},{3,0},{4,5},{5,6},{6,7},{7,4},{8,9},{9,10},{10,1... | collective-permute-start | bytes 835592 | tf_op jit(solution)/shard_map/ppermute | solution.py:95
  155.1 14.8 %collective-permute-start.15 = (bf16[4,272,128]{2,1,0:T(8,128)(2,1)S(1)}, bf16[4,272,128]{2,1,0:T(8,128)(2,1)S(1)}, u32[]{:S(2)}, u32[]{:S(2)}) collective-permute-start(bf16[4,272,128]{2,1,0:T(8,128)(2,1)S(1)} %get-tuple-element.68), channel_id=1, source_target_pairs={{0,3},{1,0},{2,1},{3,2},{4,7},{5,4},{6,5},{7,6},{8,11},{9,8},{10,9... | collective-permute-start | bytes 835592 | tf_op jit(solution)/shard_map/ppermute | solution.py:95
  157.8 8.9 %collective-permute-start.16 = (bf16[4,272,128]{2,1,0:T(8,128)(2,1)S(1)}, bf16[4,272,128]{2,1,0:T(8,128)(2,1)S(1)}, u32[]{:S(2)}, u32[]{:S(2)}) collective-permute-start(bf16[4,272,128]{2,1,0:T(8,128)(2,1)S(1)} %get-tuple-element.69), channel_id=1, source_target_pairs={{0,4},{1,5},{2,6},{3,7},{4,8},{5,9},{6,10},{7,11},{8,12},{9,13},{1... | collective-permute-start | bytes 835592 | tf_op jit(solution)/shard_map/ppermute | solution.py:99
  158.3 8.4 %collective-permute-start.17 = (bf16[4,272,128]{2,1,0:T(8,128)(2,1)S(1)}, bf16[4,272,128]{2,1,0:T(8,128)(2,1)S(1)}, u32[]{:S(2)}, u32[]{:S(2)}) collective-permute-start(bf16[4,272,128]{2,1,0:T(8,128)(2,1)S(1)} %get-tuple-element.70), channel_id=1, source_target_pairs={{0,12},{1,13},{2,14},{3,15},{4,0},{5,1},{6,2},{7,3},{8,4},{9,5},{1... | collective-permute-start | bytes 835592 | tf_op jit(solution)/shard_map/ppermute | solution.py:99
  166.8 12.7 %collective-permute-start.24 = (bf16[4,528,128]{2,1,0:T(8,128)(2,1)S(1)}, bf16[4,528,128]{2,1,0:T(8,128)(2,1)S(1)}, u32[]{:S(2)}, u32[]{:S(2)}) collective-permute-start(bf16[4,528,128]{2,1,0:T(8,128)(2,1)S(1)} %get-tuple-element.88), channel_id=1, source_target_pairs={{0,12},{1,13},{2,14},{3,15},{4,0},{5,1},{6,2},{7,3},{8,4},{9,5},{1... | collective-permute-start | bytes 1622024 | tf_op jit(solution)/shard_map/ppermute | solution.py:99
  169.9 13.1 %collective-permute-start.23 = (bf16[4,528,128]{2,1,0:T(8,128)(2,1)S(1)}, bf16[4,528,128]{2,1,0:T(8,128)(2,1)S(1)}, u32[]{:S(2)}, u32[]{:S(2)}) collective-permute-start(bf16[4,528,128]{2,1,0:T(8,128)(2,1)S(1)} %get-tuple-element.79), channel_id=1, source_target_pairs={{0,4},{1,5},{2,6},{3,7},{4,8},{5,9},{6,10},{7,11},{8,12},{9,13},{1... | collective-permute-start | bytes 1622024 | tf_op jit(solution)/shard_map/ppermute | solution.py:99
  169.9 26.7 %copy-start = (bf16[1024,128]{1,0:T(8,128)(2,1)S(1)}, bf16[1024,128]{1,0:T(8,128)(2,1)}, u32[]{:S(2)}) copy-start(bf16[1024,128]{1,0:T(8,128)(2,1)} %noise_ref.1) | copy-start | bytes 786436
  170.0 17.0 %collective-permute-start.19 = (bf16[4,528,128]{2,1,0:T(8,128)(2,1)S(1)}, bf16[4,528,128]{2,1,0:T(8,128)(2,1)S(1)}, u32[]{:S(2)}, u32[]{:S(2)}) collective-permute-start(bf16[4,528,128]{2,1,0:T(8,128)(2,1)S(1)} %get-tuple-element.82), channel_id=1, source_target_pairs={{0,3},{1,0},{2,1},{3,2},{4,7},{5,4},{6,5},{7,6},{8,11},{9,8},{10,9... | collective-permute-start | bytes 1622024 | tf_op jit(solution)/shard_map/ppermute | solution.py:95
  170.4 16.6 %collective-permute-start.18 = (bf16[4,528,128]{2,1,0:T(8,128)(2,1)S(1)}, bf16[4,528,128]{2,1,0:T(8,128)(2,1)S(1)}, u32[]{:S(2)}, u32[]{:S(2)}) collective-permute-start(bf16[4,528,128]{2,1,0:T(8,128)(2,1)S(1)} %get-tuple-element.77), channel_id=1, source_target_pairs={{0,1},{1,2},{2,3},{3,0},{4,5},{5,6},{6,7},{7,4},{8,9},{9,10},{10,1... | collective-permute-start | bytes 1622024 | tf_op jit(solution)/shard_map/ppermute | solution.py:95
  183.7 7.9 %collective-permute-start.25 = (bf16[528,128]{1,0:T(8,128)(2,1)S(1)}, bf16[528,128]{1,0:T(8,128)(2,1)S(1)}, u32[]{:S(2)}, u32[]{:S(2)}) collective-permute-start(bf16[528,128]{1,0:T(8,128)(2,1)S(1)} %get-tuple-element.90), channel_id=1, source_target_pairs={{0,1},{1,2},{2,3},{3,0},{4,5},{5,6},{6,7},{7,4},{8,9},{9,10},{10,1... | collective-permute-start | bytes 405512 | tf_op jit(solution)/shard_map/ppermute | solution.py:95
  183.8 8.4 %collective-permute-start.26 = (bf16[528,128]{1,0:T(8,128)(2,1)S(1)}, bf16[528,128]{1,0:T(8,128)(2,1)S(1)}, u32[]{:S(2)}, u32[]{:S(2)}) collective-permute-start(bf16[528,128]{1,0:T(8,128)(2,1)S(1)} %get-tuple-element.91), channel_id=1, source_target_pairs={{0,2},{1,3},{2,0},{3,1},{4,6},{5,7},{6,4},{7,5},{8,10},{9,11},{10,... | collective-permute-start | bytes 405512 | tf_op jit(solution)/shard_map/ppermute | solution.py:95
  185.8 6.5 %collective-permute-start.27 = (bf16[528,128]{1,0:T(8,128)(2,1)S(1)}, bf16[528,128]{1,0:T(8,128)(2,1)S(1)}, u32[]{:S(2)}, u32[]{:S(2)}) collective-permute-start(bf16[528,128]{1,0:T(8,128)(2,1)S(1)} %get-tuple-element.92), channel_id=1, source_target_pairs={{0,3},{1,0},{2,1},{3,2},{4,7},{5,4},{6,5},{7,6},{8,11},{9,8},{10,9... | collective-permute-start | bytes 405512 | tf_op jit(solution)/shard_map/ppermute | solution.py:95
  187.7 6.3 %collective-permute-start.20 = (bf16[528,128]{1,0:T(8,128)(2,1)S(1)}, bf16[528,128]{1,0:T(8,128)(2,1)S(1)}, u32[]{:S(2)}, u32[]{:S(2)}) collective-permute-start(bf16[528,128]{1,0:T(8,128)(2,1)S(1)} %get-tuple-element.84), channel_id=1, source_target_pairs={{0,4},{1,5},{2,6},{3,7},{4,8},{5,9},{6,10},{7,11},{8,12},{9,13},{1... | collective-permute-start | bytes 405512 | tf_op jit(solution)/shard_map/ppermute | solution.py:99
  187.8 8.2 %collective-permute-start.21 = (bf16[528,128]{1,0:T(8,128)(2,1)S(1)}, bf16[528,128]{1,0:T(8,128)(2,1)S(1)}, u32[]{:S(2)}, u32[]{:S(2)}) collective-permute-start(bf16[528,128]{1,0:T(8,128)(2,1)S(1)} %get-tuple-element.85), channel_id=1, source_target_pairs={{0,8},{1,9},{2,10},{3,11},{4,12},{5,13},{6,14},{7,15},{8,0},{9,1},... | collective-permute-start | bytes 405512 | tf_op jit(solution)/shard_map/ppermute | solution.py:99
  191.6 5.0 %collective-permute-start.22 = (bf16[528,128]{1,0:T(8,128)(2,1)S(1)}, bf16[528,128]{1,0:T(8,128)(2,1)S(1)}, u32[]{:S(2)}, u32[]{:S(2)}) collective-permute-start(bf16[528,128]{1,0:T(8,128)(2,1)S(1)} %get-tuple-element.86), channel_id=1, source_target_pairs={{0,12},{1,13},{2,14},{3,15},{4,0},{5,1},{6,2},{7,3},{8,4},{9,5},{1... | collective-permute-start | bytes 405512 | tf_op jit(solution)/shard_map/ppermute | solution.py:99
Sparse Core Ops, SparseCore 0:
  9.7 52.1 all-gather.2

commit v6 on v5

--- a/solution.py
+++ b/solution.py
@@ -20,7 +20,7 @@
 COLS = 2048
 WIDTH = 2048
 COL_BLOCK = 512
-SCORE_ROWS = 512
+SCORE_ROWS = 1024
 ROW_BLOCK = 256
 HALF = 512
 N_ROW = 8
@@ -145,13 +145,13 @@
         high = jnp.where(inside, noise_end, high)
         noise_at, data_at = noise_end, data_end
     low = low - info_ref[16]
-    high = high - info_ref[16]
+    span = (high - info_ref[16] - low).astype(jnp.uint32)
 
     half = SCORE_ROWS
     for r in range(ROWS // half):
         inner = lax.dot_general(noise_ref[half * r : half * (r + 1), :], data, (((1,), (1,)), ((), ())), preferred_element_type=F32)
         i = half * r + lax.broadcasted_iota(jnp.int32, (half, COL_BLOCK), 0)
-        score = jnp.where((i >= low) & (i < high), inner * (2.0 * KAPPA), MASKED)
+        score = jnp.where((i - low).astype(jnp.uint32) < span, inner * (2.0 * KAPPA), MASKED)
         score_ref[half * r : half * (r + 1), :] = score
         parts = [score[:, 128 * t : 128 * (t + 1)] - KAPPA * data_sq[t] for t in range(COL_BLOCK // 128)]
         at = slice(half * r, half * (r + 1))
@@ -237,7 +237,7 @@
             return tuple(jnp.maximum(carry[t], score_ref[at, 128 * t : 128 * (t + 1)] + shift) for t in range(tiles))
 
         start = tuple(big[:, 128 * t : 128 * (t + 1)] for t in range(tiles))
-        new = lax.fori_loop(0, ROW_BLOCK // GROUP, largest, start, unroll=2)
+        new = lax.fori_loop(0, ROW_BLOCK // GROUP, largest, start, unroll=4)
         for t in range(tiles):
             big[:, 128 * t : 128 * (t + 1)] = new[t]
 
@@ -261,7 +261,7 @@
             return tuple(out)
 
         start = tuple(total[:, 128 * t : 128 * (t + 1)] for t in range(tiles))
-        summed = lax.fori_loop(0, ROW_BLOCK // GROUP, add, start, unroll=2)
+        summed = lax.fori_loop(0, ROW_BLOCK // GROUP, add, start, unroll=4)
         for t in range(tiles):
             total[:, 128 * t : 128 * (t + 1)] = summed[t]
 
@@ -446,7 +446,7 @@
             sums[at, :] = summed
             return 0
 
-        lax.fori_loop(0, ROW_BLOCK // 16, body, 0, unroll=2)
+        lax.fori_loop(0, ROW_BLOCK // 16, body, 0, unroll=4)
 
     @pl.when(step < 2)
     def _():

time: 205 us -> 204 us (level)
  no operation moved by 1% of the time
where the time goes in v6:
time: 204 us
  blocking collectives  61 us (30%)
  starting transfers between devices  42.7 us (21%)
  Pallas kernels  42.5 us (21%)
  waiting for transfers between devices  34.4 us (17%)
  between operations  14.2 us (7%)
  local copies, waits for them, and re-layouts  8.92 us (4%)
    all_to_all x6, blocking collectives, swap(): return lax.all_to_all(x, axis, 0, 0, tiled=True)  61 us
    ppermute x14, starting transfers between devices, over_z(): lax.ppermute(v, 'col', [(4 * z + x, 4 * ((z + d) % 4) + x) for z in range...  22.1 us
    ppermute x14, starting transfers between devices, over_x(): lax.ppermute(v, 'col', [(4 * z + x, 4 * z + (x + d) % 4) for z in range(4...  20.5 us
    ppermute x14, waiting for transfers between devices, over_z(): lax.ppermute(v, 'col', [(4 * z + x, 4 * ((z + d) % 4) + x) for z in range...  15.8 us
    pallas_call x1, Pallas kernels, scores(): pl.pallas_call(score_kernel, grid=(COLS // COL_BLOCK,), in_specs=[pl.Bloc...  14.1 us
    ppermute x14, waiting for transfers between devices, over_x(): lax.ppermute(v, 'col', [(4 * z + x, 4 * z + (x + d) % 4) for z in range(4...  13.5 us
    pallas_call x6, Pallas kernels, pass_call(): pl.pallas_call(kernel, grid=(sweeps * (ROWS // ROW_BLOCK),), in_specs=in_...  11.6 us
    pallas_call x3, Pallas kernels, messages(): pl.pallas_call(functools.partial(target_kernel, ways), in_specs=[pl.Block...  11 us
  transfers between devices with their start and end apart: 29, of which 13 were waited for; matrix products, arithmetic and copies ran while one was open for 2% of the time, Pallas kernels for 6%

profile of v6, /device:TPU:0, one launch (start us, length us, event | category | flops | bytes accessed | tf_op | source)
XLA Modules:
  0.0 203.9 jit_solution(18143749197221670366)
XLA Ops:
  7.9 1.0 slice_bitcast_fusion
  8.9 4.0 %collective-permute-start.8 = (bf16[512,128]{1,0:T(8,128)(2,1)S(1)}, bf16[512,128]{1,0:T(8,128)(2,1)S(1)}, u32[]{:S(2)}, u32[]{:S(2)}) collective-permute-start(bf16[512,128]{1,0:T(8,128)(2,1)S(1)} %get-tuple-element.98), channel_id=1, source_target_pairs={{0,8},{1,9},{2,10},{3,11},{4,12},{5,13},{6,14},{7,15},{8,0},{9,1},... | collective-permute-start | bytes 393224 | tf_op jit(solution)/shard_map/ppermute | solution.py:99
  13.0 1.0 collective-permute-start.7
  14.0 2.2 %collective-permute-start.9 = (bf16[512,128]{1,0:T(8,128)(2,1)S(1)}, bf16[512,128]{1,0:T(8,128)(2,1)S(1)}, u32[]{:S(2)}, u32[]{:S(2)}) collective-permute-start(bf16[512,128]{1,0:T(8,128)(2,1)S(1)} %get-tuple-element.98), channel_id=1, source_target_pairs={{0,12},{1,13},{2,14},{3,15},{4,0},{5,1},{6,2},{7,3},{8,4},{9,5},{1... | collective-permute-start | bytes 393224 | tf_op jit(solution)/shard_map/ppermute | solution.py:99
  16.2 3.0 %collective-permute-start.1 = (bf16[512,128]{1,0:T(8,128)(2,1)S(1)}, bf16[512,128]{1,0:T(8,128)(2,1)S(1)}, u32[]{:S(2)}, u32[]{:S(2)}) collective-permute-start(bf16[512,128]{1,0:T(8,128)(2,1)S(1)} %get-tuple-element.97), channel_id=1, source_target_pairs={{0,2},{1,3},{2,0},{3,1},{4,6},{5,7},{6,4},{7,5},{8,10},{9,11},{10,... | collective-permute-start | bytes 393224 | tf_op jit(solution)/shard_map/ppermute | solution.py:95
  19.8 2.6 %collective-permute-start.2 = (bf16[512,128]{1,0:T(8,128)(2,1)S(1)}, bf16[512,128]{1,0:T(8,128)(2,1)S(1)}, u32[]{:S(2)}, u32[]{:S(2)}) collective-permute-start(bf16[512,128]{1,0:T(8,128)(2,1)S(1)} %get-tuple-element.97), channel_id=1, source_target_pairs={{0,3},{1,0},{2,1},{3,2},{4,7},{5,4},{6,5},{7,6},{8,11},{9,8},{10,9... | collective-permute-start | bytes 393224 | tf_op jit(solution)/shard_map/ppermute | solution.py:95
  22.9 1.7 collective-permute-start.10
  24.7 1.3 collective-permute-done
  27.5 1.4 collective-permute-start.3
  28.9 7.4 %collective-permute-done.11.refs_7_ = bf16[4,512,128]{2,1,0:T(8,128)(2,1)S(1)} collective-permute-done((bf16[4,512,128]{2,1,0:T(8,128)(2,1)S(1)}, bf16[4,512,128]{2,1,0:T(8,128)(2,1)S(1)}, u32[]{:S(2)}, u32[]{:S(2)}) %collective-permute-start.11) | collective-permute-done | bytes 524320 | tf_op jit(solution)/shard_map/ppermute | solution.py:95
  37.0 3.5 %collective-permute-start.13 = (bf16[2,512,128]{2,1,0:T(8,128)(2,1)}, bf16[2,512,128]{2,1,0:T(8,128)(2,1)S(1)}, u32[]{:S(2)}, u32[]{:S(2)}) collective-permute-start(bf16[2,512,128]{2,1,0:T(8,128)(2,1)} %slice.27), channel_id=1, source_target_pairs={{0,3},{1,0},{2,1},{3,2},{4,7},{5,4},{6,5},{7,6},{8,11},{9,8},{10,9... | collective-permute-start | bytes 786440 | tf_op jit(solution)/shard_map/ppermute | solution.py:95
  42.0 1.4 collective-permute-start.6
  44.7 0.7 concatenate.3.info_ref
  45.5 3.9 %collective-permute-done.12.refs_8_ = bf16[2,512,128]{2,1,0:T(8,128)(2,1)} collective-permute-done((bf16[2,512,128]{2,1,0:T(8,128)(2,1)}, bf16[2,512,128]{2,1,0:T(8,128)(2,1)}, u32[]{:S(2)}, u32[]{:S(2)}) %collective-permute-start.12) | collective-permute-done | bytes 262176 | tf_op jit(solution)/shard_map/ppermute | solution.py:95
  49.3 3.0 %collective-permute-done.5.refs_3_ = bf16[2,512,128]{2,1,0:T(8,128)(2,1)} collective-permute-done((bf16[2,512,128]{2,1,0:T(8,128)(2,1)}, bf16[2,512,128]{2,1,0:T(8,128)(2,1)}, u32[]{:S(2)}, u32[]{:S(2)}) %collective-permute-start.5) | collective-permute-done | bytes 262176 | tf_op jit(solution)/shard_map/ppermute | solution.py:99
  52.4 3.1 %arrange.1 = (bf16[1024,2048]{1,0:T(8,128)(2,1)S(1)}, f32[8,128]{1,0:T(8,128)S(1)}) custom-call(s32[20]{0:T(128)S(1)} %concatenate.3.info_ref, bf16[4,512,128]{2,1,0:T(8,128)(2,1)S(1)} %pad_maximum_fusion.refs_0_, bf16[4,512,128]{2,1,0:T(8,128)(2,1)S(1)} %collective-permute-done.3.refs_1_, bf16[4,512,128]{2,1,0:T(8,128)(2,1)S(1)} %collective-permute-done.4.refs_2_, ...), custom_call_target="tpu_custom_call" | custom-call | flops 4194304 | bytes 8388608 | tf_op jit(solution)/shard_map/arrange/pallas_call | solution.py:84
  55.5 2.0 %copy-done.1 = bf16[1024,2048]{1,0:T(8,128)(2,1)} copy-done((bf16[1024,2048]{1,0:T(8,128)(2,1)}, bf16[1024,2048]{1,0:T(8,128)(2,1)S(1)}, u32[]{:S(2)}) %copy-start.1) | copy-done | bytes 4194328
  57.6 4.4 %all-gather.3.cloned.1.call-done = bf16[16384,256]{1,0:T(8,128)(2,1)} async-done(((bf16[2048,256]{1,0:T(8,128)(2,1)}), bf16[16384,256]{1,0:T(8,128)(2,1)}) %all-gather.3.cloned.1.call-update) | async-done | bytes 8388624 | tf_op jit(solution)/shard_map/all_gather | solution.py:629
  61.9 2.2 %copy-done.2 = bf16[1024,2048]{1,0:T(8,128)(2,1)S(1)} copy-done((bf16[1024,2048]{1,0:T(8,128)(2,1)S(1)}, bf16[1024,2048]{1,0:T(8,128)(2,1)}, u32[]{:S(2)}) %copy-start.2) | copy-done | bytes 4194328
  64.1 14.1 %scores.1 = (f32[1024,2048]{1,0:T(8,128)S(1)}, f32[16,8,128]{2,1,0:T(8,128)S(1)}, f32[4,4,128]{2,1,0:T(4,128)S(1)}) custom-call(s32[20]{0:T(128)S(1)} %concatenate.3.info_ref, bf16[1024,2048]{1,0:T(8,128)(2,1)S(1)} %copy-done.2, bf16[8,2048,256]{2,1,0:T(8,128)(2,1)} %bitcast.17), custom_call_target="tpu_custom_call" | custom-call | flops 8589934592 | bytes 20971520 | tf_op jit(solution)/shard_map/scores/pallas_call | solution.py:179
  78.2 14.4 %all_to_all.30.parts_ref = f32[16,8,128]{2,1,0:T(8,128)S(1)} all-to-all(f32[16,8,128]{2,1,0:T(8,128)S(1)} %get-tuple-element.50), channel_id=1, replica_groups=mesh['row'=8,'col'=16] {'col'}, dimensions={0} | all-to-all | bytes 131072 | tf_op jit(solution)/shard_map/all_to_all | solution.py:622
  92.7 3.1 %first_columns.1 = (f32[8,16,128]{2,1,0:T(8,128)S(1)}, f32[8,128]{1,0:T(8,128)S(1)}, f32[1024,2048]{1,0:T(8,128)S(1)}, f32[16,128]{1,0:T(8,128)S(1)}) custom-call(f32[16,8,128]{2,1,0:T(8,128)S(1)} %all_to_all.30.parts_ref, f32[1024,2048]{1,0:T(8,128)S(1)} %get-tuple-element.51.score_ref), custom_call_target="tpu_custom_call" | custom-call | flops 8388608 | bytes 8388608 | tf_op jit(solution)/shard_map/first_columns/pallas_call | solution.py:277
  95.8 8.6 %all_to_all.31.parts_ref = f32[8,16,128]{2,1,0:T(8,128)S(1)} all-to-all(f32[8,16,128]{2,1,0:T(8,128)S(1)} %get-tuple-element.52), channel_id=1, replica_groups=mesh['row'=8,'col'=16] {'row'}, dimensions={0} | all-to-all | bytes 131072 | tf_op jit(solution)/shard_map/all_to_all | solution.py:622
  104.4 1.3 row_sums.2
  105.6 10.8 %all_to_all.32.parts_ref = f32[16,8,128]{2,1,0:T(8,128)S(1)} all-to-all(f32[16,8,128]{2,1,0:T(8,128)S(1)} %get-tuple-element.55), channel_id=1, replica_groups=mesh['row'=8,'col'=16] {'col'}, dimensions={0} | all-to-all | bytes 131072 | tf_op jit(solution)/shard_map/all_to_all | solution.py:622
  116.4 1.6 column_sums.2
  118.1 8.0 %all_to_all.33.parts_ref = f32[8,16,128]{2,1,0:T(8,128)S(1)} all-to-all(f32[8,16,128]{2,1,0:T(8,128)S(1)} %get-tuple-element.57), channel_id=1, replica_groups=mesh['row'=8,'col'=16] {'row'}, dimensions={0} | all-to-all | bytes 131072 | tf_op jit(solution)/shard_map/all_to_all | solution.py:622
  126.1 1.2 row_sums.3
  127.3 10.8 %all_to_all.34.parts_ref = f32[16,8,128]{2,1,0:T(8,128)S(1)} all-to-all(f32[16,8,128]{2,1,0:T(8,128)S(1)} %row_sums.3), channel_id=1, replica_groups=mesh['row'=8,'col'=16] {'col'}, dimensions={0} | all-to-all | bytes 131072 | tf_op jit(solution)/shard_map/all_to_all | solution.py:622
  138.1 1.0 column_sums.3
  139.2 8.4 %all_to_all.35.parts_ref = f32[8,16,128]{2,1,0:T(8,128)S(1)} all-to-all(f32[8,16,128]{2,1,0:T(8,128)S(1)} %get-tuple-element.58), channel_id=1, replica_groups=mesh['row'=8,'col'=16] {'row'}, dimensions={0} | all-to-all | bytes 131072 | tf_op jit(solution)/shard_map/all_to_all | solution.py:622
  147.6 3.3 %coupling.1 = (bf16[512,2048]{1,0:T(8,128)(2,1)S(1)}, bf16[512,2048]{1,0:T(8,128)(2,1)S(1)}, f32[8,128]{1,0:T(8,128)S(1)}, f32[8,128]{1,0:T(8,128)}, f32[16,128]{1,0:T(8,128)}) custom-call(f32[8,16,128]{2,1,0:T(8,128)S(1)} %all_to_all.35.parts_ref, f32[8,128]{1,0:T(8,128)S(1)} %get-tuple-element.59.scale_ref, f32[8,128]{1,0:T(8,128)S(1)} %get-tuple-element.60.noise_first, ...), custom_call_target="tpu_custom_call" | custom-call | flops 8388608 | bytes 8388608 | tf_op jit(solution)/shard_map/coupling/pallas_call | solution.py:277
  150.9 2.9 %targets.3 = (bf16[4,272,128]{2,1,0:T(8,128)(2,1)S(1)}, bf16[4,272,128]{2,1,0:T(8,128)(2,1)S(1)}, bf16[4,272,128]{2,1,0:T(8,128)(2,1)S(1)}, bf16[4,272,128]{2,1,0:T(8,128)(2,1)S(1)}) custom-call(s32[20]{0:T(128)S(1)} %concatenate.3.info_ref, bf16[512,2048]{1,0:T(8,128)(2,1)S(1)} %get-tuple-element.64.pa_ref, bf16[512,2048]{1,0:T(8,128)(2,1)S(1)} %get-tuple-element.65.pb_ref, ...), custom_call_target="tpu_custom_call" | custom-call | flops 2147483648 | bytes 8388608 | tf_op jit(solution)/shard_map/targets/pallas_call | solution.py:528
  154.5 2.7 %collective-permute-start.15 = (bf16[4,272,128]{2,1,0:T(8,128)(2,1)S(1)}, bf16[4,272,128]{2,1,0:T(8,128)(2,1)S(1)}, u32[]{:S(2)}, u32[]{:S(2)}) collective-permute-start(bf16[4,272,128]{2,1,0:T(8,128)(2,1)S(1)} %get-tuple-element.68), channel_id=1, source_target_pairs={{0,3},{1,0},{2,1},{3,2},{4,7},{5,4},{6,5},{7,6},{8,11},{9,8},{10,9... | collective-permute-start | bytes 835592 | tf_op jit(solution)/shard_map/ppermute | solution.py:95
  157.7 2.7 %collective-permute-start.17 = (bf16[4,272,128]{2,1,0:T(8,128)(2,1)S(1)}, bf16[4,272,128]{2,1,0:T(8,128)(2,1)S(1)}, u32[]{:S(2)}, u32[]{:S(2)}) collective-permute-start(bf16[4,272,128]{2,1,0:T(8,128)(2,1)S(1)} %get-tuple-element.70), channel_id=1, source_target_pairs={{0,12},{1,13},{2,14},{3,15},{4,0},{5,1},{6,2},{7,3},{8,4},{9,5},{1... | collective-permute-start | bytes 835592 | tf_op jit(solution)/shard_map/ppermute | solution.py:99
  160.4 5.1 %targets.4 = (bf16[4,528,128]{2,1,0:T(8,128)(2,1)S(1)}, bf16[4,528,128]{2,1,0:T(8,128)(2,1)S(1)}, bf16[4,528,128]{2,1,0:T(8,128)(2,1)S(1)}, bf16[4,528,128]{2,1,0:T(8,128)(2,1)S(1)}) custom-call(s32[20]{0:T(128)S(1)} %concatenate.3.info_ref, bf16[512,2048]{1,0:T(8,128)(2,1)S(1)} %get-tuple-element.64.pa_ref, bf16[512,2048]{1,0:T(8,128)(2,1)S(1)} %get-tuple-element.65.pb_ref, ...), custom_call_target="tpu_custom_call" | custom-call | flops 4294967296 | bytes 8388608 | tf_op jit(solution)/shard_map/targets/pallas_call | solution.py:528
  166.3 3.0 %collective-permute-start.24 = (bf16[4,528,128]{2,1,0:T(8,128)(2,1)S(1)}, bf16[4,528,128]{2,1,0:T(8,128)(2,1)S(1)}, u32[]{:S(2)}, u32[]{:S(2)}) collective-permute-start(bf16[4,528,128]{2,1,0:T(8,128)(2,1)S(1)} %get-tuple-element.88), channel_id=1, source_target_pairs={{0,12},{1,13},{2,14},{3,15},{4,0},{5,1},{6,2},{7,3},{8,4},{9,5},{1... | collective-permute-start | bytes 1622024 | tf_op jit(solution)/shard_map/ppermute | solution.py:99
  169.8 1.7 collective-permute-start.18
  171.5 2.9 %targets.5 = (bf16[4,528,128]{2,1,0:T(8,128)(2,1)S(1)}, bf16[4,528,128]{2,1,0:T(8,128)(2,1)S(1)}) custom-call(s32[20]{0:T(128)S(1)} %concatenate.3.info_ref, bf16[512,2048]{1,0:T(8,128)(2,1)S(1)} %get-tuple-element.64.pa_ref, bf16[512,2048]{1,0:T(8,128)(2,1)S(1)} %get-tuple-element.65.pb_ref, f32[8,128]{1,0:T(8,128)S(1)} %get-tuple-element.80.sums_ref, ...), custom_call_target="tpu_custom_call" | custom-call | flops 2147483648 | bytes 8388608 | tf_op jit(solution)/shard_map/targets/pallas_call | solution.py:528
  174.5 4.5 %collective-permute-done.24.right = bf16[4,528,128]{2,1,0:T(8,128)(2,1)S(1)} collective-permute-done((bf16[4,528,128]{2,1,0:T(8,128)(2,1)S(1)}, bf16[4,528,128]{2,1,0:T(8,128)(2,1)S(1)}, u32[]{:S(2)}, u32[]{:S(2)}) %collective-permute-start.24) | collective-permute-done | bytes 540704 | tf_op jit(solution)/shard_map/ppermute | solution.py:99
  178.9 3.4 %collective-permute-done.23.left = bf16[4,528,128]{2,1,0:T(8,128)(2,1)S(1)} collective-permute-done((bf16[4,528,128]{2,1,0:T(8,128)(2,1)S(1)}, bf16[4,528,128]{2,1,0:T(8,128)(2,1)S(1)}, u32[]{:S(2)}, u32[]{:S(2)}) %collective-permute-start.23) | collective-permute-done | bytes 540704 | tf_op jit(solution)/shard_map/ppermute | solution.py:99
  183.2 2.0 collective-permute-start.26
  185.2 1.2 collective-permute-start.27
  186.4 0.7 combine.2
  187.2 3.7 %collective-permute-start.21 = (bf16[528,128]{1,0:T(8,128)(2,1)S(1)}, bf16[528,128]{1,0:T(8,128)(2,1)S(1)}, u32[]{:S(2)}, u32[]{:S(2)}) collective-permute-start(bf16[528,128]{1,0:T(8,128)(2,1)S(1)} %get-tuple-element.85), channel_id=1, source_target_pairs={{0,8},{1,9},{2,10},{3,11},{4,12},{5,13},{6,14},{7,15},{8,0},{9,1},... | collective-permute-start | bytes 405512 | tf_op jit(solution)/shard_map/ppermute | solution.py:99
  191.7 1.7 collective-permute-done.20.refs_1_
  193.4 2.0 collective-permute-done.21.refs_2_
  196.0 1.0 finish.1
  (52 shorter events, 11.4 us)
Async XLA Ops:
  7.2 54.8 %all-gather.3.cloned.1.call-start = ((), (), s32[]{:S(2)}) async-start(), calls=%async_computation.6 | async-start | bytes 9437184 | tf_op jit(solution)/shard_map/all_gather | solution.py:629
  8.9 10.9 %collective-permute-start.8 = (bf16[512,128]{1,0:T(8,128)(2,1)S(1)}, bf16[512,128]{1,0:T(8,128)(2,1)S(1)}, u32[]{:S(2)}, u32[]{:S(2)}) collective-permute-start(bf16[512,128]{1,0:T(8,128)(2,1)S(1)} %get-tuple-element.98), channel_id=1, source_target_pairs={{0,8},{1,9},{2,10},{3,11},{4,12},{5,13},{6,14},{7,15},{8,0},{9,1},... | collective-permute-start | bytes 393224 | tf_op jit(solution)/shard_map/ppermute | solution.py:99
  13.0 9.5 %collective-permute-start.7 = (bf16[512,128]{1,0:T(8,128)(2,1)S(1)}, bf16[512,128]{1,0:T(8,128)(2,1)S(1)}, u32[]{:S(2)}, u32[]{:S(2)}) collective-permute-start(bf16[512,128]{1,0:T(8,128)(2,1)S(1)} %get-tuple-element.98), channel_id=1, source_target_pairs={{0,4},{1,5},{2,6},{3,7},{4,8},{5,9},{6,10},{7,11},{8,12},{9,13},{1... | collective-permute-start | bytes 393224 | tf_op jit(solution)/shard_map/ppermute | solution.py:99
  14.0 8.5 %collective-permute-start.9 = (bf16[512,128]{1,0:T(8,128)(2,1)S(1)}, bf16[512,128]{1,0:T(8,128)(2,1)S(1)}, u32[]{:S(2)}, u32[]{:S(2)}) collective-permute-start(bf16[512,128]{1,0:T(8,128)(2,1)S(1)} %get-tuple-element.98), channel_id=1, source_target_pairs={{0,12},{1,13},{2,14},{3,15},{4,0},{5,1},{6,2},{7,3},{8,4},{9,5},{1... | collective-permute-start | bytes 393224 | tf_op jit(solution)/shard_map/ppermute | solution.py:99
  16.2 8.4 %collective-permute-start.1 = (bf16[512,128]{1,0:T(8,128)(2,1)S(1)}, bf16[512,128]{1,0:T(8,128)(2,1)S(1)}, u32[]{:S(2)}, u32[]{:S(2)}) collective-permute-start(bf16[512,128]{1,0:T(8,128)(2,1)S(1)} %get-tuple-element.97), channel_id=1, source_target_pairs={{0,2},{1,3},{2,0},{3,1},{4,6},{5,7},{6,4},{7,5},{8,10},{9,11},{10,... | collective-permute-start | bytes 393224 | tf_op jit(solution)/shard_map/ppermute | solution.py:95
  19.2 6.8 %collective-permute-start = (bf16[512,128]{1,0:T(8,128)(2,1)S(1)}, bf16[512,128]{1,0:T(8,128)(2,1)S(1)}, u32[]{:S(2)}, u32[]{:S(2)}) collective-permute-start(bf16[512,128]{1,0:T(8,128)(2,1)S(1)} %get-tuple-element.97), channel_id=1, source_target_pairs={{0,1},{1,2},{2,3},{3,0},{4,5},{5,6},{6,7},{7,4},{8,9},{9,10},{10,1... | collective-permute-start | bytes 393224 | tf_op jit(solution)/shard_map/ppermute | solution.py:95
  19.8 6.9 %collective-permute-start.2 = (bf16[512,128]{1,0:T(8,128)(2,1)S(1)}, bf16[512,128]{1,0:T(8,128)(2,1)S(1)}, u32[]{:S(2)}, u32[]{:S(2)}) collective-permute-start(bf16[512,128]{1,0:T(8,128)(2,1)S(1)} %get-tuple-element.97), channel_id=1, source_target_pairs={{0,3},{1,0},{2,1},{3,2},{4,7},{5,4},{6,5},{7,6},{8,11},{9,8},{10,9... | collective-permute-start | bytes 393224 | tf_op jit(solution)/shard_map/ppermute | solution.py:95
  22.6 13.8 %collective-permute-start.11 = (bf16[4,512,128]{2,1,0:T(8,128)(2,1)S(1)}, bf16[4,512,128]{2,1,0:T(8,128)(2,1)S(1)}, u32[]{:S(2)}, u32[]{:S(2)}) collective-permute-start(bf16[4,512,128]{2,1,0:T(8,128)(2,1)S(1)} %pad_maximum_fusion.1.refs_5_), channel_id=1, source_target_pairs={{0,3},{1,0},{2,1},{3,2},{4,7},{5,4},{6,5},{7,6},{8,11},{9,8},{10,9... | collective-permute-start | bytes 1572872 | tf_op jit(solution)/shard_map/ppermute | solution.py:95
  22.9 17.6 %collective-permute-start.10 = (bf16[4,512,128]{2,1,0:T(8,128)(2,1)S(1)}, bf16[4,512,128]{2,1,0:T(8,128)(2,1)S(1)}, u32[]{:S(2)}, u32[]{:S(2)}) collective-permute-start(bf16[4,512,128]{2,1,0:T(8,128)(2,1)S(1)} %pad_maximum_fusion.1.refs_5_), channel_id=1, source_target_pairs={{0,1},{1,2},{2,3},{3,0},{4,5},{5,6},{6,7},{7,4},{8,9},{9,10},{10,1... | collective-permute-start | bytes 1572872 | tf_op jit(solution)/shard_map/ppermute | solution.py:95
  26.8 14.5 %collective-permute-start.4 = (bf16[4,512,128]{2,1,0:T(8,128)(2,1)S(1)}, bf16[4,512,128]{2,1,0:T(8,128)(2,1)S(1)}, u32[]{:S(2)}, u32[]{:S(2)}) collective-permute-start(bf16[4,512,128]{2,1,0:T(8,128)(2,1)S(1)} %pad_maximum_fusion.refs_0_), channel_id=1, source_target_pairs={{0,12},{1,13},{2,14},{3,15},{4,0},{5,1},{6,2},{7,3},{8,4},{9,5},{1... | collective-permute-start | bytes 1572872 | tf_op jit(solution)/shard_map/ppermute | solution.py:99
  27.5 15.9 %collective-permute-start.3 = (bf16[4,512,128]{2,1,0:T(8,128)(2,1)S(1)}, bf16[4,512,128]{2,1,0:T(8,128)(2,1)S(1)}, u32[]{:S(2)}, u32[]{:S(2)}) collective-permute-start(bf16[4,512,128]{2,1,0:T(8,128)(2,1)S(1)} %pad_maximum_fusion.refs_0_), channel_id=1, source_target_pairs={{0,4},{1,5},{2,6},{3,7},{4,8},{5,9},{6,10},{7,11},{8,12},{9,13},{1... | collective-permute-start | bytes 1572872 | tf_op jit(solution)/shard_map/ppermute | solution.py:99
  37.0 8.4 %collective-permute-start.13 = (bf16[2,512,128]{2,1,0:T(8,128)(2,1)}, bf16[2,512,128]{2,1,0:T(8,128)(2,1)S(1)}, u32[]{:S(2)}, u32[]{:S(2)}) collective-permute-start(bf16[2,512,128]{2,1,0:T(8,128)(2,1)} %slice.27), channel_id=1, source_target_pairs={{0,3},{1,0},{2,1},{3,2},{4,7},{5,4},{6,5},{7,6},{8,11},{9,8},{10,9... | collective-permute-start | bytes 786440 | tf_op jit(solution)/shard_map/ppermute | solution.py:95
  41.2 8.1 %collective-permute-start.12 = (bf16[2,512,128]{2,1,0:T(8,128)(2,1)}, bf16[2,512,128]{2,1,0:T(8,128)(2,1)}, u32[]{:S(2)}, u32[]{:S(2)}) collective-permute-start(bf16[2,512,128]{2,1,0:T(8,128)(2,1)} %slice.26), channel_id=1, source_target_pairs={{0,1},{1,2},{2,3},{3,0},{4,5},{5,6},{6,7},{7,4},{8,9},{9,10},{10,1... | collective-permute-start | bytes 786440 | tf_op jit(solution)/shard_map/ppermute | solution.py:95
  42.0 7.4 %collective-permute-start.6 = (bf16[2,512,128]{2,1,0:T(8,128)(2,1)}, bf16[2,512,128]{2,1,0:T(8,128)(2,1)}, u32[]{:S(2)}, u32[]{:S(2)}) collective-permute-start(bf16[2,512,128]{2,1,0:T(8,128)(2,1)} %slice.25), channel_id=1, source_target_pairs={{0,12},{1,13},{2,14},{3,15},{4,0},{5,1},{6,2},{7,3},{8,4},{9,5},{1... | collective-permute-start | bytes 786440 | tf_op jit(solution)/shard_map/ppermute | solution.py:99
  44.1 8.3 %collective-permute-start.5 = (bf16[2,512,128]{2,1,0:T(8,128)(2,1)}, bf16[2,512,128]{2,1,0:T(8,128)(2,1)}, u32[]{:S(2)}, u32[]{:S(2)}) collective-permute-start(bf16[2,512,128]{2,1,0:T(8,128)(2,1)} %slice.24), channel_id=1, source_target_pairs={{0,4},{1,5},{2,6},{3,7},{4,8},{5,9},{6,10},{7,11},{8,12},{9,13},{1... | collective-permute-start | bytes 786440 | tf_op jit(solution)/shard_map/ppermute | solution.py:99
  55.5 2.1 %copy-start.1 = (bf16[1024,2048]{1,0:T(8,128)(2,1)}, bf16[1024,2048]{1,0:T(8,128)(2,1)S(1)}, u32[]{:S(2)}) copy-start(bf16[1024,2048]{1,0:T(8,128)(2,1)S(1)} %get-tuple-element.49.noise_ref) | copy-start | bytes 12582916
  61.9 2.2 %copy-start.2 = (bf16[1024,2048]{1,0:T(8,128)(2,1)S(1)}, bf16[1024,2048]{1,0:T(8,128)(2,1)}, u32[]{:S(2)}) copy-start(bf16[1024,2048]{1,0:T(8,128)(2,1)} %copy-done.1) | copy-start | bytes 12582916
  138.1 12.8 %slice-start = ((s8[8388608]{0:T(1024)(128)(4,1)}), s8[4194304]{0:T(1024)(128)(4,1)S(1)}, s32[]{:S(2)}) async-start(s8[8388608]{0:T(1024)(128)(4,1)} %bitcast.18), calls=%async_computation.7 | async-start | bytes 8388608
  139.2 11.8 %slice-start.1 = ((s8[8388608]{0:T(1024)(128)(4,1)}), s8[4194304]{0:T(1024)(128)(4,1)S(1)}, s32[]{:S(2)}) async-start(s8[8388608]{0:T(1024)(128)(4,1)} %bitcast.18), calls=%async_computation.8 | async-start | bytes 8388608
  153.9 15.4 %collective-permute-start.14 = (bf16[4,272,128]{2,1,0:T(8,128)(2,1)S(1)}, bf16[4,272,128]{2,1,0:T(8,128)(2,1)S(1)}, u32[]{:S(2)}, u32[]{:S(2)}) collective-permute-start(bf16[4,272,128]{2,1,0:T(8,128)(2,1)S(1)} %get-tuple-element.67), channel_id=1, source_target_pairs={{0,1},{1,2},{2,3},{3,0},{4,5},{5,6},{6,7},{7,4},{8,9},{9,10},{10,1... | collective-permute-start | bytes 835592 | tf_op jit(solution)/shard_map/ppermute | solution.py:95
  154.5 14.8 %collective-permute-start.15 = (bf16[4,272,128]{2,1,0:T(8,128)(2,1)S(1)}, bf16[4,272,128]{2,1,0:T(8,128)(2,1)S(1)}, u32[]{:S(2)}, u32[]{:S(2)}) collective-permute-start(bf16[4,272,128]{2,1,0:T(8,128)(2,1)S(1)} %get-tuple-element.68), channel_id=1, source_target_pairs={{0,3},{1,0},{2,1},{3,2},{4,7},{5,4},{6,5},{7,6},{8,11},{9,8},{10,9... | collective-permute-start | bytes 835592 | tf_op jit(solution)/shard_map/ppermute | solution.py:95
  157.2 8.9 %collective-permute-start.16 = (bf16[4,272,128]{2,1,0:T(8,128)(2,1)S(1)}, bf16[4,272,128]{2,1,0:T(8,128)(2,1)S(1)}, u32[]{:S(2)}, u32[]{:S(2)}) collective-permute-start(bf16[4,272,128]{2,1,0:T(8,128)(2,1)S(1)} %get-tuple-element.69), channel_id=1, source_target_pairs={{0,4},{1,5},{2,6},{3,7},{4,8},{5,9},{6,10},{7,11},{8,12},{9,13},{1... | collective-permute-start | bytes 835592 | tf_op jit(solution)/shard_map/ppermute | solution.py:99
  157.7 8.4 %collective-permute-start.17 = (bf16[4,272,128]{2,1,0:T(8,128)(2,1)S(1)}, bf16[4,272,128]{2,1,0:T(8,128)(2,1)S(1)}, u32[]{:S(2)}, u32[]{:S(2)}) collective-permute-start(bf16[4,272,128]{2,1,0:T(8,128)(2,1)S(1)} %get-tuple-element.70), channel_id=1, source_target_pairs={{0,12},{1,13},{2,14},{3,15},{4,0},{5,1},{6,2},{7,3},{8,4},{9,5},{1... | collective-permute-start | bytes 835592 | tf_op jit(solution)/shard_map/ppermute | solution.py:99
  166.3 12.7 %collective-permute-start.24 = (bf16[4,528,128]{2,1,0:T(8,128)(2,1)S(1)}, bf16[4,528,128]{2,1,0:T(8,128)(2,1)S(1)}, u32[]{:S(2)}, u32[]{:S(2)}) collective-permute-start(bf16[4,528,128]{2,1,0:T(8,128)(2,1)S(1)} %get-tuple-element.88), channel_id=1, source_target_pairs={{0,12},{1,13},{2,14},{3,15},{4,0},{5,1},{6,2},{7,3},{8,4},{9,5},{1... | collective-permute-start | bytes 1622024 | tf_op jit(solution)/shard_map/ppermute | solution.py:99
  169.3 13.1 %collective-permute-start.23 = (bf16[4,528,128]{2,1,0:T(8,128)(2,1)S(1)}, bf16[4,528,128]{2,1,0:T(8,128)(2,1)S(1)}, u32[]{:S(2)}, u32[]{:S(2)}) collective-permute-start(bf16[4,528,128]{2,1,0:T(8,128)(2,1)S(1)} %get-tuple-element.79), channel_id=1, source_target_pairs={{0,4},{1,5},{2,6},{3,7},{4,8},{5,9},{6,10},{7,11},{8,12},{9,13},{1... | collective-permute-start | bytes 1622024 | tf_op jit(solution)/shard_map/ppermute | solution.py:99
  169.3 26.7 %copy-start = (bf16[1024,128]{1,0:T(8,128)(2,1)S(1)}, bf16[1024,128]{1,0:T(8,128)(2,1)}, u32[]{:S(2)}) copy-start(bf16[1024,128]{1,0:T(8,128)(2,1)} %noise_ref.1) | copy-start | bytes 786436
  169.4 17.0 %collective-permute-start.19 = (bf16[4,528,128]{2,1,0:T(8,128)(2,1)S(1)}, bf16[4,528,128]{2,1,0:T(8,128)(2,1)S(1)}, u32[]{:S(2)}, u32[]{:S(2)}) collective-permute-start(bf16[4,528,128]{2,1,0:T(8,128)(2,1)S(1)} %get-tuple-element.82), channel_id=1, source_target_pairs={{0,3},{1,0},{2,1},{3,2},{4,7},{5,4},{6,5},{7,6},{8,11},{9,8},{10,9... | collective-permute-start | bytes 1622024 | tf_op jit(solution)/shard_map/ppermute | solution.py:95
  169.8 16.6 %collective-permute-start.18 = (bf16[4,528,128]{2,1,0:T(8,128)(2,1)S(1)}, bf16[4,528,128]{2,1,0:T(8,128)(2,1)S(1)}, u32[]{:S(2)}, u32[]{:S(2)}) collective-permute-start(bf16[4,528,128]{2,1,0:T(8,128)(2,1)S(1)} %get-tuple-element.77), channel_id=1, source_target_pairs={{0,1},{1,2},{2,3},{3,0},{4,5},{5,6},{6,7},{7,4},{8,9},{9,10},{10,1... | collective-permute-start | bytes 1622024 | tf_op jit(solution)/shard_map/ppermute | solution.py:95
  183.1 7.9 %collective-permute-start.25 = (bf16[528,128]{1,0:T(8,128)(2,1)S(1)}, bf16[528,128]{1,0:T(8,128)(2,1)S(1)}, u32[]{:S(2)}, u32[]{:S(2)}) collective-permute-start(bf16[528,128]{1,0:T(8,128)(2,1)S(1)} %get-tuple-element.90), channel_id=1, source_target_pairs={{0,1},{1,2},{2,3},{3,0},{4,5},{5,6},{6,7},{7,4},{8,9},{9,10},{10,1... | collective-permute-start | bytes 405512 | tf_op jit(solution)/shard_map/ppermute | solution.py:95
  183.2 8.4 %collective-permute-start.26 = (bf16[528,128]{1,0:T(8,128)(2,1)S(1)}, bf16[528,128]{1,0:T(8,128)(2,1)S(1)}, u32[]{:S(2)}, u32[]{:S(2)}) collective-permute-start(bf16[528,128]{1,0:T(8,128)(2,1)S(1)} %get-tuple-element.91), channel_id=1, source_target_pairs={{0,2},{1,3},{2,0},{3,1},{4,6},{5,7},{6,4},{7,5},{8,10},{9,11},{10,... | collective-permute-start | bytes 405512 | tf_op jit(solution)/shard_map/ppermute | solution.py:95
  185.2 6.5 %collective-permute-start.27 = (bf16[528,128]{1,0:T(8,128)(2,1)S(1)}, bf16[528,128]{1,0:T(8,128)(2,1)S(1)}, u32[]{:S(2)}, u32[]{:S(2)}) collective-permute-start(bf16[528,128]{1,0:T(8,128)(2,1)S(1)} %get-tuple-element.92), channel_id=1, source_target_pairs={{0,3},{1,0},{2,1},{3,2},{4,7},{5,4},{6,5},{7,6},{8,11},{9,8},{10,9... | collective-permute-start | bytes 405512 | tf_op jit(solution)/shard_map/ppermute | solution.py:95
  187.2 6.3 %collective-permute-start.20 = (bf16[528,128]{1,0:T(8,128)(2,1)S(1)}, bf16[528,128]{1,0:T(8,128)(2,1)S(1)}, u32[]{:S(2)}, u32[]{:S(2)}) collective-permute-start(bf16[528,128]{1,0:T(8,128)(2,1)S(1)} %get-tuple-element.84), channel_id=1, source_target_pairs={{0,4},{1,5},{2,6},{3,7},{4,8},{5,9},{6,10},{7,11},{8,12},{9,13},{1... | collective-permute-start | bytes 405512 | tf_op jit(solution)/shard_map/ppermute | solution.py:99
  187.2 8.2 %collective-permute-start.21 = (bf16[528,128]{1,0:T(8,128)(2,1)S(1)}, bf16[528,128]{1,0:T(8,128)(2,1)S(1)}, u32[]{:S(2)}, u32[]{:S(2)}) collective-permute-start(bf16[528,128]{1,0:T(8,128)(2,1)S(1)} %get-tuple-element.85), channel_id=1, source_target_pairs={{0,8},{1,9},{2,10},{3,11},{4,12},{5,13},{6,14},{7,15},{8,0},{9,1},... | collective-permute-start | bytes 405512 | tf_op jit(solution)/shard_map/ppermute | solution.py:99
  191.0 5.0 %collective-permute-start.22 = (bf16[528,128]{1,0:T(8,128)(2,1)S(1)}, bf16[528,128]{1,0:T(8,128)(2,1)S(1)}, u32[]{:S(2)}, u32[]{:S(2)}) collective-permute-start(bf16[528,128]{1,0:T(8,128)(2,1)S(1)} %get-tuple-element.86), channel_id=1, source_target_pairs={{0,12},{1,13},{2,14},{3,15},{4,0},{5,1},{6,2},{7,3},{8,4},{9,5},{1... | collective-permute-start | bytes 405512 | tf_op jit(solution)/shard_map/ppermute | solution.py:99
Sparse Core Ops, SparseCore 0:
  9.7 52.1 all-gather.2

commit v7 on v6

--- a/solution.py
+++ b/solution.py
@@ -181,7 +181,7 @@
         grid=(COLS // COL_BLOCK,),
         in_specs=[
             pl.BlockSpec(memory_space=pltpu.SMEM),
-            vmem((ROWS, WIDTH)),
+            pl.BlockSpec(memory_space=pltpu.VMEM),
             vmem((N_ROW, COL_BLOCK, 256), lambda j: (0, j, 0)),
         ],
         out_specs=[

time: 204 us -> 204 us (level)
  no operation moved by 1% of the time
where the time goes in v7:
time: 204 us
  blocking collectives  61 us (30%)
  starting transfers between devices  42.7 us (21%)
  Pallas kernels  42.5 us (21%)
  waiting for transfers between devices  34.4 us (17%)
  between operations  14.2 us (7%)
  local copies, waits for them, and re-layouts  8.92 us (4%)
    all_to_all x6, blocking collectives, swap(): return lax.all_to_all(x, axis, 0, 0, tiled=True)  61 us
    ppermute x14, starting transfers between devices, over_z(): lax.ppermute(v, 'col', [(4 * z + x, 4 * ((z + d) % 4) + x) for z in range...  22.1 us
    ppermute x14, starting transfers between devices, over_x(): lax.ppermute(v, 'col', [(4 * z + x, 4 * z + (x + d) % 4) for z in range(4...  20.5 us
    ppermute x14, waiting for transfers between devices, over_z(): lax.ppermute(v, 'col', [(4 * z + x, 4 * ((z + d) % 4) + x) for z in range...  15.8 us
    pallas_call x1, Pallas kernels, scores(): pl.pallas_call(score_kernel, grid=(COLS // COL_BLOCK,), in_specs=[pl.Bloc...  14.1 us
    ppermute x14, waiting for transfers between devices, over_x(): lax.ppermute(v, 'col', [(4 * z + x, 4 * z + (x + d) % 4) for z in range(4...  13.5 us
    pallas_call x6, Pallas kernels, pass_call(): pl.pallas_call(kernel, grid=(sweeps * (ROWS // ROW_BLOCK),), in_specs=in_...  11.6 us
    pallas_call x3, Pallas kernels, messages(): pl.pallas_call(functools.partial(target_kernel, ways), in_specs=[pl.Block...  11 us
  transfers between devices with their start and end apart: 29, of which 13 were waited for; matrix products, arithmetic and copies ran while one was open for 2% of the time, Pallas kernels for 6%

profile of v7, /device:TPU:0, one launch (start us, length us, event | category | flops | bytes accessed | tf_op | source)
XLA Modules:
  0.0 203.9 jit_solution(18143749197221670366)
XLA Ops:
  7.9 1.0 slice_bitcast_fusion
  8.9 4.0 %collective-permute-start.8 = (bf16[512,128]{1,0:T(8,128)(2,1)S(1)}, bf16[512,128]{1,0:T(8,128)(2,1)S(1)}, u32[]{:S(2)}, u32[]{:S(2)}) collective-permute-start(bf16[512,128]{1,0:T(8,128)(2,1)S(1)} %get-tuple-element.98), channel_id=1, source_target_pairs={{0,8},{1,9},{2,10},{3,11},{4,12},{5,13},{6,14},{7,15},{8,0},{9,1},... | collective-permute-start | bytes 393224 | tf_op jit(solution)/shard_map/ppermute | solution.py:99
  13.0 1.0 collective-permute-start.7
  14.0 2.2 %collective-permute-start.9 = (bf16[512,128]{1,0:T(8,128)(2,1)S(1)}, bf16[512,128]{1,0:T(8,128)(2,1)S(1)}, u32[]{:S(2)}, u32[]{:S(2)}) collective-permute-start(bf16[512,128]{1,0:T(8,128)(2,1)S(1)} %get-tuple-element.98), channel_id=1, source_target_pairs={{0,12},{1,13},{2,14},{3,15},{4,0},{5,1},{6,2},{7,3},{8,4},{9,5},{1... | collective-permute-start | bytes 393224 | tf_op jit(solution)/shard_map/ppermute | solution.py:99
  16.2 3.0 %collective-permute-start.1 = (bf16[512,128]{1,0:T(8,128)(2,1)S(1)}, bf16[512,128]{1,0:T(8,128)(2,1)S(1)}, u32[]{:S(2)}, u32[]{:S(2)}) collective-permute-start(bf16[512,128]{1,0:T(8,128)(2,1)S(1)} %get-tuple-element.97), channel_id=1, source_target_pairs={{0,2},{1,3},{2,0},{3,1},{4,6},{5,7},{6,4},{7,5},{8,10},{9,11},{10,... | collective-permute-start | bytes 393224 | tf_op jit(solution)/shard_map/ppermute | solution.py:95
  19.8 2.6 %collective-permute-start.2 = (bf16[512,128]{1,0:T(8,128)(2,1)S(1)}, bf16[512,128]{1,0:T(8,128)(2,1)S(1)}, u32[]{:S(2)}, u32[]{:S(2)}) collective-permute-start(bf16[512,128]{1,0:T(8,128)(2,1)S(1)} %get-tuple-element.97), channel_id=1, source_target_pairs={{0,3},{1,0},{2,1},{3,2},{4,7},{5,4},{6,5},{7,6},{8,11},{9,8},{10,9... | collective-permute-start | bytes 393224 | tf_op jit(solution)/shard_map/ppermute | solution.py:95
  22.9 1.7 collective-permute-start.10
  24.7 1.3 collective-permute-done
  27.5 1.4 collective-permute-start.3
  28.9 7.4 %collective-permute-done.11.refs_7_ = bf16[4,512,128]{2,1,0:T(8,128)(2,1)S(1)} collective-permute-done((bf16[4,512,128]{2,1,0:T(8,128)(2,1)S(1)}, bf16[4,512,128]{2,1,0:T(8,128)(2,1)S(1)}, u32[]{:S(2)}, u32[]{:S(2)}) %collective-permute-start.11) | collective-permute-done | bytes 524320 | tf_op jit(solution)/shard_map/ppermute | solution.py:95
  37.0 3.5 %collective-permute-start.13 = (bf16[2,512,128]{2,1,0:T(8,128)(2,1)}, bf16[2,512,128]{2,1,0:T(8,128)(2,1)S(1)}, u32[]{:S(2)}, u32[]{:S(2)}) collective-permute-start(bf16[2,512,128]{2,1,0:T(8,128)(2,1)} %slice.27), channel_id=1, source_target_pairs={{0,3},{1,0},{2,1},{3,2},{4,7},{5,4},{6,5},{7,6},{8,11},{9,8},{10,9... | collective-permute-start | bytes 786440 | tf_op jit(solution)/shard_map/ppermute | solution.py:95
  42.0 1.4 collective-permute-start.6
  44.7 0.7 concatenate.3.info_ref
  45.5 3.9 %collective-permute-done.12.refs_8_ = bf16[2,512,128]{2,1,0:T(8,128)(2,1)} collective-permute-done((bf16[2,512,128]{2,1,0:T(8,128)(2,1)}, bf16[2,512,128]{2,1,0:T(8,128)(2,1)}, u32[]{:S(2)}, u32[]{:S(2)}) %collective-permute-start.12) | collective-permute-done | bytes 262176 | tf_op jit(solution)/shard_map/ppermute | solution.py:95
  49.3 3.0 %collective-permute-done.5.refs_3_ = bf16[2,512,128]{2,1,0:T(8,128)(2,1)} collective-permute-done((bf16[2,512,128]{2,1,0:T(8,128)(2,1)}, bf16[2,512,128]{2,1,0:T(8,128)(2,1)}, u32[]{:S(2)}, u32[]{:S(2)}) %collective-permute-start.5) | collective-permute-done | bytes 262176 | tf_op jit(solution)/shard_map/ppermute | solution.py:99
  52.4 3.1 %arrange.1 = (bf16[1024,2048]{1,0:T(8,128)(2,1)S(1)}, f32[8,128]{1,0:T(8,128)S(1)}) custom-call(s32[20]{0:T(128)S(1)} %concatenate.3.info_ref, bf16[4,512,128]{2,1,0:T(8,128)(2,1)S(1)} %pad_maximum_fusion.refs_0_, bf16[4,512,128]{2,1,0:T(8,128)(2,1)S(1)} %collective-permute-done.3.refs_1_, bf16[4,512,128]{2,1,0:T(8,128)(2,1)S(1)} %collective-permute-done.4.refs_2_, ...), custom_call_target="tpu_custom_call" | custom-call | flops 4194304 | bytes 8388608 | tf_op jit(solution)/shard_map/arrange/pallas_call | solution.py:84
  55.5 2.0 %copy-done.1 = bf16[1024,2048]{1,0:T(8,128)(2,1)} copy-done((bf16[1024,2048]{1,0:T(8,128)(2,1)}, bf16[1024,2048]{1,0:T(8,128)(2,1)S(1)}, u32[]{:S(2)}) %copy-start.1) | copy-done | bytes 4194328
  57.6 4.4 %all-gather.3.cloned.1.call-done = bf16[16384,256]{1,0:T(8,128)(2,1)} async-done(((bf16[2048,256]{1,0:T(8,128)(2,1)}), bf16[16384,256]{1,0:T(8,128)(2,1)}) %all-gather.3.cloned.1.call-update) | async-done | bytes 8388624 | tf_op jit(solution)/shard_map/all_gather | solution.py:629
  61.9 2.2 %copy-done.2 = bf16[1024,2048]{1,0:T(8,128)(2,1)S(1)} copy-done((bf16[1024,2048]{1,0:T(8,128)(2,1)S(1)}, bf16[1024,2048]{1,0:T(8,128)(2,1)}, u32[]{:S(2)}) %copy-start.2) | copy-done | bytes 4194328
  64.1 14.1 %scores.1 = (f32[1024,2048]{1,0:T(8,128)S(1)}, f32[16,8,128]{2,1,0:T(8,128)S(1)}, f32[4,4,128]{2,1,0:T(4,128)S(1)}) custom-call(s32[20]{0:T(128)S(1)} %concatenate.3.info_ref, bf16[1024,2048]{1,0:T(8,128)(2,1)S(1)} %copy-done.2, bf16[8,2048,256]{2,1,0:T(8,128)(2,1)} %bitcast.17), custom_call_target="tpu_custom_call" | custom-call | flops 8589934592 | bytes 20971520 | tf_op jit(solution)/shard_map/scores/pallas_call | solution.py:179
  78.2 14.4 %all_to_all.30.parts_ref = f32[16,8,128]{2,1,0:T(8,128)S(1)} all-to-all(f32[16,8,128]{2,1,0:T(8,128)S(1)} %get-tuple-element.50), channel_id=1, replica_groups=mesh['row'=8,'col'=16] {'col'}, dimensions={0} | all-to-all | bytes 131072 | tf_op jit(solution)/shard_map/all_to_all | solution.py:622
  92.7 3.1 %first_columns.1 = (f32[8,16,128]{2,1,0:T(8,128)S(1)}, f32[8,128]{1,0:T(8,128)S(1)}, f32[1024,2048]{1,0:T(8,128)S(1)}, f32[16,128]{1,0:T(8,128)S(1)}) custom-call(f32[16,8,128]{2,1,0:T(8,128)S(1)} %all_to_all.30.parts_ref, f32[1024,2048]{1,0:T(8,128)S(1)} %get-tuple-element.51.score_ref), custom_call_target="tpu_custom_call" | custom-call | flops 8388608 | bytes 8388608 | tf_op jit(solution)/shard_map/first_columns/pallas_call | solution.py:277
  95.8 8.6 %all_to_all.31.parts_ref = f32[8,16,128]{2,1,0:T(8,128)S(1)} all-to-all(f32[8,16,128]{2,1,0:T(8,128)S(1)} %get-tuple-element.52), channel_id=1, replica_groups=mesh['row'=8,'col'=16] {'row'}, dimensions={0} | all-to-all | bytes 131072 | tf_op jit(solution)/shard_map/all_to_all | solution.py:622
  104.4 1.3 row_sums.2
  105.6 10.8 %all_to_all.32.parts_ref = f32[16,8,128]{2,1,0:T(8,128)S(1)} all-to-all(f32[16,8,128]{2,1,0:T(8,128)S(1)} %get-tuple-element.55), channel_id=1, replica_groups=mesh['row'=8,'col'=16] {'col'}, dimensions={0} | all-to-all | bytes 131072 | tf_op jit(solution)/shard_map/all_to_all | solution.py:622
  116.4 1.6 column_sums.2
  118.1 8.0 %all_to_all.33.parts_ref = f32[8,16,128]{2,1,0:T(8,128)S(1)} all-to-all(f32[8,16,128]{2,1,0:T(8,128)S(1)} %get-tuple-element.57), channel_id=1, replica_groups=mesh['row'=8,'col'=16] {'row'}, dimensions={0} | all-to-all | bytes 131072 | tf_op jit(solution)/shard_map/all_to_all | solution.py:622
  126.1 1.2 row_sums.3
  127.3 10.8 %all_to_all.34.parts_ref = f32[16,8,128]{2,1,0:T(8,128)S(1)} all-to-all(f32[16,8,128]{2,1,0:T(8,128)S(1)} %row_sums.3), channel_id=1, replica_groups=mesh['row'=8,'col'=16] {'col'}, dimensions={0} | all-to-all | bytes 131072 | tf_op jit(solution)/shard_map/all_to_all | solution.py:622
  138.1 1.0 column_sums.3
  139.2 8.4 %all_to_all.35.parts_ref = f32[8,16,128]{2,1,0:T(8,128)S(1)} all-to-all(f32[8,16,128]{2,1,0:T(8,128)S(1)} %get-tuple-element.58), channel_id=1, replica_groups=mesh['row'=8,'col'=16] {'row'}, dimensions={0} | all-to-all | bytes 131072 | tf_op jit(solution)/shard_map/all_to_all | solution.py:622
  147.6 3.3 %coupling.1 = (bf16[512,2048]{1,0:T(8,128)(2,1)S(1)}, bf16[512,2048]{1,0:T(8,128)(2,1)S(1)}, f32[8,128]{1,0:T(8,128)S(1)}, f32[8,128]{1,0:T(8,128)}, f32[16,128]{1,0:T(8,128)}) custom-call(f32[8,16,128]{2,1,0:T(8,128)S(1)} %all_to_all.35.parts_ref, f32[8,128]{1,0:T(8,128)S(1)} %get-tuple-element.59.scale_ref, f32[8,128]{1,0:T(8,128)S(1)} %get-tuple-element.60.noise_first, ...), custom_call_target="tpu_custom_call" | custom-call | flops 8388608 | bytes 8388608 | tf_op jit(solution)/shard_map/coupling/pallas_call | solution.py:277
  150.9 2.9 %targets.3 = (bf16[4,272,128]{2,1,0:T(8,128)(2,1)S(1)}, bf16[4,272,128]{2,1,0:T(8,128)(2,1)S(1)}, bf16[4,272,128]{2,1,0:T(8,128)(2,1)S(1)}, bf16[4,272,128]{2,1,0:T(8,128)(2,1)S(1)}) custom-call(s32[20]{0:T(128)S(1)} %concatenate.3.info_ref, bf16[512,2048]{1,0:T(8,128)(2,1)S(1)} %get-tuple-element.64.pa_ref, bf16[512,2048]{1,0:T(8,128)(2,1)S(1)} %get-tuple-element.65.pb_ref, ...), custom_call_target="tpu_custom_call" | custom-call | flops 2147483648 | bytes 8388608 | tf_op jit(solution)/shard_map/targets/pallas_call | solution.py:528
  154.5 2.7 %collective-permute-start.15 = (bf16[4,272,128]{2,1,0:T(8,128)(2,1)S(1)}, bf16[4,272,128]{2,1,0:T(8,128)(2,1)S(1)}, u32[]{:S(2)}, u32[]{:S(2)}) collective-permute-start(bf16[4,272,128]{2,1,0:T(8,128)(2,1)S(1)} %get-tuple-element.68), channel_id=1, source_target_pairs={{0,3},{1,0},{2,1},{3,2},{4,7},{5,4},{6,5},{7,6},{8,11},{9,8},{10,9... | collective-permute-start | bytes 835592 | tf_op jit(solution)/shard_map/ppermute | solution.py:95
  157.7 2.7 %collective-permute-start.17 = (bf16[4,272,128]{2,1,0:T(8,128)(2,1)S(1)}, bf16[4,272,128]{2,1,0:T(8,128)(2,1)S(1)}, u32[]{:S(2)}, u32[]{:S(2)}) collective-permute-start(bf16[4,272,128]{2,1,0:T(8,128)(2,1)S(1)} %get-tuple-element.70), channel_id=1, source_target_pairs={{0,12},{1,13},{2,14},{3,15},{4,0},{5,1},{6,2},{7,3},{8,4},{9,5},{1... | collective-permute-start | bytes 835592 | tf_op jit(solution)/shard_map/ppermute | solution.py:99
  160.4 5.1 %targets.4 = (bf16[4,528,128]{2,1,0:T(8,128)(2,1)S(1)}, bf16[4,528,128]{2,1,0:T(8,128)(2,1)S(1)}, bf16[4,528,128]{2,1,0:T(8,128)(2,1)S(1)}, bf16[4,528,128]{2,1,0:T(8,128)(2,1)S(1)}) custom-call(s32[20]{0:T(128)S(1)} %concatenate.3.info_ref, bf16[512,2048]{1,0:T(8,128)(2,1)S(1)} %get-tuple-element.64.pa_ref, bf16[512,2048]{1,0:T(8,128)(2,1)S(1)} %get-tuple-element.65.pb_ref, ...), custom_call_target="tpu_custom_call" | custom-call | flops 4294967296 | bytes 8388608 | tf_op jit(solution)/shard_map/targets/pallas_call | solution.py:528
  166.3 3.0 %collective-permute-start.24 = (bf16[4,528,128]{2,1,0:T(8,128)(2,1)S(1)}, bf16[4,528,128]{2,1,0:T(8,128)(2,1)S(1)}, u32[]{:S(2)}, u32[]{:S(2)}) collective-permute-start(bf16[4,528,128]{2,1,0:T(8,128)(2,1)S(1)} %get-tuple-element.88), channel_id=1, source_target_pairs={{0,12},{1,13},{2,14},{3,15},{4,0},{5,1},{6,2},{7,3},{8,4},{9,5},{1... | collective-permute-start | bytes 1622024 | tf_op jit(solution)/shard_map/ppermute | solution.py:99
  169.8 1.7 collective-permute-start.18
  171.5 2.9 %targets.5 = (bf16[4,528,128]{2,1,0:T(8,128)(2,1)S(1)}, bf16[4,528,128]{2,1,0:T(8,128)(2,1)S(1)}) custom-call(s32[20]{0:T(128)S(1)} %concatenate.3.info_ref, bf16[512,2048]{1,0:T(8,128)(2,1)S(1)} %get-tuple-element.64.pa_ref, bf16[512,2048]{1,0:T(8,128)(2,1)S(1)} %get-tuple-element.65.pb_ref, f32[8,128]{1,0:T(8,128)S(1)} %get-tuple-element.80.sums_ref, ...), custom_call_target="tpu_custom_call" | custom-call | flops 2147483648 | bytes 8388608 | tf_op jit(solution)/shard_map/targets/pallas_call | solution.py:528
  174.5 4.5 %collective-permute-done.24.right = bf16[4,528,128]{2,1,0:T(8,128)(2,1)S(1)} collective-permute-done((bf16[4,528,128]{2,1,0:T(8,128)(2,1)S(1)}, bf16[4,528,128]{2,1,0:T(8,128)(2,1)S(1)}, u32[]{:S(2)}, u32[]{:S(2)}) %collective-permute-start.24) | collective-permute-done | bytes 540704 | tf_op jit(solution)/shard_map/ppermute | solution.py:99
  178.9 3.4 %collective-permute-done.23.left = bf16[4,528,128]{2,1,0:T(8,128)(2,1)S(1)} collective-permute-done((bf16[4,528,128]{2,1,0:T(8,128)(2,1)S(1)}, bf16[4,528,128]{2,1,0:T(8,128)(2,1)S(1)}, u32[]{:S(2)}, u32[]{:S(2)}) %collective-permute-start.23) | collective-permute-done | bytes 540704 | tf_op jit(solution)/shard_map/ppermute | solution.py:99
  183.2 2.0 collective-permute-start.26
  185.2 1.2 collective-permute-start.27
  186.4 0.7 combine.2
  187.2 3.7 %collective-permute-start.21 = (bf16[528,128]{1,0:T(8,128)(2,1)S(1)}, bf16[528,128]{1,0:T(8,128)(2,1)S(1)}, u32[]{:S(2)}, u32[]{:S(2)}) collective-permute-start(bf16[528,128]{1,0:T(8,128)(2,1)S(1)} %get-tuple-element.85), channel_id=1, source_target_pairs={{0,8},{1,9},{2,10},{3,11},{4,12},{5,13},{6,14},{7,15},{8,0},{9,1},... | collective-permute-start | bytes 405512 | tf_op jit(solution)/shard_map/ppermute | solution.py:99
  191.7 1.7 collective-permute-done.20.refs_1_
  193.4 2.0 collective-permute-done.21.refs_2_
  196.0 1.0 finish.1
  (52 shorter events, 11.4 us)
Async XLA Ops:
  7.2 54.8 %all-gather.3.cloned.1.call-start = ((), (), s32[]{:S(2)}) async-start(), calls=%async_computation.6 | async-start | bytes 9437184 | tf_op jit(solution)/shard_map/all_gather | solution.py:629
  8.9 10.9 %collective-permute-start.8 = (bf16[512,128]{1,0:T(8,128)(2,1)S(1)}, bf16[512,128]{1,0:T(8,128)(2,1)S(1)}, u32[]{:S(2)}, u32[]{:S(2)}) collective-permute-start(bf16[512,128]{1,0:T(8,128)(2,1)S(1)} %get-tuple-element.98), channel_id=1, source_target_pairs={{0,8},{1,9},{2,10},{3,11},{4,12},{5,13},{6,14},{7,15},{8,0},{9,1},... | collective-permute-start | bytes 393224 | tf_op jit(solution)/shard_map/ppermute | solution.py:99
  13.0 9.5 %collective-permute-start.7 = (bf16[512,128]{1,0:T(8,128)(2,1)S(1)}, bf16[512,128]{1,0:T(8,128)(2,1)S(1)}, u32[]{:S(2)}, u32[]{:S(2)}) collective-permute-start(bf16[512,128]{1,0:T(8,128)(2,1)S(1)} %get-tuple-element.98), channel_id=1, source_target_pairs={{0,4},{1,5},{2,6},{3,7},{4,8},{5,9},{6,10},{7,11},{8,12},{9,13},{1... | collective-permute-start | bytes 393224 | tf_op jit(solution)/shard_map/ppermute | solution.py:99
  14.0 8.5 %collective-permute-start.9 = (bf16[512,128]{1,0:T(8,128)(2,1)S(1)}, bf16[512,128]{1,0:T(8,128)(2,1)S(1)}, u32[]{:S(2)}, u32[]{:S(2)}) collective-permute-start(bf16[512,128]{1,0:T(8,128)(2,1)S(1)} %get-tuple-element.98), channel_id=1, source_target_pairs={{0,12},{1,13},{2,14},{3,15},{4,0},{5,1},{6,2},{7,3},{8,4},{9,5},{1... | collective-permute-start | bytes 393224 | tf_op jit(solution)/shard_map/ppermute | solution.py:99
  16.2 8.4 %collective-permute-start.1 = (bf16[512,128]{1,0:T(8,128)(2,1)S(1)}, bf16[512,128]{1,0:T(8,128)(2,1)S(1)}, u32[]{:S(2)}, u32[]{:S(2)}) collective-permute-start(bf16[512,128]{1,0:T(8,128)(2,1)S(1)} %get-tuple-element.97), channel_id=1, source_target_pairs={{0,2},{1,3},{2,0},{3,1},{4,6},{5,7},{6,4},{7,5},{8,10},{9,11},{10,... | collective-permute-start | bytes 393224 | tf_op jit(solution)/shard_map/ppermute | solution.py:95
  19.2 6.8 %collective-permute-start = (bf16[512,128]{1,0:T(8,128)(2,1)S(1)}, bf16[512,128]{1,0:T(8,128)(2,1)S(1)}, u32[]{:S(2)}, u32[]{:S(2)}) collective-permute-start(bf16[512,128]{1,0:T(8,128)(2,1)S(1)} %get-tuple-element.97), channel_id=1, source_target_pairs={{0,1},{1,2},{2,3},{3,0},{4,5},{5,6},{6,7},{7,4},{8,9},{9,10},{10,1... | collective-permute-start | bytes 393224 | tf_op jit(solution)/shard_map/ppermute | solution.py:95
  19.8 6.9 %collective-permute-start.2 = (bf16[512,128]{1,0:T(8,128)(2,1)S(1)}, bf16[512,128]{1,0:T(8,128)(2,1)S(1)}, u32[]{:S(2)}, u32[]{:S(2)}) collective-permute-start(bf16[512,128]{1,0:T(8,128)(2,1)S(1)} %get-tuple-element.97), channel_id=1, source_target_pairs={{0,3},{1,0},{2,1},{3,2},{4,7},{5,4},{6,5},{7,6},{8,11},{9,8},{10,9... | collective-permute-start | bytes 393224 | tf_op jit(solution)/shard_map/ppermute | solution.py:95
  22.6 13.8 %collective-permute-start.11 = (bf16[4,512,128]{2,1,0:T(8,128)(2,1)S(1)}, bf16[4,512,128]{2,1,0:T(8,128)(2,1)S(1)}, u32[]{:S(2)}, u32[]{:S(2)}) collective-permute-start(bf16[4,512,128]{2,1,0:T(8,128)(2,1)S(1)} %pad_maximum_fusion.1.refs_5_), channel_id=1, source_target_pairs={{0,3},{1,0},{2,1},{3,2},{4,7},{5,4},{6,5},{7,6},{8,11},{9,8},{10,9... | collective-permute-start | bytes 1572872 | tf_op jit(solution)/shard_map/ppermute | solution.py:95
  22.9 17.6 %collective-permute-start.10 = (bf16[4,512,128]{2,1,0:T(8,128)(2,1)S(1)}, bf16[4,512,128]{2,1,0:T(8,128)(2,1)S(1)}, u32[]{:S(2)}, u32[]{:S(2)}) collective-permute-start(bf16[4,512,128]{2,1,0:T(8,128)(2,1)S(1)} %pad_maximum_fusion.1.refs_5_), channel_id=1, source_target_pairs={{0,1},{1,2},{2,3},{3,0},{4,5},{5,6},{6,7},{7,4},{8,9},{9,10},{10,1... | collective-permute-start | bytes 1572872 | tf_op jit(solution)/shard_map/ppermute | solution.py:95
  26.8 14.5 %collective-permute-start.4 = (bf16[4,512,128]{2,1,0:T(8,128)(2,1)S(1)}, bf16[4,512,128]{2,1,0:T(8,128)(2,1)S(1)}, u32[]{:S(2)}, u32[]{:S(2)}) collective-permute-start(bf16[4,512,128]{2,1,0:T(8,128)(2,1)S(1)} %pad_maximum_fusion.refs_0_), channel_id=1, source_target_pairs={{0,12},{1,13},{2,14},{3,15},{4,0},{5,1},{6,2},{7,3},{8,4},{9,5},{1... | collective-permute-start | bytes 1572872 | tf_op jit(solution)/shard_map/ppermute | solution.py:99
  27.5 15.9 %collective-permute-start.3 = (bf16[4,512,128]{2,1,0:T(8,128)(2,1)S(1)}, bf16[4,512,128]{2,1,0:T(8,128)(2,1)S(1)}, u32[]{:S(2)}, u32[]{:S(2)}) collective-permute-start(bf16[4,512,128]{2,1,0:T(8,128)(2,1)S(1)} %pad_maximum_fusion.refs_0_), channel_id=1, source_target_pairs={{0,4},{1,5},{2,6},{3,7},{4,8},{5,9},{6,10},{7,11},{8,12},{9,13},{1... | collective-permute-start | bytes 1572872 | tf_op jit(solution)/shard_map/ppermute | solution.py:99
  37.0 8.4 %collective-permute-start.13 = (bf16[2,512,128]{2,1,0:T(8,128)(2,1)}, bf16[2,512,128]{2,1,0:T(8,128)(2,1)S(1)}, u32[]{:S(2)}, u32[]{:S(2)}) collective-permute-start(bf16[2,512,128]{2,1,0:T(8,128)(2,1)} %slice.27), channel_id=1, source_target_pairs={{0,3},{1,0},{2,1},{3,2},{4,7},{5,4},{6,5},{7,6},{8,11},{9,8},{10,9... | collective-permute-start | bytes 786440 | tf_op jit(solution)/shard_map/ppermute | solution.py:95
  41.2 8.1 %collective-permute-start.12 = (bf16[2,512,128]{2,1,0:T(8,128)(2,1)}, bf16[2,512,128]{2,1,0:T(8,128)(2,1)}, u32[]{:S(2)}, u32[]{:S(2)}) collective-permute-start(bf16[2,512,128]{2,1,0:T(8,128)(2,1)} %slice.26), channel_id=1, source_target_pairs={{0,1},{1,2},{2,3},{3,0},{4,5},{5,6},{6,7},{7,4},{8,9},{9,10},{10,1... | collective-permute-start | bytes 786440 | tf_op jit(solution)/shard_map/ppermute | solution.py:95
  42.0 7.4 %collective-permute-start.6 = (bf16[2,512,128]{2,1,0:T(8,128)(2,1)}, bf16[2,512,128]{2,1,0:T(8,128)(2,1)}, u32[]{:S(2)}, u32[]{:S(2)}) collective-permute-start(bf16[2,512,128]{2,1,0:T(8,128)(2,1)} %slice.25), channel_id=1, source_target_pairs={{0,12},{1,13},{2,14},{3,15},{4,0},{5,1},{6,2},{7,3},{8,4},{9,5},{1... | collective-permute-start | bytes 786440 | tf_op jit(solution)/shard_map/ppermute | solution.py:99
  44.1 8.3 %collective-permute-start.5 = (bf16[2,512,128]{2,1,0:T(8,128)(2,1)}, bf16[2,512,128]{2,1,0:T(8,128)(2,1)}, u32[]{:S(2)}, u32[]{:S(2)}) collective-permute-start(bf16[2,512,128]{2,1,0:T(8,128)(2,1)} %slice.24), channel_id=1, source_target_pairs={{0,4},{1,5},{2,6},{3,7},{4,8},{5,9},{6,10},{7,11},{8,12},{9,13},{1... | collective-permute-start | bytes 786440 | tf_op jit(solution)/shard_map/ppermute | solution.py:99
  55.5 2.1 %copy-start.1 = (bf16[1024,2048]{1,0:T(8,128)(2,1)}, bf16[1024,2048]{1,0:T(8,128)(2,1)S(1)}, u32[]{:S(2)}) copy-start(bf16[1024,2048]{1,0:T(8,128)(2,1)S(1)} %get-tuple-element.49.noise_ref) | copy-start | bytes 12582916
  61.9 2.2 %copy-start.2 = (bf16[1024,2048]{1,0:T(8,128)(2,1)S(1)}, bf16[1024,2048]{1,0:T(8,128)(2,1)}, u32[]{:S(2)}) copy-start(bf16[1024,2048]{1,0:T(8,128)(2,1)} %copy-done.1) | copy-start | bytes 12582916
  138.1 12.8 %slice-start = ((s8[8388608]{0:T(1024)(128)(4,1)}), s8[4194304]{0:T(1024)(128)(4,1)S(1)}, s32[]{:S(2)}) async-start(s8[8388608]{0:T(1024)(128)(4,1)} %bitcast.18), calls=%async_computation.7 | async-start | bytes 8388608
  139.2 11.8 %slice-start.1 = ((s8[8388608]{0:T(1024)(128)(4,1)}), s8[4194304]{0:T(1024)(128)(4,1)S(1)}, s32[]{:S(2)}) async-start(s8[8388608]{0:T(1024)(128)(4,1)} %bitcast.18), calls=%async_computation.8 | async-start | bytes 8388608
  153.9 15.4 %collective-permute-start.14 = (bf16[4,272,128]{2,1,0:T(8,128)(2,1)S(1)}, bf16[4,272,128]{2,1,0:T(8,128)(2,1)S(1)}, u32[]{:S(2)}, u32[]{:S(2)}) collective-permute-start(bf16[4,272,128]{2,1,0:T(8,128)(2,1)S(1)} %get-tuple-element.67), channel_id=1, source_target_pairs={{0,1},{1,2},{2,3},{3,0},{4,5},{5,6},{6,7},{7,4},{8,9},{9,10},{10,1... | collective-permute-start | bytes 835592 | tf_op jit(solution)/shard_map/ppermute | solution.py:95
  154.5 14.8 %collective-permute-start.15 = (bf16[4,272,128]{2,1,0:T(8,128)(2,1)S(1)}, bf16[4,272,128]{2,1,0:T(8,128)(2,1)S(1)}, u32[]{:S(2)}, u32[]{:S(2)}) collective-permute-start(bf16[4,272,128]{2,1,0:T(8,128)(2,1)S(1)} %get-tuple-element.68), channel_id=1, source_target_pairs={{0,3},{1,0},{2,1},{3,2},{4,7},{5,4},{6,5},{7,6},{8,11},{9,8},{10,9... | collective-permute-start | bytes 835592 | tf_op jit(solution)/shard_map/ppermute | solution.py:95
  157.2 8.9 %collective-permute-start.16 = (bf16[4,272,128]{2,1,0:T(8,128)(2,1)S(1)}, bf16[4,272,128]{2,1,0:T(8,128)(2,1)S(1)}, u32[]{:S(2)}, u32[]{:S(2)}) collective-permute-start(bf16[4,272,128]{2,1,0:T(8,128)(2,1)S(1)} %get-tuple-element.69), channel_id=1, source_target_pairs={{0,4},{1,5},{2,6},{3,7},{4,8},{5,9},{6,10},{7,11},{8,12},{9,13},{1... | collective-permute-start | bytes 835592 | tf_op jit(solution)/shard_map/ppermute | solution.py:99
  157.7 8.4 %collective-permute-start.17 = (bf16[4,272,128]{2,1,0:T(8,128)(2,1)S(1)}, bf16[4,272,128]{2,1,0:T(8,128)(2,1)S(1)}, u32[]{:S(2)}, u32[]{:S(2)}) collective-permute-start(bf16[4,272,128]{2,1,0:T(8,128)(2,1)S(1)} %get-tuple-element.70), channel_id=1, source_target_pairs={{0,12},{1,13},{2,14},{3,15},{4,0},{5,1},{6,2},{7,3},{8,4},{9,5},{1... | collective-permute-start | bytes 835592 | tf_op jit(solution)/shard_map/ppermute | solution.py:99
  166.3 12.7 %collective-permute-start.24 = (bf16[4,528,128]{2,1,0:T(8,128)(2,1)S(1)}, bf16[4,528,128]{2,1,0:T(8,128)(2,1)S(1)}, u32[]{:S(2)}, u32[]{:S(2)}) collective-permute-start(bf16[4,528,128]{2,1,0:T(8,128)(2,1)S(1)} %get-tuple-element.88), channel_id=1, source_target_pairs={{0,12},{1,13},{2,14},{3,15},{4,0},{5,1},{6,2},{7,3},{8,4},{9,5},{1... | collective-permute-start | bytes 1622024 | tf_op jit(solution)/shard_map/ppermute | solution.py:99
  169.3 13.1 %collective-permute-start.23 = (bf16[4,528,128]{2,1,0:T(8,128)(2,1)S(1)}, bf16[4,528,128]{2,1,0:T(8,128)(2,1)S(1)}, u32[]{:S(2)}, u32[]{:S(2)}) collective-permute-start(bf16[4,528,128]{2,1,0:T(8,128)(2,1)S(1)} %get-tuple-element.79), channel_id=1, source_target_pairs={{0,4},{1,5},{2,6},{3,7},{4,8},{5,9},{6,10},{7,11},{8,12},{9,13},{1... | collective-permute-start | bytes 1622024 | tf_op jit(solution)/shard_map/ppermute | solution.py:99
  169.3 26.7 %copy-start = (bf16[1024,128]{1,0:T(8,128)(2,1)S(1)}, bf16[1024,128]{1,0:T(8,128)(2,1)}, u32[]{:S(2)}) copy-start(bf16[1024,128]{1,0:T(8,128)(2,1)} %noise_ref.1) | copy-start | bytes 786436
  169.4 17.0 %collective-permute-start.19 = (bf16[4,528,128]{2,1,0:T(8,128)(2,1)S(1)}, bf16[4,528,128]{2,1,0:T(8,128)(2,1)S(1)}, u32[]{:S(2)}, u32[]{:S(2)}) collective-permute-start(bf16[4,528,128]{2,1,0:T(8,128)(2,1)S(1)} %get-tuple-element.82), channel_id=1, source_target_pairs={{0,3},{1,0},{2,1},{3,2},{4,7},{5,4},{6,5},{7,6},{8,11},{9,8},{10,9... | collective-permute-start | bytes 1622024 | tf_op jit(solution)/shard_map/ppermute | solution.py:95
  169.8 16.6 %collective-permute-start.18 = (bf16[4,528,128]{2,1,0:T(8,128)(2,1)S(1)}, bf16[4,528,128]{2,1,0:T(8,128)(2,1)S(1)}, u32[]{:S(2)}, u32[]{:S(2)}) collective-permute-start(bf16[4,528,128]{2,1,0:T(8,128)(2,1)S(1)} %get-tuple-element.77), channel_id=1, source_target_pairs={{0,1},{1,2},{2,3},{3,0},{4,5},{5,6},{6,7},{7,4},{8,9},{9,10},{10,1... | collective-permute-start | bytes 1622024 | tf_op jit(solution)/shard_map/ppermute | solution.py:95
  183.1 7.9 %collective-permute-start.25 = (bf16[528,128]{1,0:T(8,128)(2,1)S(1)}, bf16[528,128]{1,0:T(8,128)(2,1)S(1)}, u32[]{:S(2)}, u32[]{:S(2)}) collective-permute-start(bf16[528,128]{1,0:T(8,128)(2,1)S(1)} %get-tuple-element.90), channel_id=1, source_target_pairs={{0,1},{1,2},{2,3},{3,0},{4,5},{5,6},{6,7},{7,4},{8,9},{9,10},{10,1... | collective-permute-start | bytes 405512 | tf_op jit(solution)/shard_map/ppermute | solution.py:95
  183.2 8.4 %collective-permute-start.26 = (bf16[528,128]{1,0:T(8,128)(2,1)S(1)}, bf16[528,128]{1,0:T(8,128)(2,1)S(1)}, u32[]{:S(2)}, u32[]{:S(2)}) collective-permute-start(bf16[528,128]{1,0:T(8,128)(2,1)S(1)} %get-tuple-element.91), channel_id=1, source_target_pairs={{0,2},{1,3},{2,0},{3,1},{4,6},{5,7},{6,4},{7,5},{8,10},{9,11},{10,... | collective-permute-start | bytes 405512 | tf_op jit(solution)/shard_map/ppermute | solution.py:95
  185.2 6.5 %collective-permute-start.27 = (bf16[528,128]{1,0:T(8,128)(2,1)S(1)}, bf16[528,128]{1,0:T(8,128)(2,1)S(1)}, u32[]{:S(2)}, u32[]{:S(2)}) collective-permute-start(bf16[528,128]{1,0:T(8,128)(2,1)S(1)} %get-tuple-element.92), channel_id=1, source_target_pairs={{0,3},{1,0},{2,1},{3,2},{4,7},{5,4},{6,5},{7,6},{8,11},{9,8},{10,9... | collective-permute-start | bytes 405512 | tf_op jit(solution)/shard_map/ppermute | solution.py:95
  187.2 6.3 %collective-permute-start.20 = (bf16[528,128]{1,0:T(8,128)(2,1)S(1)}, bf16[528,128]{1,0:T(8,128)(2,1)S(1)}, u32[]{:S(2)}, u32[]{:S(2)}) collective-permute-start(bf16[528,128]{1,0:T(8,128)(2,1)S(1)} %get-tuple-element.84), channel_id=1, source_target_pairs={{0,4},{1,5},{2,6},{3,7},{4,8},{5,9},{6,10},{7,11},{8,12},{9,13},{1... | collective-permute-start | bytes 405512 | tf_op jit(solution)/shard_map/ppermute | solution.py:99
  187.2 8.2 %collective-permute-start.21 = (bf16[528,128]{1,0:T(8,128)(2,1)S(1)}, bf16[528,128]{1,0:T(8,128)(2,1)S(1)}, u32[]{:S(2)}, u32[]{:S(2)}) collective-permute-start(bf16[528,128]{1,0:T(8,128)(2,1)S(1)} %get-tuple-element.85), channel_id=1, source_target_pairs={{0,8},{1,9},{2,10},{3,11},{4,12},{5,13},{6,14},{7,15},{8,0},{9,1},... | collective-permute-start | bytes 405512 | tf_op jit(solution)/shard_map/ppermute | solution.py:99
  191.0 5.0 %collective-permute-start.22 = (bf16[528,128]{1,0:T(8,128)(2,1)S(1)}, bf16[528,128]{1,0:T(8,128)(2,1)S(1)}, u32[]{:S(2)}, u32[]{:S(2)}) collective-permute-start(bf16[528,128]{1,0:T(8,128)(2,1)S(1)} %get-tuple-element.86), channel_id=1, source_target_pairs={{0,12},{1,13},{2,14},{3,15},{4,0},{5,1},{6,2},{7,3},{8,4},{9,5},{1... | collective-permute-start | bytes 405512 | tf_op jit(solution)/shard_map/ppermute | solution.py:99
Sparse Core Ops, SparseCore 0:
  9.7 52.1 all-gather.2
